TPU v7x, 32 devices: a whole 2x2x4 slice. The times are simulated.
32 devices in a mesh: wide: 16 (over z, x, core), narrow: 2 (over y).
Axes of the slice: x: 2, y: 2, z: 4, core: 2. Of those that a mesh axis runs over, the one named last changes fastest.
Arguments:
- layer_in: bfloat16 [16, 1280, 768], P('wide', 'narrow'), may hold values from -6 to 6
- pre_gain: float32 [768], replicated, may hold values from 0.5 to 1.5
- w_heads: bfloat16 [768, 24, 130], P(None, 'narrow'), may hold values from -0.21875 to 0.21875
- w_bc: bfloat16 [768, 256], replicated, may hold values from -0.21875 to 0.21875
- conv_x: float32 [7, 24, 64], P(None, 'narrow'), may hold values from -2 to 2
- conv_bc: float32 [7, 256], replicated, may hold values from -2 to 2
- dt_bias: float32 [24, 2], P('narrow'), may hold values from -7 to -3
- a_log: float32 [24], P('narrow'), may hold values from -1 to 1.5
- skip_d: float32 [24], P('narrow'), may hold values from 0.5 to 1.5
- norm_gain: float32 [24, 64], P('narrow'), may hold values from 0.5 to 1.5
- w_out: bfloat16 [24, 64, 768], P('narrow'), may hold values from -0.15625 to 0.15625
- cotangent: bfloat16 [16, 1280, 768], P('wide', 'narrow'), may hold values from -6 to 6
- starts: int32 [16, 4], P('wide'), may hold values from 0 to 1279, as said below
- live: int32 [16, 1280], P('wide'), may hold values from 0 to 1, as said below
Outputs:
- out: bfloat16 [16, 1280, 768], P('wide', 'narrow')
- grad_input: float32 [16, 1280, 768], P('wide', 'narrow')
- grad_pre_gain: float32 [768], P('wide')
- grad_w_heads: float32 [768, 24, 130], P('wide', 'narrow')
- grad_w_bc: float32 [768, 256], P('wide')
- grad_conv_x: float32 [7, 24, 64], P(None, 'narrow', 'wide')
- grad_conv_bc: float32 [7, 256], P(None, 'wide')
- grad_dt_bias: float32 [24, 2], P('narrow')
- grad_a_log: float32 [24], P('narrow')
- grad_skip_d: float32 [24], P('narrow')
- grad_norm_gain: float32 [24, 64], P('narrow', 'wide')
- grad_w_out: float32 [24, 64, 768], P('narrow', None, 'wide')
Inputs may be any that keep to these rules, and one draw needn't show every extreme that they name: Per row the starts are increasing and the first is 0; in every row the second document starts below 160 and the third at or beyond 1280 - 1280 / 16; in some row the last document starts at the row's last position. In every row the live positions are a prefix of the row, of 1200 or more positions.
All inputs are finite; a program needn't handle non-finite values.
Results may differ from a plain program's by a relative error of at most 0.0088.
Values may be sent and summed in bfloat16 or wider, within the bound.
A program may use at most 384 MiB of HBM per device.

v0:
```python
import jax
import jax.numpy as jnp
from jax import lax
from jax.sharding import PartitionSpec as P

H = 24
HD = 64
BLOCK = 128
SEQ_LEN = 1280


EPS = 1e-05
HIGH = lax.Precision.HIGHEST


def rounded(value):
    return value + lax.stop_gradient(value.astype(jnp.bfloat16).astype(jnp.float32) - value)


def segment_ids(starts):
    where_at = jnp.arange(SEQ_LEN, dtype=jnp.int32)
    hits = (starts[:, :, None] <= where_at[None, None, :]).astype(jnp.int32)
    return jnp.sum(hits, axis=1) - 1


def conv_doc(values, taps, seg):
    half = (taps.shape[0] - 1) // 2
    length = values.shape[1]
    padded = jnp.pad(values, ((0, 0), (half, half), (0, 0)))
    seg_pad = jnp.pad(seg, ((0, 0), (half, half)), constant_values=-1)
    total = jnp.zeros_like(values)
    for offset in range(taps.shape[0]):
        same = (seg_pad[:, offset : offset + length] == seg).astype(values.dtype)
        total = total + taps[offset] * padded[:, offset : offset + length] * same[:, :, None]
    return total


def ssd_forward(xc, steps, decays, bmat, cmat, seg, prec):
    rows, length, heads, hdim = xc.shape
    blocks = length // BLOCK
    xb = xc.reshape(rows, blocks, BLOCK, heads, hdim)
    stepb = steps.reshape(rows, blocks, BLOCK, heads)
    cum = jnp.cumsum(decays.reshape(rows, blocks, BLOCK, heads), axis=2)
    bb = bmat.reshape(rows, blocks, BLOCK, -1)
    cb = cmat.reshape(rows, blocks, BLOCK, -1)
    sb = seg.reshape(rows, blocks, BLOCK)
    order = jnp.arange(BLOCK, dtype=jnp.int32)
    causal = order[:, None] >= order[None, :]
    same = ((sb[:, :, :, None] == sb[:, :, None, :]) & causal)[..., None]
    diff = cum[:, :, :, None, :] - cum[:, :, None, :, :]
    weights = jnp.where(same, jnp.exp(jnp.where(same, diff, 0.0)), 0.0)
    inner = jnp.einsum("rbtn,rbsn->rbts", cb, bb, precision=prec)
    mix = weights * inner[..., None] * stepb[:, :, None, :, :]
    intra = jnp.einsum("rbtsh,rbshp->rbthp", mix, xb, precision=prec)
    last = sb[:, :, -1]
    cum_end = cum[:, :, -1, :]
    to_end = (
        (sb == last[:, :, None]).astype(cum.dtype)[..., None]
        * jnp.exp(cum_end[:, :, None, :] - cum)
        * stepb
    )
    states = jnp.einsum("rbshp,rbsn->rbhpn", to_end[..., None] * xb, bb, precision=prec)
    decay_end = jnp.exp(cum_end)

    def carry_step(carry, item):
        state, seg_prev = carry
        block_state, block_last, block_decay = item
        keep = (block_last == seg_prev).astype(state.dtype)[:, None, None, None]
        fresh = keep * block_decay[:, :, None, None] * state + block_state
        return ((fresh, block_last), (state, seg_prev))

    init = (
        jnp.zeros((rows, heads, hdim, bb.shape[-1]), xc.dtype),
        jnp.full((rows,), -1, jnp.int32),
    )
    items = (jnp.moveaxis(states, 1, 0), jnp.moveaxis(last, 1, 0), jnp.moveaxis(decay_end, 1, 0))
    _, (before, seg_before) = lax.scan(carry_step, init, items)
    before = jnp.moveaxis(before, 0, 1)
    seg_before = jnp.moveaxis(seg_before, 0, 1)
    enter = (sb == seg_before[:, :, None]).astype(cum.dtype)[..., None] * jnp.exp(cum)
    inter = jnp.einsum("rbtn,rbhpn->rbthp", cb, before, precision=prec) * enter[..., None]
    return (intra + inter).reshape(rows, length, heads, hdim)


def mixer(proj, bcproj, conv_x, conv_bc, dt_bias, a_log, skip_d, seg, mask, rounder, prec):
    rows, length, heads, width = proj.shape
    hdim = (width - 2) // 2
    state = bcproj.shape[-1] // 4
    gate = proj[..., :hdim]
    values = proj[..., hdim : 2 * hdim] * mask[:, :, None, None]
    mixed_x = conv_doc(
        values.reshape(rows, length, heads * hdim),
        conv_x.reshape(conv_x.shape[0], heads * hdim),
        seg,
    )
    xc = rounder(jax.nn.silu(mixed_x)).reshape(rows, length, heads, hdim)
    maps = rounder(jax.nn.silu(conv_doc(bcproj * mask[:, :, None], conv_bc, seg)))
    b_fwd = maps[..., :state]
    c_fwd = maps[..., state : 2 * state]
    b_bwd = maps[..., 2 * state : 3 * state]
    c_bwd = maps[..., 3 * state :]
    rate = -jnp.exp(a_log)
    dt_fwd = jax.nn.softplus(proj[..., 2 * hdim] + dt_bias[:, 0]) * mask[:, :, None]
    dt_bwd = jax.nn.softplus(proj[..., 2 * hdim + 1] + dt_bias[:, 1]) * mask[:, :, None]
    out_fwd = ssd_forward(xc, dt_fwd, dt_fwd * rate, b_fwd, c_fwd, seg, prec)

    def flip(v):
        return jnp.flip(v, axis=1)

    out_bwd = flip(
        ssd_forward(
            flip(xc), flip(dt_bwd), flip(dt_bwd * rate), flip(b_bwd), flip(c_bwd), flip(seg), prec
        )
    )
    keep_prev = (seg[:, 1:] == seg[:, :-1]).astype(xc.dtype)[:, :, None, None]
    shifted_fwd = jnp.pad(out_fwd[:, :-1] * keep_prev, ((0, 0), (1, 0), (0, 0), (0, 0)))
    shifted_bwd = jnp.pad(out_bwd[:, 1:] * keep_prev, ((0, 0), (0, 1), (0, 0), (0, 0)))
    return (shifted_fwd + shifted_bwd + skip_d[:, None] * xc, gate)


def shards(
    layer_in,
    pre_gain,
    w_heads,
    w_bc,
    conv_x,
    conv_bc,
    dt_bias,
    a_log,
    skip_d,
    norm_gain,
    w_out,
    cotangent,
    starts,
    live,
):
    seg = segment_ids(starts)
    mask = live.astype(jnp.float32)
    x_here = layer_in.astype(jnp.float32)
    scale = lax.rsqrt(jnp.mean(x_here * x_here, axis=-1, keepdims=True) + EPS)
    normed_here = (x_here * scale * pre_gain).astype(jnp.bfloat16)
    normed = lax.all_gather(normed_here, "narrow", axis=1, tiled=True)
    proj = jnp.einsum("rld,dhc->rlhc", normed, w_heads, preferred_element_type=jnp.float32)
    bcproj = jnp.einsum("rld,dc->rlc", normed, w_bc, preferred_element_type=jnp.float32)

    def mix_local(proj_in, bc_in, taps_x, taps_bc, bias_in, log_rate, diag_in):
        return mixer(
            proj_in, bc_in, taps_x, taps_bc, bias_in, log_rate, diag_in, seg, mask, rounded, HIGH
        )

    (ymix, gate), pull_mix = jax.vjp(
        mix_local, proj, bcproj, conv_x, conv_bc, dt_bias, a_log, skip_d
    )
    rows, length, heads, hdim = ymix.shape
    sigma = jax.nn.sigmoid(gate)
    act = gate * sigma
    gated = (ymix * act).reshape(rows, length, heads * hdim)
    squares = lax.psum(jnp.sum(gated * gated, axis=-1), "narrow")
    inv = lax.rsqrt(squares / (H * HD) + EPS)[..., None]
    gain_flat = norm_gain.reshape(-1)
    normalized = gated * inv
    hn = (normalized * gain_flat).astype(jnp.bfloat16)
    w_flat = w_out.reshape(heads * hdim, -1)
    partial_value = jnp.einsum("rlc,cd->rld", hn, w_flat, preferred_element_type=jnp.float32)
    branch = lax.psum_scatter(partial_value, "narrow", scatter_dimension=1, tiled=True)
    out = (x_here + branch).astype(jnp.bfloat16)
    grad_out = lax.all_gather(cotangent, "narrow", axis=1, tiled=True)
    g_w_out = jnp.einsum("rlc,rld->cd", hn, grad_out, preferred_element_type=jnp.float32)
    g_hn = jnp.einsum("rld,cd->rlc", grad_out, w_flat, preferred_element_type=jnp.float32)
    g_gain = jnp.sum(g_hn * normalized, axis=(0, 1))
    weighted = g_hn * gain_flat
    cross = lax.psum(jnp.sum(weighted * gated, axis=-1), "narrow")
    g_gated = inv * weighted - gated * (inv * inv * inv) * (cross / (H * HD))[..., None]
    g_gated = g_gated.reshape(rows, length, heads, hdim)
    g_ymix = g_gated * act
    g_gate = g_gated * ymix * (sigma * (1.0 + gate * (1.0 - sigma)))
    g_proj, g_bcproj, g_conv_x, g_conv_bc, g_dt_bias, g_a_log, g_skip = pull_mix((g_ymix, g_gate))
    g_proj_low = g_proj.astype(jnp.bfloat16)
    g_w_heads = jnp.einsum("rld,rlhc->dhc", normed, g_proj_low, preferred_element_type=jnp.float32)
    g_w_bc = jnp.einsum(
        "rld,rlc->dc", normed, g_bcproj, precision=HIGH, preferred_element_type=jnp.float32
    )
    g_normed = jnp.einsum("rlhc,dhc->rld", g_proj_low, w_heads, preferred_element_type=jnp.float32)
    g_normed = g_normed + jnp.einsum(
        "rlc,dc->rld", g_bcproj, w_bc, precision=HIGH, preferred_element_type=jnp.float32
    )
    g_normed_here = lax.psum_scatter(g_normed, "narrow", scatter_dimension=1, tiled=True)
    weighted_in = g_normed_here * pre_gain
    g_pre = jnp.sum(g_normed_here * x_here * scale, axis=(0, 1))
    g_x = scale * weighted_in - x_here * (scale * scale * scale) * jnp.mean(
        weighted_in * x_here, axis=-1, keepdims=True
    )
    grad_input = cotangent.astype(jnp.float32) + g_x
    g_pre, g_w_bc, g_conv_bc = lax.psum((g_pre, g_w_bc, g_conv_bc), "narrow")
    reduced = (
        lax.psum_scatter(g_w_heads, "wide", scatter_dimension=0, tiled=True),
        lax.psum_scatter(g_w_out.reshape(heads, hdim, -1), "wide", scatter_dimension=2, tiled=True),
        lax.psum_scatter(g_conv_x, "wide", scatter_dimension=2, tiled=True),
        lax.psum_scatter(g_gain.reshape(heads, hdim), "wide", scatter_dimension=1, tiled=True),
        lax.psum_scatter(g_pre, "wide", scatter_dimension=0, tiled=True),
        lax.psum_scatter(g_w_bc, "wide", scatter_dimension=0, tiled=True),
        lax.psum_scatter(g_conv_bc, "wide", scatter_dimension=1, tiled=True),
    )
    share_pre, share_bc, share_conv = (reduced[4], reduced[5], reduced[6])
    head_bias, head_rate, head_diag = lax.psum((g_dt_bias, g_a_log, g_skip), "wide")
    return (
        out,
        grad_input,
        share_pre,
        reduced[0],
        share_bc,
        reduced[2],
        share_conv,
        head_bias,
        head_rate,
        head_diag,
        reduced[3],
        reduced[1],
    )


def solution(mesh):
    return jax.shard_map(
        shards,
        mesh=mesh,
        in_specs=(
            P("wide", "narrow", None),
            P(),
            P(None, "narrow", None),
            P(),
            P(None, "narrow", None),
            P(),
            P("narrow", None),
            P("narrow"),
            P("narrow"),
            P("narrow", None),
            P("narrow", None, None),
            P("wide", "narrow", None),
            P("wide", None),
            P("wide", None),
        ),
        out_specs=(
            P("wide", "narrow", None),
            P("wide", "narrow", None),
            P("wide"),
            P("wide", "narrow", None),
            P("wide", None),
            P(None, "narrow", "wide"),
            P(None, "wide"),
            P("narrow", None),
            P("narrow"),
            P("narrow"),
            P("narrow", "wide"),
            P("narrow", None, "wide"),
        ),
        check_vma=False,
    )
```

profile of v0, /device:TPU:0, one launch (start us, length us, event | category | flops | bytes accessed | tf_op | source)
XLA Modules:
  0.0 1340.2 jit_solution(560317651806766355)
XLA Ops:
  24.5 22.5 %all-gather.3.cloned.1.call-done = bf16[1,1280,768]{2,1,0:T(8,128)(2,1)} async-done(((bf16[1,640,768]{2,1,0:T(8,128)(2,1)}), bf16[1,1280,768]{2,1,0:T(8,128)(2,1)}) %all-gather.3.cloned.1.call-update) | async-done | bytes 1966096 | tf_op jit(solution)/shard_map/all_gather | solution.py:142
  47.1 5.1 convolution_bitcast_fusion
  68.8 5.5 rev.46
  94.6 8.9 subtract_add_fusion
  103.5 6.2 reshape.1847
  114.5 6.4 fusion.106
  123.4 54.1 %while.80 = (s32[]{:T(128)}, f32[1,12,64,64]{3,2,1,0:T(8,128)S(1)}, s32[1]{0:T(128)}, f32[10,1,12,64,64]{4,3,2,1,0:T(8,128)}, s32[10,1]{0,1:T(1,128)S(1)}, /*ind...) while((s32[]{:T(128)}, f32[1,12,64,64]{3,2,1,0:T(8,128)S(1)}, ...), condition=%wide.region_4.6_spmd.clone, body=%wide.region_3.5_spmd.clone.sunk | while | flops 196637 | bytes 1180570 | solution.py:77
  181.0 5.5 fusion.50
  186.6 20.0 %fusion.31 = f32[1,10,12,8,8,128]{5,4,3,2,1,0:T(8,128)S(1)} fusion(f32[10,128,12,64]{1,3,2,0:T(8,128)S(1)} %fusion.50, f32[10,128,12]{1,2,0:T(8,128)S(1)} %exponential_multiply_fusion.1, f32[10,128,12]{1,2,0:T(8,128)S(1)} %get-tuple-element.993, f32[10,128,128]{2,1,0:T(8,128)S(1)} %fusion.257, f32[10,128,12]{1,2,0:T(8,128)S(1)} %bitcast.695, ...), kind=kOutput, calls=%fused_computation.102 | convolution fusion | flops 1521745920 | bytes 12800000 | tf_op jit(solution)/shard_map/jvp(rbtsh,rbshp->rbthp)/dot_general | solution.py:54
  214.6 5.9 rev.48
  220.5 8.1 rev.44
  228.6 6.0 reshape.1854
  234.5 5.7 rev.49
  248.4 6.4 fusion.109
  258.9 88.2 %while.81 = (s32[]{:T(128)}, f32[1,12,64,64]{3,2,1,0:T(8,128)S(1)}, s32[1]{0:T(128)}, f32[10,1,12,64,64]{4,3,2,1,0:T(8,128)}, s32[10,1]{0,1:T(1,128)}, /*index=5...) while((s32[]{:T(128)}, f32[1,12,64,64]{3,2,1,0:T(8,128)S(1)}, ...), condition=%wide.region_7.9_spmd.clone, body=%wide.region_6.8_spmd.clone.sunk | while | flops 196637 | bytes 1181542 | solution.py:77
  348.8 6.0 fusion.46
  356.4 19.1 %fusion.30 = f32[1,10,12,8,8,128]{5,4,3,2,1,0:T(8,128)S(1)} fusion(f32[10,128,12,64]{1,3,2,0:T(8,128)S(1)} %fusion.46, f32[10,128,12]{1,2,0:T(8,128)S(1)} %exponential_multiply_fusion, f32[10,128,12]{1,2,0:T(8,128)S(1)} %copy-done.95, f32[10,128,128]{2,1,0:T(8,128)S(1)} %fusion.258, f32[10,128,12]{1,2,0:T(8,128)S(1)} %bitcast.699, ...), kind=kOutput, calls=%fused_computation.100 | convolution fusion | flops 1521745920 | bytes 12800000 | tf_op jit(solution)/shard_map/jvp(rbtsh,rbshp->rbthp)/dot_general | solution.py:54
  377.8 8.1 reverse.6
  390.8 5.6 multiply_reduce_fusion.13
  396.4 5.0 psum.56
  401.4 8.3 multiply_reduce_fusion.2
  409.8 5.0 psum.57
  420.4 5.9 multiply_reduce_fusion.3
  434.0 6.1 reshape.1873
  440.1 8.7 fusion.103
  448.8 10.7 fusion.150
  462.5 8.1 rev.50
  470.5 6.0 reshape.1870
  476.5 6.0 reshape.1865
  482.5 9.0 fusion.100
  491.5 10.5 fusion.155
  502.1 6.0 reshape.1875
  516.3 51.3 %while.82 = (s32[]{:T(128)}, f32[1,12,64,64]{3,2,1,0:T(8,128)S(1)}, f32[10,1,12,64,64]{4,3,2,1,0:T(8,128)}, f32[10,1,12]{2,1,0:T(1,128)}, f32[10,1,12,64,64]{4,3...) while((s32[]{:T(128)}, f32[1,12,64,64]{3,2,1,0:T(8,128)S(1)}, ...), condition=%wide.region_16.18_spmd.clone, body=%wide.region_14.17_spmd.clone.sunk | while | flops 294916 | bytes 1377688 | solution.py:77
  567.6 7.8 fusion.26
  577.5 6.2 multiply_reduce_fusion.12
  585.9 6.1 multiply_reduce_fusion.11
  595.1 51.2 %while.83 = (s32[]{:T(128)}, f32[1,12,64,64]{3,2,1,0:T(8,128)S(1)}, f32[10,1,12,64,64]{4,3,2,1,0:T(8,128)}, f32[10,1,12]{2,1,0:T(1,128)}, f32[10,1,12,64,64]{4,3...) while((s32[]{:T(128)}, f32[1,12,64,64]{3,2,1,0:T(8,128)S(1)}, ...), condition=%wide.region_25.27_spmd.clone, body=%wide.region_23.26_spmd.clone.sunk | while | flops 294916 | bytes 1377688 | solution.py:77
  646.3 9.6 fusion.32
  658.8 22.1 %fusion.23 = (f32[10,128,12]{1,2,0:T(8,128)}, f32[10,128,12]{1,2,0:T(8,128)}, f32[10,128,12]{1,2,0:T(8,128)}, f32[10,128,128]{2,1,0:T(8,128)S(1)}) fusion(f32[10,128,12]{1,2,0:T(8,128)S(1)} %copy-done.91, f32[10,128,128]{2,1,0:T(8,128)} %copy-done.65, f32[10,128,12]{1,2,0:T(8,128)S(1)} %bitcast.696, pred[10,128,128]{2,1,0:T(8,128)(4,1)} %get-tuple-element.1045, ...), kind=kOutput, calls=%fused_computation.67 | convolution fusion | flops 1539230720 | bytes 9646080 | tf_op jit(solution)/shard_map/transpose(jvp(rbtsh,rbshp->rbthp))/dot_general | solution.py:54
  682.2 10.6 fusion.175
  697.6 25.3 %fusion.21 = (f32[10,128,12]{1,2,0:T(8,128)}, f32[10,128,12]{1,2,0:T(8,128)}, f32[10,128,12]{1,2,0:T(8,128)}, f32[10,128,128]{2,1,0:T(8,128)S(1)}) fusion(f32[10,128,12]{1,2,0:T(8,128)} %bitcast.698, f32[10,128,128]{2,1,0:T(8,128)} %copy-done.67, f32[10,128,12]{1,2,0:T(8,128)} %get-tuple-element.996, pred[10,128,128]{2,1,0:T(8,128)(4,1)} %get-tuple-element.1046, ...), kind=kOutput, calls=%fused_computation.65 | convolution fusion | flops 1539230720 | bytes 9646080 | tf_op jit(solution)/shard_map/transpose(jvp(rbtsh,rbshp->rbthp))/dot_general | solution.py:54
  724.2 10.6 fusion.165
  736.0 5.9 rev.55
  749.9 9.6 multiply_reduce_fusion.20
  759.6 5.3 multiply_multiply_fusion.26
  765.1 11.1 fusion.28
  776.2 10.3 fusion.29
  788.7 8.1 rev.53
  796.7 5.4 bitcast_add_fusion.4
  803.5 9.3 multiply_reduce_fusion.10
  812.8 7.8 multiply_multiply_fusion.12
  820.6 10.7 pad_add_fusion.1
  866.0 6.6 fusion.193
  896.9 6.4 fusion.243
  909.3 5.1 fusion.130
  920.8 6.8 fusion.122
  927.9 11.5 fusion.126
  942.9 27.1 %reduce-scatter.17.cloned.1.call-done = f32[7,12,4]{1,0,2:T(8,128)} async-done(((f32[7,12,64]{1,0,2:T(8,128)}), f32[7,12,4]{1,0,2:T(8,128)}) %reduce-scatter.17.cloned.1.call-update) | async-done | bytes 1360 | tf_op jit(solution)/shard_map/reduce_scatter | solution.py:198
  971.4 51.8 %reduce-scatter.13.cloned.1.call-done = f32[1,640,768]{2,1,0:T(8,128)} async-done(((f32[1,1280,768]{2,1,0:T(8,128)}), f32[1,640,768]{2,1,0:T(8,128)}) %reduce-scatter.13.cloned.1.call-update) | async-done | bytes 1966096 | tf_op jit(solution)/shard_map/reduce_scatter | solution.py:187
  1025.5 61.4 %all-reduce.49 = (f32[768]{0:T(1024)S(1)}, f32[12,2]{0,1:T(2,128)}, f32[12]{0:T(128)}, f32[12]{0:T(128)}, f32[12,64]{1,0:T(8,128)S(1)}) all-reduce(f32[768]{0:T(1024)S(1)} %get-tuple-element.877, f32[12,2]{0,1:T(2,128)S(1)} %pad_add_fusion.15, f32[12]{0:T(128)S(1)} %negate_multiply_fusion, ...), channel_id=4, replica_groups=mesh['wide'=16,'narrow'=2] {'wide'}, use_global_device_ids=true, to_apply=%region_39.41.clone | all-reduce | flops 1584 | bytes 12672
  1087.7 10.0 all-reduce.50
  1097.7 40.2 %reduce-scatter.11.cloned.1.call-done = f32[1,640,768]{2,1,0:T(8,128)} async-done(((f32[1,1280,768]{2,1,0:T(8,128)}), f32[1,640,768]{2,1,0:T(8,128)}) %reduce-scatter.11.cloned.1.call-update) | async-done | bytes 1966096 | tf_op jit(solution)/shard_map/reduce_scatter | solution.py:165
  1142.7 75.3 %reduce-scatter.19.cloned.1.call-done = f32[12,64,48]{1,2,0:T(8,128)} async-done(((f32[12,64,768]{1,2,0:T(8,128)}), f32[12,64,48]{1,2,0:T(8,128)}) %reduce-scatter.19.cloned.1.call-update) | async-done | bytes 147472 | tf_op jit(solution)/shard_map/reduce_scatter | solution.py:197
  1218.0 115.1 %reduce-scatter.15.cloned.1.call-done = f32[48,12,130]{2,0,1:T(8,128)} async-done(((f32[768,12,130]{2,0,1:T(8,128)}), f32[48,12,130]{2,0,1:T(8,128)}) %reduce-scatter.15.cloned.1.call-update) | async-done | bytes 299536 | tf_op jit(solution)/shard_map/reduce_scatter | solution.py:196
  (802 shorter events, 449.7 us)
Async XLA Ops:
  7.2 39.9 %copy-start = (bf16[768,12,130]{0,2,1:T(8,128)(2,1)S(1)}, bf16[768,12,130]{0,2,1:T(8,128)(2,1)}, u32[]{:S(2)}) copy-start(bf16[768,12,130]{0,2,1:T(8,128)(2,1)} %param.25) | copy-start | bytes 7188484
  7.3 39.8 %all-gather.3.cloned.1.call-start = ((), (), s32[]{:S(2)}) async-start(), calls=%async_computation.7 | async-start | bytes 2949120 | tf_op jit(solution)/shard_map/all_gather | solution.py:142
  12.6 388.9 %all-gather.5.cloned.1.call-start = ((), (), s32[]{:S(2)}) async-start(), calls=%async_computation.9 | async-start | bytes 2949120 | tf_op jit(solution)/shard_map/all_gather | solution.py:167
  14.0 928.1 %reduce-scatter.23.cloned.1.call-start = ((), (), s32[]{:S(2)}) async-start(), calls=%async_computation.15 | async-start | bytes 139264
  14.2 38.0 %copy-start.98 = (s32[1280]{0:T(1024)}, s32[1280]{0:T(1024)S(1)}, u32[]{:S(2)}) copy-start(s32[1280]{0:T(1024)S(1)} %convert_reduce_fusion) | copy-start | bytes 15364
  14.3 37.9 %copy-start.107 = (s32[1280]{0:T(1024)}, s32[1280]{0:T(1024)S(1)}, u32[]{:S(2)}) copy-start(s32[1280]{0:T(1024)S(1)} %reverse.5) | copy-start | bytes 15364
  14.5 79.0 %copy-start.70 = (f32[1280]{0:T(1024)}, f32[1280]{0:T(1024)S(1)}, u32[]{:S(2)}) copy-start(f32[1280]{0:T(1024)S(1)} %get-tuple-element.895) | copy-start | bytes 15364
  14.5 79.0 %copy-start.72 = (f32[1280]{0:T(1024)}, f32[1280]{0:T(1024)S(1)}, u32[]{:S(2)}) copy-start(f32[1280]{0:T(1024)S(1)} %get-tuple-element.896) | copy-start | bytes 15364
  14.5 79.0 %copy-start.74 = (f32[1280]{0:T(1024)}, f32[1280]{0:T(1024)S(1)}, u32[]{:S(2)}) copy-start(f32[1280]{0:T(1024)S(1)} %get-tuple-element.897) | copy-start | bytes 15364
  14.5 79.0 %copy-start.76 = (f32[1280]{0:T(1024)}, f32[1280]{0:T(1024)S(1)}, u32[]{:S(2)}) copy-start(f32[1280]{0:T(1024)S(1)} %get-tuple-element.898) | copy-start | bytes 15364
  14.5 79.0 %copy-start.78 = (f32[1280]{0:T(1024)}, f32[1280]{0:T(1024)S(1)}, u32[]{:S(2)}) copy-start(f32[1280]{0:T(1024)S(1)} %get-tuple-element.899) | copy-start | bytes 15364
  14.5 79.0 %copy-start.80 = (f32[1280]{0:T(1024)}, f32[1280]{0:T(1024)S(1)}, u32[]{:S(2)}) copy-start(f32[1280]{0:T(1024)S(1)} %get-tuple-element.900) | copy-start | bytes 15364
  15.5 36.7 %copy-start.116 = (f32[10,128]{1,0:T(8,128)}, f32[10,128]{1,0:T(8,128)S(1)}, u32[]{:S(2)}) copy-start(f32[10,128]{1,0:T(8,128)S(1)} %compare_convert_fusion.8) | copy-start | bytes 15364
  16.4 35.8 %copy-start.114 = (f32[10,128]{1,0:T(8,128)}, f32[10,128]{1,0:T(8,128)S(1)}, u32[]{:S(2)}) copy-start(f32[10,128]{1,0:T(8,128)S(1)} %compare_convert_fusion.10) | copy-start | bytes 15364
  17.1 68.3 %copy-start.82 = (f32[1280]{0:T(1024)}, f32[1280]{0:T(1024)S(1)}, u32[]{:S(2)}) copy-start(f32[1280]{0:T(1024)S(1)} %convert_reduce_fusion.1) | copy-start | bytes 15364
  17.7 70.0 %copy-start.148 = (f32[1,256]{1,0:T(1,128)}, f32[1,256]{1,0:T(1,128)S(1)}, u32[]{:S(2)}) copy-start(f32[1,256]{1,0:T(1,128)S(1)} %get-tuple-element.1054) | copy-start | bytes 3076
  20.8 72.7 %copy-start.128 = (f32[768]{0:T(1024)}, f32[768]{0:T(1024)S(1)}, u32[]{:S(2)}) copy-start(f32[768]{0:T(1024)S(1)} %mul.1672) | copy-start | bytes 9220
  20.9 72.6 %copy-start.130 = (f32[768]{0:T(1024)}, f32[768]{0:T(1024)S(1)}, u32[]{:S(2)}) copy-start(f32[768]{0:T(1024)S(1)} %mul.1665) | copy-start | bytes 9220
  21.0 72.6 %copy-start.132 = (f32[768]{0:T(1024)}, f32[768]{0:T(1024)S(1)}, u32[]{:S(2)}) copy-start(f32[768]{0:T(1024)S(1)} %mul.1658) | copy-start | bytes 9220
  21.0 72.5 %copy-start.134 = (f32[768]{0:T(1024)}, f32[768]{0:T(1024)S(1)}, u32[]{:S(2)}) copy-start(f32[768]{0:T(1024)S(1)} %mul.1655) | copy-start | bytes 9220
  21.1 72.5 %copy-start.136 = (f32[768]{0:T(1024)}, f32[768]{0:T(1024)S(1)}, u32[]{:S(2)}) copy-start(f32[768]{0:T(1024)S(1)} %mul.1648) | copy-start | bytes 9220
  21.2 72.4 %copy-start.138 = (f32[768]{0:T(1024)}, f32[768]{0:T(1024)S(1)}, u32[]{:S(2)}) copy-start(f32[768]{0:T(1024)S(1)} %mul.1641) | copy-start | bytes 9220
  21.2 72.3 %copy-start.140 = (f32[768]{0:T(1024)}, f32[768]{0:T(1024)S(1)}, u32[]{:S(2)}) copy-start(f32[768]{0:T(1024)S(1)} %mul.1626) | copy-start | bytes 9220
  24.5 30.9 %copy-start.159 = (f32[12]{0:T(128)S(1)}, f32[12]{0:T(128)}, u32[]{:S(2)}) copy-start(f32[12]{0:T(128)} %get-tuple-element.1063) | copy-start | bytes 148
  24.5 30.9 %copy-start.161 = (f32[12]{0:T(128)S(1)}, f32[12]{0:T(128)}, u32[]{:S(2)}) copy-start(f32[12]{0:T(128)} %get-tuple-element.1064) | copy-start | bytes 148
  57.0 27.7 %copy-start.63 = (f32[1280,12]{0,1:T(8,128)}, f32[1280,12]{0,1:T(8,128)S(1)}, u32[]{:S(2)}) copy-start(f32[1280,12]{0,1:T(8,128)S(1)} %get-tuple-element.886) | copy-start | bytes 184324
  64.4 122.1 %copy-start.55 = (f32[1,10,128,12]{2,3,1,0:T(8,128)}, f32[1,10,128,12]{2,3,1,0:T(8,128)S(1)}, u32[]{:S(2)}) copy-start(f32[1,10,128,12]{2,3,1,0:T(8,128)S(1)} %copy.565) | copy-start | bytes 184324
  111.2 75.4 %copy-start.90 = (f32[10,128,12]{1,2,0:T(8,128)}, f32[10,128,12]{1,2,0:T(8,128)S(1)}, u32[]{:S(2)}) copy-start(f32[10,128,12]{1,2,0:T(8,128)S(1)} %get-tuple-element.993) | copy-start | bytes 184324
  123.3 54.7 %copy-start.99 = (s32[1280]{0:T(1024)S(1)}, s32[1280]{0:T(1024)}, u32[]{:S(2)}) copy-start(s32[1280]{0:T(1024)} %copy-done.98) | copy-start | bytes 15364
  186.5 20.1 %copy-start.29 = (f32[10,128,12,64]{1,3,2,0:T(8,128)}, f32[10,128,12,64]{1,3,2,0:T(8,128)S(1)}, u32[]{:S(2)}) copy-start(f32[10,128,12,64]{1,3,2,0:T(8,128)S(1)} %fusion.50) | copy-start | bytes 11796484
  213.3 141.6 %copy-start.22 = (f32[1,1280,64]{2,1,0:T(8,128)}, f32[1,1280,64]{2,1,0:T(8,128)S(1)}, u32[]{:S(2)}) copy-start(f32[1,1280,64]{2,1,0:T(8,128)S(1)} %rev.47) | copy-start | bytes 983044
  354.8 20.7 %copy-start.30 = (f32[10,128,12,64]{1,3,2,0:T(8,128)}, f32[10,128,12,64]{1,3,2,0:T(8,128)S(1)}, u32[]{:S(2)}) copy-start(f32[10,128,12,64]{1,3,2,0:T(8,128)S(1)} %fusion.46) | copy-start | bytes 11796484
  356.4 19.2 %copy-start.67 = (f32[10,128,128]{2,1,0:T(8,128)}, f32[10,128,128]{2,1,0:T(8,128)S(1)}, u32[]{:S(2)}) copy-start(f32[10,128,128]{2,1,0:T(8,128)S(1)} %fusion.258) | copy-start | bytes 1966084
  655.9 25.1 %copy-start.53 = (f32[10,128,12]{1,2,0:T(8,128)}, f32[10,128,12]{1,2,0:T(8,128)S(1)}, u32[]{:S(2)}) copy-start(f32[10,128,12]{1,2,0:T(8,128)S(1)} %get-tuple-element.1068) | copy-start | bytes 184324
  658.8 23.4 %copy-start.10 = (f32[10,1,12,64,64]{4,3,2,1,0:T(8,128)S(1)}, f32[10,1,12,64,64]{4,3,2,1,0:T(8,128)}, u32[]{:S(2)}) copy-start(f32[10,1,12,64,64]{4,3,2,1,0:T(8,128)} %get-tuple-element.461) | copy-start | bytes 5898244
  697.6 25.3 %copy-start.23 = (f32[1,1280,64]{2,1,0:T(8,128)S(1)}, f32[1,1280,64]{2,1,0:T(8,128)}, u32[]{:S(2)}) copy-start(f32[1,1280,64]{2,1,0:T(8,128)} %copy-done.22) | copy-start | bytes 983044
  697.6 26.6 %copy-start.11 = (f32[10,1,12,64,64]{4,3,2,1,0:T(8,128)S(1)}, f32[10,1,12,64,64]{4,3,2,1,0:T(8,128)}, u32[]{:S(2)}) copy-start(f32[10,1,12,64,64]{4,3,2,1,0:T(8,128)} %get-tuple-element.456) | copy-start | bytes 5898244
  724.2 17.7 %copy-start.26 = (f32[1,1280,64]{2,1,0:T(8,128)S(1)}, f32[1,1280,64]{2,1,0:T(8,128)}, u32[]{:S(2)}) copy-start(f32[1,1280,64]{2,1,0:T(8,128)} %rev.48) | copy-start | bytes 983044
  734.8 14.9 %copy-start.71 = (f32[1280]{0:T(1024)S(1)}, f32[1280]{0:T(1024)}, u32[]{:S(2)}) copy-start(f32[1280]{0:T(1024)} %copy-done.70) | copy-start | bytes 15364
  734.8 14.9 %copy-start.73 = (f32[1280]{0:T(1024)S(1)}, f32[1280]{0:T(1024)}, u32[]{:S(2)}) copy-start(f32[1280]{0:T(1024)} %copy-done.72) | copy-start | bytes 15364
  734.8 14.9 %copy-start.75 = (f32[1280]{0:T(1024)S(1)}, f32[1280]{0:T(1024)}, u32[]{:S(2)}) copy-start(f32[1280]{0:T(1024)} %copy-done.74) | copy-start | bytes 15364
  734.9 14.9 %copy-start.77 = (f32[1280]{0:T(1024)S(1)}, f32[1280]{0:T(1024)}, u32[]{:S(2)}) copy-start(f32[1280]{0:T(1024)} %copy-done.76) | copy-start | bytes 15364
  734.9 14.9 %copy-start.79 = (f32[1280]{0:T(1024)S(1)}, f32[1280]{0:T(1024)}, u32[]{:S(2)}) copy-start(f32[1280]{0:T(1024)} %copy-done.78) | copy-start | bytes 15364
  734.9 14.9 %copy-start.81 = (f32[1280]{0:T(1024)S(1)}, f32[1280]{0:T(1024)}, u32[]{:S(2)}) copy-start(f32[1280]{0:T(1024)} %copy-done.80) | copy-start | bytes 15364
  749.9 15.1 %copy-start.48 = (f32[10,12,64,128]{3,2,1,0:T(8,128)S(1)}, f32[10,12,64,128]{3,2,1,0:T(8,128)}, u32[]{:S(2)}) copy-start(f32[10,12,64,128]{3,2,1,0:T(8,128)} %get-tuple-element.1069) | copy-start | bytes 11796484
  759.6 16.5 %slice-start = ((s8[6291456]{0:T(1024)(128)(4,1)}), s8[4194304]{0:T(1024)(128)(4,1)S(1)}, s32[]{:S(2)}) async-start(s8[6291456]{0:T(1024)(128)(4,1)} %bitcast.687), calls=%async_computation.16 | async-start | bytes 8388608
  837.9 25.2 %copy-start.17 = (f32[1,10,128,12]{3,1,2,0:T(8,128)S(1)}, f32[1,10,128,12]{3,1,2,0:T(8,128)}, u32[]{:S(2)}) copy-start(f32[1,10,128,12]{3,1,2,0:T(8,128)} %copy-done.16) | copy-start | bytes 184324
  857.1 112.9 %reduce-scatter.17.cloned.1.call-start = ((), (), s32[]{:S(2)}) async-start(), calls=%async_computation.12 | async-start | bytes 278528 | tf_op jit(solution)/shard_map/reduce_scatter | solution.py:198
  880.1 14.6 %copy-start.102 = (f32[1,1280,12]{1,0,2:T(1,128)S(1)}, f32[1,1280,12]{1,0,2:T(1,128)}, u32[]{:S(2)}) copy-start(f32[1,1280,12]{1,0,2:T(1,128)} %get-tuple-element.994) | copy-start | bytes 184324
  880.1 14.6 %copy-start.103 = (f32[1,1280,12]{1,0,2:T(1,128)S(1)}, f32[1,1280,12]{1,0,2:T(1,128)}, u32[]{:S(2)}) copy-start(f32[1,1280,12]{1,0,2:T(1,128)} %get-tuple-element.1013) | copy-start | bytes 184324
  880.2 14.6 %copy-start.145 = (f32[1280]{0:T(1024)S(1)}, f32[1280]{0:T(1024)}, u32[]{:S(2)}) copy-start(f32[1280]{0:T(1024)} %fusion.225) | copy-start | bytes 15364
  880.2 14.6 %copy-start.160 = (f32[12]{0:T(128)S(1)}, f32[12]{0:T(128)}, u32[]{:S(2)}) copy-start(f32[12]{0:T(128)} %get-tuple-element.1063) | copy-start | bytes 148
  880.2 14.6 %copy-start.162 = (f32[12]{0:T(128)S(1)}, f32[12]{0:T(128)}, u32[]{:S(2)}) copy-start(f32[12]{0:T(128)} %get-tuple-element.1064) | copy-start | bytes 148
  880.2 14.6 %copy-start.171 = (f32[12]{0:T(128)S(1)}, f32[12]{0:T(128)}, u32[]{:S(2)}) copy-start(f32[12]{0:T(128)} %exponential_negate_fusion) | copy-start | bytes 148
  894.4 128.8 %reduce-scatter.13.cloned.1.call-start = ((), (), s32[]{:S(2)}) async-start(), calls=%async_computation.10 | async-start | bytes 5898240 | tf_op jit(solution)/shard_map/reduce_scatter | solution.py:187
  909.2 178.5 %reduce-scatter.21.cloned.1.call-start = ((), (), s32[]{:S(2)}) async-start(), calls=%async_computation.14 | async-start | bytes 835584 | tf_op jit(solution)/shard_map/reduce_scatter | solution.py:201
  914.4 223.6 %reduce-scatter.11.cloned.1.call-start = ((), (), s32[]{:S(2)}) async-start(), calls=%async_computation.8 | async-start | bytes 5898240 | tf_op jit(solution)/shard_map/reduce_scatter | solution.py:165
  920.7 297.3 %reduce-scatter.19.cloned.1.call-start = ((), (), s32[]{:S(2)}) async-start(), calls=%async_computation.13 | async-start | bytes 5013504 | tf_op jit(solution)/shard_map/reduce_scatter | solution.py:197
  927.6 405.6 %reduce-scatter.15.cloned.1.call-start = ((), (), s32[]{:S(2)}) async-start(), calls=%async_computation.11 | async-start | bytes 10027008 | tf_op jit(solution)/shard_map/reduce_scatter | solution.py:196
  939.5 83.7 %copy-start.32 = (bf16[1,640,768]{2,1,0:T(8,128)(2,1)S(1)}, bf16[1,640,768]{2,1,0:T(8,128)(2,1)}, u32[]{:S(2)}) copy-start(bf16[1,640,768]{2,1,0:T(8,128)(2,1)} %param.23) | copy-start | bytes 2949124
  939.5 83.7 %copy-start.126 = (f32[640]{0:T(1024)S(1)}, f32[640]{0:T(1024)}, u32[]{:S(2)}) copy-start(f32[640]{0:T(1024)} %copy-done.125) | copy-start | bytes 7684
  939.5 83.7 %copy-start.127 = (f32[768]{0:T(1024)S(1)}, f32[768]{0:T(1024)}, u32[]{:S(2)}) copy-start(f32[768]{0:T(1024)} %param.24) | copy-start | bytes 9220
  939.5 86.0 %copy-start.169 = (f32[12]{0:T(128)S(1)}, f32[12]{0:T(128)}, u32[]{:S(2)}) copy-start(f32[12]{0:T(128)} %get-tuple-element.983) | copy-start | bytes 148
  939.5 198.5 %copy-start.146 = (f32[640]{0:T(1024)S(1)}, f32[640]{0:T(1024)}, u32[]{:S(2)}) copy-start(f32[640]{0:T(1024)} %get-tuple-element.1061) | copy-start | bytes 7684
  (125 other events, 883.1 us)
Sparse Core Ops, SparseCore 0:
  12.7 34.3 all-gather.2
  48.6 31.6 all-gather.4
  857.2 55.0 reduce-scatter.22
  915.7 54.3 reduce-scatter.16
  972.1 51.0 reduce-scatter.12
  1027.6 56.5 reduce-scatter.20
  1086.4 51.4 reduce-scatter.10
  1142.9 75.0 reduce-scatter.18
  1222.7 110.4 reduce-scatter.14
where the time goes:
time: 1360 us; the launch traced here: 1340 us
  waiting for transfers between devices  332 us (24%)
  local copies, waits for them, and re-layouts  310 us (23%)
  other arithmetic  296 us (22%)
  matrix products  275 us (20%)
  blocking collectives  81.4 us (6%)
  loops' own time  27.1 us (2%)
  between operations  17.9 us (1%)
    reduce_scatter x1, waiting for transfers between devices, shards(): lax.psum_scatter(g_w_heads, 'wide', scatter_dimension=0, tiled=True)  115 us
    dot_general x6, matrix products, ssd_forward(): intra = jnp.einsum('rbtsh,rbshp->rbthp', mix, xb, precision=prec)  108 us
    reduce_scatter x1, waiting for transfers between devices, shards(): lax.psum_scatter(g_w_out.reshape(heads, hdim, -1), 'wide', scatter_dimens...  75.3 us
    dynamic_update_slice x80, other arithmetic, ssd_forward(): _, (before, seg_before) = lax.scan(carry_step, init, items)  73.4 us
    unnamed x1, blocking collectives  61.4 us
    rev x11, local copies, waits for them, and re-layouts, flip(): return jnp.flip(v, axis=1)  61 us
    reduce_scatter x1, waiting for transfers between devices, shards(): lax.psum_scatter(g_normed, 'narrow', scatter_dimension=1, tiled=True)  51.8 us
    dot_general x6, matrix products, ssd_forward(): jnp.einsum('rbshp,rbsn->rbhpn', to_end[..., None] * xb, bb, precision=prec)  51.5 us
  transfers between devices with their start and end apart: 9, of which 6 were waited for; matrix products, arithmetic and copies ran while one was open for 31% of the time, Pallas kernels for 0%

commit v1 on v0

--- a/solution.py
+++ b/solution.py
@@ -1,6 +1,10 @@
+import functools
+
 import jax
 import jax.numpy as jnp
 from jax import lax
+from jax.experimental import pallas as pl
+from jax.experimental.pallas import tpu as pltpu
 from jax.sharding import PartitionSpec as P
 
 H = 24
@@ -219,9 +223,1025 @@
     )
 
 
+HALO = 16
+F32 = jnp.float32
+BF16 = jnp.bfloat16
+LOGZERO = -1e30
+VMEM_LIMIT = 56 * 2**20
+
+
+def mm(a, b, dims=((1,), (0,)), precision=None):
+    return lax.dot_general(a, b, (dims, ((), ())), precision=precision, preferred_element_type=F32)
+
+
+def nt(a, b):
+    return mm(a, b, ((1,), (1,)))
+
+
+def tn(a, b):
+    return mm(a, b, ((0,), (0,)))
+
+
+def seg_at(info, pos):
+    seg = jnp.full(pos.shape, -1, jnp.int32)
+    for j in range(4):
+        seg = seg + (pos >= info[j]).astype(jnp.int32)
+    return jnp.where(pos >= info[6], 99, seg)
+
+
+def iota(shape, dim):
+    return lax.broadcasted_iota(jnp.int32, shape, dim)
+
+
+def silu_parts(v):
+    sg = 1.0 / (1.0 + jnp.exp(-v))
+    return v * sg, sg * (1.0 + v * (1.0 - sg))
+
+
+def conv_taps(src, seg_src, taps, first, rows):
+    seg0 = seg_src[first : first + rows, :]
+    total = src[first : first + rows, :] * taps[3:4, :]
+    for k in (0, 1, 2, 4, 5, 6):
+        lo = first + k - 3
+        same = seg_src[lo : lo + rows, :] == seg0
+        total = total + jnp.where(same, src[lo : lo + rows, :], 0.0) * taps[k : k + 1, :]
+    return total
+
+
+def front_kernel(
+    length, hl, starts, live_ref, x_in, edge, gain, wdt_a, wdt_b, wbc_ref, taps_ref, small_a, small_b,
+    info, taps_o, gain_o, skip_o, wdt, wbc, taps, normed_o, rs_o, bcm_o, dsl_o, b_o, bk_o, bkt_o, c_o, ce_o, cet_o, g_o, gt_o,
+    colt_o, rows_o, coltt_o, rowst_o, et_o, wt_o, dpt_o, dt_o, sig_o, seg_s, maps_s, cum_s, x_s,
+):
+    nb = length // BLOCK
+    ext = length + 2 * HALO
+    dm = x_in.shape[1]
+    n = lax.axis_index("narrow")
+    for i in range(4):
+        info[i] = starts[0, i]
+    count = jnp.sum(live_ref[...].astype(F32)).astype(jnp.int32)
+    off = n * length
+    info[4] = count
+    info[5] = off
+    info[6] = live_ref.shape[1]
+    info[7] = n
+    ch = small_a.shape[1]
+    taps_o[:, 0:ch] = small_a[0:8, :]
+    taps_o[:, ch : 2 * ch] = small_b[0:8, :]
+    gain_o[:, 0:ch] = small_a[8:16, :]
+    gain_o[:, ch : 2 * ch] = small_b[8:16, :]
+    skip_o[:, 0:ch] = small_a[16:24, :]
+    skip_o[:, ch : 2 * ch] = small_b[16:24, :]
+    src = iota((2 * hl, 128), 0)
+    dst = iota((2 * hl, 128), 1)
+    place = (src % 2) * 64 + src // 2
+    one = jnp.float32(1.0)
+    at_a = jnp.where(dst == place, one, 0.0).astype(BF16)
+    at_b = jnp.where(dst == place + hl, one, 0.0).astype(BF16)
+    wdt[...] = (mm(wdt_a[...], at_a) + mm(wdt_b[...], at_b)).astype(BF16)
+    wbc[...] = pack_columns(wbc_ref[...])
+    taps[...] = pack_columns(taps_ref[...])
+
+    bias = small_a[24:25, 0:128] + pltpu.roll(small_b[24:25, 0:128], hl, 1)
+    alog = small_a[25:26, 0:128] + pltpu.roll(small_b[25:26, 0:128], hl, 1)
+    zero_edge = jnp.zeros((HALO, dm), BF16)
+    x_s[0:HALO, :] = jnp.where(n == 1, edge[...], zero_edge)
+    x_s[HALO : HALO + length, :] = x_in[...]
+    x_s[HALO + length : ext, :] = jnp.where(n == 1, zero_edge, edge[...])
+    x = x_s[...].astype(F32)
+    rs = lax.rsqrt(jnp.mean(x * x, axis=1, keepdims=True) + EPS)
+    normed = (x * rs * gain[...]).astype(BF16)
+    normed_o[...] = normed
+    rs_o[...] = rs[HALO : HALO + length, :]
+    pos256 = iota((ext, 256), 0) + (off - HALO)
+    seg_s[...] = seg_at(info, pos256)
+    live = pos256 < count
+    bcm_o[...] = jnp.where(live, mm(normed, wbc[...]), 0.0)
+    crows = length + HALO
+    cfirst = HALO // 2
+    mix = conv_taps(bcm_o, seg_s, taps, cfirst, crows)
+    maps, dsl = silu_parts(mix)
+    dsl_o[...] = jnp.zeros_like(dsl_o)
+    dsl_o[cfirst : cfirst + crows, :] = dsl
+    maps_s[...] = jnp.zeros_like(maps_s)
+    maps_s[cfirst : cfirst + crows, :] = maps.astype(BF16).astype(F32)
+    own = slice(HALO, HALO + length)
+    segx = seg_s[own, 0:128]
+    lane = iota((length, 128), 1)
+    fwd = lane < 64
+    segp = seg_s[HALO - 1 : HALO - 1 + length, 0:128]
+    segn = seg_s[HALO + 1 : HALO + 1 + length, 0:128]
+    bmap = maps_s[own, 0:128]
+    cprev = jnp.where(segp == segx, maps_s[HALO - 1 : HALO - 1 + length, 128:256], 0.0)
+    cnext = jnp.where(segn == segx, maps_s[HALO + 1 : HALO + 1 + length, 128:256], 0.0)
+    cmap = jnp.where(fwd, cprev, cnext)
+    b_o[...] = bmap.astype(BF16)
+    c_o[...] = cmap.astype(BF16)
+    raw = mm(normed[own, :], wdt[...]) + bias
+    softp = jnp.maximum(raw, 0.0) + jnp.log(1.0 + jnp.exp(-jnp.abs(raw)))
+    softp = jnp.where(raw < -15.0, jnp.exp(jnp.minimum(raw, 0.0)), softp)
+    pos128 = iota((length, 128), 0) + off
+    m = pos128 < count
+    dt = jnp.where(m, softp, 0.0)
+    sg = jnp.where(m, 1.0 / (1.0 + jnp.exp(-raw)), 0.0)
+    ratio = jnp.where(m, jnp.where(raw < -15.0, 1.0, sg / jnp.maximum(softp, 1e-30)), 0.0)
+    rate = -jnp.exp(alog)
+    a = dt * rate
+    dt_o[...] = a
+    sig_o[:, 0:128] = sg * rate
+    sig_o[:, 128:256] = ratio
+    tri = (iota((BLOCK, BLOCK), 0) >= iota((BLOCK, BLOCK), 1)).astype(F32)
+    logdt = jnp.maximum(jnp.log(dt), LOGZERO)
+    sub = iota((BLOCK, BLOCK), 0)
+    ln = iota((BLOCK, BLOCK), 1)
+    fwdb = ln < 64
+    cum_s[...] = jnp.zeros_like(cum_s)
+    dvals, ends = [], []
+    for b in range(nb):
+        blk = slice(b * BLOCK, (b + 1) * BLOCK)
+        ab = a[blk, :]
+        cum = mm(tri, ab, precision=HIGH)
+        cx = cum - ab
+        end = cum[BLOCK - 1 : BLOCK, :]
+        colt = jnp.where(fwdb, cx, end - cum)
+        rows = jnp.where(fwdb, logdt[blk, :] - cum, cx + logdt[blk, :] - end)
+        colt_o[blk, :] = colt
+        rows_o[blk, :] = rows
+        coltt = colt.T
+        coltt_o[b] = coltt
+        et_o[b] = jnp.exp(coltt)
+        rowst_o[b] = rows.T
+        wt_o[b] = jnp.exp(jnp.minimum(rows + end, 60.0)).T
+        first_pos = off + b * BLOCK
+        sp = seg_at(info, sub + first_pos)
+        st = seg_at(info, ln + first_pos)
+        before = seg_at(info, sub * 0 + (first_pos - 1))
+        begin = seg_at(info, sub * 0 + first_pos)
+        last = seg_at(info, sub * 0 + (first_pos + BLOCK - 1))
+        after = seg_at(info, sub * 0 + (first_pos + BLOCK))
+        enter = jnp.where(fwdb, (sp == before).astype(F32), (sp == after).astype(F32))
+        keep = jnp.where(fwdb, (sp == last).astype(F32), (sp == begin).astype(F32))
+        ce = cmap[blk, :] * enter
+        bk = bmap[blk, :] * keep
+        ce_o[blk, :] = ce
+        bk_o[blk, :] = bk
+        cet_o[b] = ce.T
+        bkt_o[b] = bk.T
+        chain = jnp.where(fwdb[0:1, :], (last == before).astype(F32)[0:1, :], (begin == after).astype(F32)[0:1, :])
+        dvals.append(jnp.exp(end) * chain)
+        ends.append(end)
+        cb = cmap[blk, :].astype(BF16)
+        bb = bmap[blk, :].astype(BF16)
+        zero = jnp.zeros_like(bb)
+        same = sp == st
+        low = same & (sub > ln)
+        high = same & (sub < ln)
+        bf = jnp.where(fwdb, bb, zero)
+        br = jnp.where(fwdb, zero, bb)
+        g_o[b] = jnp.where(low, nt(cb, bf), jnp.where(high, nt(cb, br), 0.0))
+        gt_o[b] = jnp.where(high, nt(bf, cb), jnp.where(low, nt(br, cb), 0.0))
+    ones = jnp.ones((1, 128), F32)
+    prefix, suffix = [ones], [ones]
+    for b in range(nb):
+        prefix.append(prefix[-1] * dvals[b])
+        suffix.append(suffix[-1] * dvals[nb - 1 - b])
+    suffix = suffix[::-1]
+    f1 = fwdb[0:1, :]
+    for b in range(nb):
+        cum_s[b : b + 1, :] = dvals[b]
+        cum_s[48 + b : 49 + b, :] = ends[b]
+    for i in range(nb + 1):
+        cum_s[16 + i : 17 + i, :] = jnp.where(f1, prefix[i], suffix[i])
+        cum_s[32 + i : 33 + i, :] = jnp.where(f1, suffix[i], prefix[i])
+    dpt_o[...] = cum_s[...].T
+
+
+def pair_rows(dpt, j, base, i, half):
+    lane = iota((1, 128), 1)
+    one = dpt[pl.ds(half * 64 + 2 * j, 1), :][:, base + i : base + i + 1]
+    two = dpt[pl.ds(half * 64 + 2 * j + 1, 1), :][:, base + i : base + i + 1]
+    return jnp.where(lane < 64, one, two)
+
+
+def assemble(dst, pieces):
+    quarter = dst.shape[0] // 4
+    q = lax.axis_index("wide") % 4
+    cbit = q % 2
+    xbit = q // 2
+    places = (q, (1 - xbit) * 2 + cbit, xbit * 2 + 1 - cbit, (1 - xbit) * 2 + 1 - cbit)
+    for place, piece in zip(places, pieces):
+        dst[pl.ds(pl.multiple_of(place * quarter, quarter), quarter), :] = piece[...]
+
+
+def vals_kernel(
+    length, other, info, normed, *refs,
+):
+    nb = length // BLOCK
+    ext = length + 2 * HALO
+    j = pl.program_id(0)
+    step = j
+    if other:
+        p0, p1, p2, p3, taps, wt, bkt, dpt = refs[:8]
+        xc_o, vm_o, ds_o, s_o, bnd_o, wvo_o, vm_s, seg_s, wall_s = refs[13:]
+        j = j + pl.num_programs(0)
+
+        @pl.when(step == 0)
+        def _():
+            assemble(wvo_o, (p0, p1, p2, p3))
+            for i in range(wall_s.shape[0]):
+                wall_s[i] = wvo_o[:, i * 128 : (i + 1) * 128]
+
+        wv = wall_s[step]
+    else:
+        wv_ref, taps, wt, bkt, dpt, xc_o, vm_o, ds_o, s_o, bnd_o, vm_s, seg_s = refs
+        wv = wv_ref[...]
+    off, count = info[5], info[4]
+
+    @pl.when(step == 0)
+    def _():
+        seg_s[...] = seg_at(info, iota((ext, 128), 0) + (off - HALO))
+
+    live = iota((ext, 128), 0) + (off - HALO) < count
+    vm = jnp.where(live, mm(normed[...], wv), 0.0)
+    vm_s[...] = vm
+    vm_o[...] = vm.astype(BF16)
+    mix = conv_taps(vm_s, seg_s, taps, HALO, length)
+    act, ds = silu_parts(mix)
+    xc = act.astype(BF16)
+    xc_o[...] = xc
+    ds_o[...] = ds.astype(BF16)
+    lane = iota((BLOCK, 128), 1)
+    top = iota((BLOCK, 128), 0) < 64
+    loc = []
+    for b in range(nb):
+        blk = slice(b * BLOCK, (b + 1) * BLOCK)
+        got = []
+        for i in range(2):
+            h = 2 * j + i
+            w = jnp.where(top, wt[b, pl.ds(h, 1), :], wt[b, pl.ds(64 + h, 1), :])
+            got.append(mm((bkt[b] * w).astype(BF16), xc[blk, :]))
+        loc.append(jnp.where(lane < 64, got[0], got[1]))
+    state = jnp.zeros((64, 128), F32)
+    s_o[0, 0, 0:64, :] = state.astype(BF16)
+    for b in range(nb):
+        state = pair_rows(dpt, j, 0, b, 0) * state + loc[b][0:64, :]
+        s_o[0, b + 1, 0:64, :] = state.astype(BF16)
+    end_f = state
+    state = jnp.zeros((64, 128), F32)
+    s_o[0, nb, 64:128, :] = state.astype(BF16)
+    for b in range(nb - 1, -1, -1):
+        state = pair_rows(dpt, j, 0, b, 1) * state + loc[b][64:128, :]
+        s_o[0, b, 64:128, :] = state.astype(BF16)
+    bnd_o[0] = jnp.where(info[7] == 0, end_f, state).astype(BF16)
+
+
+def scan_kernel(length, info, xc_ref, s_ref, s0_ref, dpt, colt, rowst, ce, g, skip, y_o, st_o):
+    nb = length // BLOCK
+    j = pl.program_id(0)
+    right = (info[7] == 1).astype(F32)
+    s0 = s0_ref[0].astype(F32)
+    lane = iota((BLOCK, 128), 1)
+    first = lane < 64
+    low = iota((BLOCK, BLOCK), 0) > lane
+    for i in range(nb + 1):
+        f = s_ref[0, i, 0:64, :].astype(F32) + pair_rows(dpt, j, 16, i, 0) * (s0 * right)
+        r = s_ref[0, i, 64:128, :].astype(F32) + pair_rows(dpt, j, 16, i, 1) * (s0 * (1.0 - right))
+        st_o[0, i, 0:64, :] = f.astype(BF16)
+        st_o[0, i, 64:128, :] = r.astype(BF16)
+    for b in range(nb):
+        blk = slice(b * BLOCK, (b + 1) * BLOCK)
+        xb = xc_ref[blk, :]
+        rhs = jnp.concatenate([xb, st_o[0, b, 0:64, :], st_o[0, b + 1, 64:128, :]], axis=0)
+        got = []
+        for i in range(2):
+            h = 2 * j + i
+            mine = pltpu.roll(colt[blk, :], 128 - h, 1)
+            cf = jnp.broadcast_to(mine[:, 0:1], (BLOCK, 128))
+            cb = jnp.broadcast_to(mine[:, 64:65], (BLOCK, 128))
+            diff = jnp.where(low, cf + rowst[b, pl.ds(h, 1), :], cb + rowst[b, pl.ds(64 + h, 1), :])
+            mix = jnp.exp(jnp.minimum(diff, 60.0)) * g[b]
+            ct = ce[blk, :] * jnp.exp(jnp.where(first, cf, cb))
+            lhs = jnp.concatenate([mix.astype(BF16), ct.astype(BF16)], axis=1)
+            got.append(mm(lhs, rhs))
+        y = jnp.where(first, got[0], got[1]) + skip[0:1, :] * xb.astype(F32)
+        y_o[blk, :] = y.astype(BF16)
+
+
+def by_core(v, keep, send):
+    share = v.shape[0] // 16
+    cbit = lax.axis_index("wide") % 2
+    v = v.astype(BF16).reshape(8, 2, share, v.shape[1])
+    keep[...] = jnp.where(cbit == 0, v[:, 0], v[:, 1]).reshape(8 * share, v.shape[3])
+    send[...] = jnp.where(cbit == 0, v[:, 1], v[:, 0]).reshape(8 * share, v.shape[3])
+
+
+def gate_kernel(
+    tiles, x_ref, g_ref, normed, y_ref, wout_a, wg_a, p0, p1, p2, p3, gain,
+    out_o, gy_o, keep_o, send_o, ggate_o, ggain_o, wgo_o, hn_s, other_s,
+):
+    i = pl.program_id(0)
+    dm = x_ref.shape[1]
+
+    @pl.when(i == 0)
+    def _():
+        assemble(other_s, (p0, p1, p2, p3))
+        wgo_o[...] = other_s[:, dm:]
+
+    wout = (wout_a[...], other_s[:, 0:dm])
+
+    chans = y_ref.shape[1]
+    half = chans // 2
+    y = y_ref[...].astype(F32)
+    nrows = normed[pl.ds(pl.multiple_of(i * BLOCK + HALO, HALO), BLOCK), :]
+    gate = jnp.concatenate([mm(nrows, wg_a[...]), mm(nrows, other_s[:, dm:])], axis=1)
+    act, dact = silu_parts(gate)
+    gated = y * act
+    inv = lax.rsqrt(jnp.sum(gated * gated, axis=1, keepdims=True) * (1.0 / chans) + EPS)
+    nrm = gated * inv
+    gainv = gain[0:1, :]
+    hn = (nrm * gainv).astype(BF16)
+    rows = pl.ds(pl.multiple_of(i * BLOCK, BLOCK), BLOCK)
+    hn_s[rows, :] = hn
+    branch = mm(hn[:, 0:half], wout[0]) + mm(hn[:, half:], wout[1])
+    out_o[...] = (x_ref[rows, :].astype(F32) + branch).astype(BF16)
+    g = g_ref[rows, :]
+    ghn = jnp.concatenate([nt(g, wout[0]), nt(g, wout[1])], axis=1)
+
+    @pl.when(i == 0)
+    def _():
+        ggain_o[...] = jnp.zeros_like(ggain_o)
+
+    ggain_o[0:1, :] += jnp.sum(ghn * nrm, axis=0, keepdims=True)
+    wgt = ghn * gainv
+    cross = jnp.sum(wgt * gated, axis=1, keepdims=True) * (1.0 / chans)
+    ggated = inv * wgt - gated * (inv * inv * inv * cross)
+    gy_o[...] = (ggated * act).astype(BF16)
+    ggate_o[rows, :] = (ggated * y * dact).astype(BF16)
+
+    @pl.when(i == tiles - 1)
+    def _():
+        length = g_ref.shape[0]
+        gt = g_ref[...].T
+        nt_ = normed[HALO : HALO + length, :].T
+        for k in range(2):
+            for p in range(half // 256):
+                cols = slice(k * half + p * 256, k * half + (p + 1) * 256)
+                dst = slice(p * 256, (p + 1) * 256)
+                dst2 = slice(half + p * 256, half + (p + 1) * 256)
+                by_core(mm(gt, hn_s[:, cols]), keep_o.at[k, :, dst], send_o.at[k, :, dst])
+                by_core(mm(nt_, ggate_o[:, cols]), keep_o.at[k, :, dst2], send_o.at[k, :, dst2])
+
+
+def gstate_kernel(length, info, gy_ref, et, cet, dpt, gs_o, bnd_o):
+    nb = length // BLOCK
+    j = pl.program_id(0)
+    lane = iota((BLOCK, 128), 1)
+    top = iota((BLOCK, 128), 0) < 64
+    loc = []
+    for b in range(nb):
+        blk = slice(b * BLOCK, (b + 1) * BLOCK)
+        gy = gy_ref[blk, :]
+        got = []
+        for i in range(2):
+            h = 2 * j + i
+            e = jnp.where(top, et[b, pl.ds(h, 1), :], et[b, pl.ds(64 + h, 1), :])
+            got.append(mm((cet[b] * e).astype(BF16), gy))
+        loc.append(jnp.where(lane < 64, got[0], got[1]))
+    state = jnp.zeros((64, 128), F32)
+    gs_o[0, nb, 0:64, :] = state.astype(BF16)
+    for b in range(nb - 1, -1, -1):
+        state = pair_rows(dpt, j, 0, b, 0) * state + loc[b][0:64, :]
+        gs_o[0, b, 0:64, :] = state.astype(BF16)
+    end_f = state
+    state = jnp.zeros((64, 128), F32)
+    gs_o[0, 0, 64:128, :] = state.astype(BF16)
+    for b in range(nb):
+        state = pair_rows(dpt, j, 0, b, 1) * state + loc[b][64:128, :]
+        gs_o[0, b + 1, 64:128, :] = state.astype(BF16)
+    bnd_o[0] = jnp.where(info[7] == 1, end_f, state).astype(BF16)
+
+
+def gscan_kernel(
+    length, info, xc_ref, ds_ref, gy_ref, st_ref, gs_ref, gs0_ref, dpt, rows_ref, coltt, et, gt, bk, cet, skip,
+    gmix_o, ggt_o, gb_o, gct_o, k_o, r_o, phi_o, gskip_o, gst_s,
+):
+    nb = length // BLOCK
+    j = pl.program_id(0)
+    right = (info[7] == 1).astype(F32)
+    s0 = gs0_ref[0].astype(F32)
+    sub = iota((BLOCK, BLOCK), 0)
+    lane = iota((BLOCK, 128), 1)
+    first = lane < 64
+    later = lane > sub
+    top = sub < 64
+
+    @pl.when(j == 0)
+    def _():
+        ggt_o[...] = jnp.zeros_like(ggt_o)
+        gb_o[...] = jnp.zeros_like(gb_o)
+        gct_o[...] = jnp.zeros_like(gct_o)
+        k_o[...] = jnp.zeros_like(k_o)
+        r_o[...] = jnp.zeros_like(r_o)
+
+    phi_o[...] = jnp.zeros_like(phi_o)
+    for i in range(nb + 1):
+        f = gs_ref[0, i, 0:64, :].astype(F32) + pair_rows(dpt, j, 32, i, 0) * (s0 * (1.0 - right))
+        r = gs_ref[0, i, 64:128, :].astype(F32) + pair_rows(dpt, j, 32, i, 1) * (s0 * right)
+        f = f.astype(BF16)
+        r = r.astype(BF16)
+        gst_s[i, 0:64, :] = f
+        gst_s[i, 64:128, :] = r
+        if i > 0:
+            phi_o[i - 1 : i, :] = jnp.sum(f.astype(F32) * st_ref[0, i, 0:64, :].astype(F32), axis=0, keepdims=True)
+        if i < nb:
+            phi_o[8 + i : 9 + i, :] = jnp.sum(
+                r.astype(F32) * st_ref[0, i, 64:128, :].astype(F32), axis=0, keepdims=True
+            )
+    gskip = jnp.zeros((1, 128), F32)
+    for b in range(nb):
+        blk = slice(b * BLOCK, (b + 1) * BLOCK)
+        xb = xc_ref[blk, :]
+        gy = gy_ref[blk, :]
+        gyf = gy.astype(F32)
+        gskip = gskip + jnp.sum(gyf * xb.astype(F32), axis=0, keepdims=True)
+        rhs = jnp.concatenate([gy, gst_s[b + 1, 0:64, :], gst_s[b, 64:128, :]], axis=0)
+        left = jnp.concatenate([xb, st_ref[0, b, 0:64, :], st_ref[0, b + 1, 64:128, :]], axis=0)
+        lane2 = iota((2 * BLOCK, 128), 1)
+        got = []
+        for i in range(2):
+            h = 2 * j + i
+            mine = pltpu.roll(rows_ref[blk, :], 128 - h, 1)
+            cf = jnp.broadcast_to(mine[:, 0:1], (BLOCK, 128))
+            cb = jnp.broadcast_to(mine[:, 64:65], (BLOCK, 128))
+            diff = jnp.where(later, cf + coltt[b, pl.ds(h, 1), :], cb + coltt[b, pl.ds(64 + h, 1), :])
+            et_m = jnp.exp(jnp.minimum(diff, 60.0))
+            mt = et_m * gt[b]
+            endf = dpt[pl.ds(h, 1), :][:, 48 + b : 49 + b]
+            endb = dpt[pl.ds(64 + h, 1), :][:, 48 + b : 49 + b]
+            w = jnp.exp(jnp.minimum(jnp.where(first, cf + endf, cb + endb), 60.0))
+            bt = bk[blk, :] * w
+            lhs_b = jnp.where((lane2 < 64) == (i == 0), left, jnp.zeros_like(left))
+            big = nt(lhs_b, rhs)
+            gmt = big[0:BLOCK, 0:BLOCK]
+            gbt = big[0:BLOCK, BLOCK:]
+            gctt = big[BLOCK:, 0:BLOCK]
+            ge = gmt * et_m
+            ggt_o[b] += ge
+            q = gmt * mt
+            qf = jnp.where(later, q, 0.0)
+            qb = q - qf
+            e = jnp.where(top, et[b, pl.ds(h, 1), :], et[b, pl.ds(64 + h, 1), :])
+            gce = gctt * e
+            gct_o[b] += gce
+            ct = gce * cet[b]
+            r_o[b, pl.ds(h, 1), :] = jnp.sum(qf, axis=0, keepdims=True) + jnp.sum(ct[0:64, :], axis=0, keepdims=True)
+            r_o[b, pl.ds(64 + h, 1), :] = jnp.sum(qb, axis=0, keepdims=True) + jnp.sum(
+                ct[64:128, :], axis=0, keepdims=True
+            )
+            gb_o[b] += gbt * w
+            u = gbt * bt
+            kf = jnp.sum(qf + jnp.where(first, u, 0.0), axis=1, keepdims=True)
+            kb = jnp.sum(qb + jnp.where(first, 0.0, u), axis=1, keepdims=True)
+            k_o[blk, :] += jnp.where(lane == h, kf, jnp.where(lane == 64 + h, kb, 0.0))
+            lhs = jnp.concatenate([mt.astype(BF16), bt.astype(BF16)], axis=1)
+            got.append(mm(lhs, rhs))
+        gx = jnp.where(first, got[0], got[1]) + skip[0:1, :] * gyf
+        gmix_o[blk, :] = (gx * ds_ref[blk, :].astype(F32)).astype(BF16)
+    gskip_o[...] = jnp.broadcast_to(gskip, (8, 128))
+
+
+def join_kernel(
+    length, heads, info, ggt, gb, gct, k_ref, r_ref, phi, b_ref, c_ref, bk, dsl, a_ref, sig,
+    gmb_o, gv_o, small_o, gc_s, gm_s,
+):
+    nb = length // BLOCK
+    off = info[5]
+    chans = phi.shape[1]
+    sub = iota((BLOCK, BLOCK), 0)
+    lane = iota((BLOCK, 128), 1)
+    first = lane < 64
+    low = sub > lane
+    high = sub < lane
+    upper_strict = high.astype(F32)
+    upper = (sub <= lane).astype(F32)
+    lower_strict = low.astype(F32)
+    lower = (sub >= lane).astype(F32)
+    owner = iota((chans, 128), 0) // 64
+    to_f = (owner == iota((chans, 128), 1)).astype(F32)
+    to_b = (owner + 64 == iota((chans, 128), 1)).astype(F32)
+    phi_f = mm(phi[0:8, :], to_f, precision=HIGH)
+    phi_b = mm(phi[8:16, :], to_b, precision=HIGH)
+    gc_s[...] = jnp.zeros_like(gc_s)
+    gm_s[...] = jnp.zeros_like(gm_s)
+    sum_bias = jnp.zeros((1, 128), F32)
+    sum_rate = jnp.zeros((1, 128), F32)
+    for b in range(nb):
+        blk = slice(b * BLOCK, (b + 1) * BLOCK)
+        ext = slice(HALO + b * BLOCK, HALO + (b + 1) * BLOCK)
+        first_pos = off + b * BLOCK
+        sp = seg_at(info, sub + first_pos)
+        st = seg_at(info, lane + first_pos)
+        before = seg_at(info, sub * 0 + (first_pos - 1))
+        begin = seg_at(info, sub * 0 + first_pos)
+        last = seg_at(info, sub * 0 + (first_pos + BLOCK - 1))
+        after = seg_at(info, sub * 0 + (first_pos + BLOCK))
+        enter = jnp.where(first, (sp == before).astype(F32), (sp == after).astype(F32))
+        keep = jnp.where(first, (sp == last).astype(F32), (sp == begin).astype(F32))
+        same = sp == st
+        gg = ggt[b]
+        gf = jnp.where(same & high, gg, 0.0).astype(BF16)
+        gr = jnp.where(same & low, gg, 0.0).astype(BF16)
+        cm = c_ref[blk, :]
+        bm = b_ref[blk, :]
+        gm_s[ext, 0:128] = jnp.where(first, mm(gf, cm), mm(gr, cm)) + gb[b] * keep
+        gc_s[ext, :] = jnp.where(first, tn(gf, bm), tn(gr, bm)) + gct[b].T * enter
+        kb = k_ref[blk, :]
+        rb = r_ref[b].T
+        ga_f = mm(upper_strict, rb, precision=HIGH) - mm(upper, kb, precision=HIGH) + phi_f[b : b + 1, :]
+        ga_b = mm(lower_strict, rb, precision=HIGH) - mm(lower, kb, precision=HIGH) + phi_b[b : b + 1, :]
+        ga = jnp.where(first, ga_f, ga_b)
+        gv = kb * sig[blk, 128:256] + ga * sig[blk, 0:128]
+        gv_o[blk, :] = gv.astype(BF16)
+        sum_bias = sum_bias + jnp.sum(gv, axis=0, keepdims=True)
+        sum_rate = sum_rate + jnp.sum(ga * a_ref[blk, :], axis=0, keepdims=True)
+    small_o[...] = jnp.zeros_like(small_o)
+    small_o[0:1, :] = sum_bias
+    small_o[1:2, :] = sum_rate
+    small_o[8:9, :] = pltpu.roll(sum_bias, 128 - heads // 2, 1)
+    small_o[9:10, :] = pltpu.roll(sum_rate, 128 - heads // 2, 1)
+    mid = length + HALO
+    lo = HALO // 2
+    pos = iota((mid, 128), 0) + (off - HALO + lo)
+    seg0 = seg_at(info, pos)
+    segn = seg_at(info, pos + 1)
+    segp = seg_at(info, pos - 1)
+    from_next = jnp.where(seg0 == segn, gc_s[lo + 1 : lo + 1 + mid, :], 0.0)
+    from_prev = jnp.where(seg0 == segp, gc_s[lo - 1 : lo - 1 + mid, :], 0.0)
+    gm_s[lo : lo + mid, 128:256] = jnp.where(iota((mid, 128), 1) < 64, from_next, from_prev)
+    gmb_o[...] = gm_s[...] * dsl[...]
+
+
+def back_kernel(
+    length, steps, info, gmix, edge, vm, wv_a, wg_a, wv_b, wg_b, ggate, normed, taps, gmb, edge_bc, bcm, taps_bc, gv, wdt, wbc, x_ref, g_ref, rs, pre,
+    keep_o, send_o, gtaps_o, keepbc_o, sendbc_o, gtapsbc_o, gin_o, gpre_o, acc_s, ext_s, vm_s, seg_s,
+):
+    j = pl.program_id(0)
+    ext = length + 2 * HALO
+    off, count = info[5], info[4]
+    own = slice(HALO, HALO + length)
+
+    @pl.when(j == 0)
+    def _():
+        seg_s[...] = seg_at(info, iota((ext, 128), 0) + (off - HALO))
+        ext_s[...] = jnp.zeros_like(ext_s)
+
+    seg0 = seg_s[own, :]
+    live = iota((length, 128), 0) + off < count
+
+    def back_conv(grad, data, tap, gtap):
+        total = grad[own, :] * tap[3:4, :]
+        mine = grad[own, :]
+        gtap[3:4, :] = jnp.sum(mine * data[own, :], axis=0, keepdims=True)
+        for k in (0, 1, 2, 4, 5, 6):
+            lo = HALO + 3 - k
+            same = seg_s[lo : lo + length, :] == seg0
+            total = total + jnp.where(same, grad[lo : lo + length, :], 0.0) * tap[k : k + 1, :]
+            up = HALO + k - 3
+            same = seg_s[up : up + length, :] == seg0
+            gtap[k : k + 1, :] = jnp.sum(
+                jnp.where(same, data[up : up + length, :], 0.0) * mine, axis=0, keepdims=True
+            )
+        gtap[7:8, :] = jnp.zeros((1, 128), F32)
+        return jnp.where(live, total, 0.0)
+
+    @pl.when(j == 0)
+    def _():
+        no = normed[own, :]
+        both = []
+        for k in range(2):
+            cols = slice(k * 128, (k + 1) * 128)
+            ext_s[...] = gmb[:, cols]
+            lo = HALO // 2
+            hi = length + lo
+            got = edge_bc[:, cols]
+            ext_s[lo : lo + HALO, :] += jnp.where(info[7] == 1, got, 0.0)
+            ext_s[hi : hi + HALO, :] += jnp.where(info[7] == 1, 0.0, got)
+            vm_s[...] = bcm[:, cols]
+            gbc = back_conv(ext_s, vm_s, taps_bc.at[:, cols], gtapsbc_o.at[:, cols])
+            both.append(gbc.astype(BF16))
+        gbc = jnp.concatenate(both + [gv[...]], axis=1)
+        gw = tn(no, gbc)
+        by_core(gw, keepbc_o.at[0], sendbc_o.at[0])
+        turned = pltpu.roll(gw[:, 256:], 128 - steps, 1)
+        by_core(jnp.concatenate([gw[:, 0:256], turned], axis=1), keepbc_o.at[1], sendbc_o.at[1])
+        acc_s[...] = nt(gbc[:, 0:256], wbc[...]) + nt(gv[...], wdt[...])
+
+    ext_s[own, :] = gmix[...].astype(F32)
+    halo = edge[...].astype(F32)
+    right = info[7] == 1
+    ext_s[0:HALO, :] = jnp.where(right, halo, 0.0)
+    ext_s[HALO + length : ext, :] = jnp.where(right, 0.0, halo)
+    vm_s[...] = vm[...].astype(F32)
+    gvals = back_conv(ext_s, vm_s, taps, gtaps_o).astype(BF16)
+    by_core(tn(normed[own, :], gvals), keep_o.at[0], send_o.at[0])
+    both = jnp.concatenate([gvals, ggate[...]], axis=1)
+    mine = j < steps // 2
+    weights = jnp.concatenate(
+        [jnp.where(mine, wv_a[...], wv_b[...]), jnp.where(mine, wg_a[...], wg_b[...])], axis=1
+    )
+    acc_s[...] += nt(both, weights)
+
+    @pl.when(j == steps - 1)
+    def _():
+        x = x_ref[...].astype(F32)
+        gn = acc_s[...]
+        r = rs[...]
+        wp = gn * pre[...]
+        mean = jnp.mean(wp * x, axis=1, keepdims=True)
+        gin_o[...] = g_ref[...].astype(F32) + r * wp - x * (r * r * r * mean)
+        gpre_o[...] = jnp.broadcast_to(jnp.sum(gn * x * r, axis=0, keepdims=True), gpre_o.shape)
+
+
+def whole(shape, grid):
+    zeros = (0,) * len(shape)
+    if grid:
+        return pl.BlockSpec(shape, lambda j: zeros)
+    return pl.BlockSpec(shape, lambda: zeros)
+
+
+def columns(rows, first=0):
+    return pl.BlockSpec((rows, 128), lambda j: (0, first + j))
+
+
+SMEM = pl.BlockSpec(memory_space=pltpu.SMEM)
+VMEM = pl.BlockSpec(memory_space=pltpu.VMEM)
+ANY = pl.BlockSpec(memory_space=pl.ANY)
+
+
+def sds(shape, dtype):
+    return jax.ShapeDtypeStruct(shape, dtype)
+
+
+def params(grid):
+    if grid:
+        return pltpu.CompilerParams(vmem_limit_bytes=VMEM_LIMIT, dimension_semantics=("arbitrary",))
+    return pltpu.CompilerParams(vmem_limit_bytes=VMEM_LIMIT)
+
+
+def cost(us):
+    return pl.CostEstimate(flops=int(us * 1.1e9), bytes_accessed=int(us * 1e6), transcendentals=0)
+
+
+def pack_columns(v):
+    n = v.shape[-1] // 4
+    return jnp.concatenate([v[..., 0:n], v[..., 2 * n : 3 * n], v[..., n : 2 * n], v[..., 3 * n :]], axis=-1)
+
+
+def small_kernel(hl, conv, gain, dtb, alog, skip, out_o):
+    ch = out_o.shape[1]
+    out_o[...] = jnp.zeros_like(out_o)
+    lane = iota((1, 128), 1)
+    wide_lane = iota((1, ch), 1)
+    bias = jnp.zeros((1, 128), F32)
+    rate = jnp.zeros((1, 128), F32)
+    diag = jnp.zeros((1, ch), F32)
+    for h in range(hl):
+        cols = slice(h * HD, (h + 1) * HD)
+        out_o[0:7, cols] = conv[:, h, :]
+        out_o[8:9, cols] = gain[h : h + 1, :]
+        bias = jnp.where(lane == h, dtb[h, 0], jnp.where(lane == 64 + h, dtb[h, 1], bias))
+        rate = jnp.where((lane == h) | (lane == 64 + h), alog[h], rate)
+        diag = jnp.where(wide_lane // HD == h, skip[h], diag)
+    out_o[16:17, :] = diag
+    out_o[24:25, 0:128] = bias
+    out_o[25:26, 0:128] = rate
+
+
+def swap(v):
+    return lax.ppermute(v, "narrow", [(0, 1), (1, 0)])
+
+
+def flip(v, bit, wide):
+    return lax.ppermute(v, "wide", [(i, i ^ bit) for i in range(wide)])
+
+
+def cross(v, bit, wide):
+    pairs = [(i * 2 + k, (i ^ bit) * 2 + 1 - k) for i in range(wide) for k in range(2)]
+    return lax.ppermute(v, ("wide", "narrow"), pairs)
+
+
+def pick(v, dim, index):
+    return lax.dynamic_index_in_dim(v, index, dim, keepdims=False)
+
+
+def total(*parts):
+    acc = parts[0].astype(F32)
+    for v in parts[1:]:
+        acc = acc + v.astype(F32)
+    return acc
+
+
+def split_positions(
+    wide, layer_in, pre_gain, w_heads, w_bc, conv_x, conv_bc, dt_bias, a_log, skip_d, norm_gain, w_out, cotangent, starts, live
+):
+    n = lax.axis_index("narrow")
+    w = lax.axis_index("wide")
+    left = n == 0
+    _, length, dm = layer_in.shape
+    hl = w_heads.shape[1]
+    heads = 2 * hl
+    ch = hl * HD
+    chans = 2 * ch
+    pairs = heads // 2
+    hp = pairs // 2
+    nb = length // BLOCK
+    ext = length + 2 * HALO
+    share = dm // wide
+    x = layer_in[0]
+    g = cotangent[0]
+    xbit = (w // 2) % 2
+    zbits = w // 4
+
+    edge = swap(jnp.where(left, x[length - HALO :], x[:HALO]))
+    small_own = pl.pallas_call(
+        functools.partial(small_kernel, hl),
+        out_shape=sds((32, ch), F32),
+        in_specs=[VMEM, VMEM, SMEM, SMEM, SMEM],
+        out_specs=VMEM,
+        name="small",
+    )(conv_x, norm_gain, dt_bias, a_log, skip_d)
+    small_other = swap(small_own)
+    wdt = w_heads[:, :, 2 * HD :].reshape(dm, 2 * hl)
+    wdt_other = swap(wdt)
+
+    quarter = dm // 4
+    q = w % 4
+
+    def gather(own):
+        p0 = swap(lax.dynamic_slice(own, (q * quarter, 0), (quarter, own.shape[1])))
+        p1 = flip(p0, 2, wide)
+        return p0, p1, flip(p0, 1, wide), flip(p1, 1, wide)
+
+    wv = w_heads[:, :, HD : 2 * HD].reshape(dm, ch)
+    wg = w_heads[:, :, :HD].reshape(dm, ch)
+    wo = w_out.reshape(ch, dm)
+    wv_pieces = gather(wv)
+    wog_pieces = gather(jnp.concatenate([wo, wg], axis=1))
+
+    pos = (length, 128)
+    sq = (nb, BLOCK, BLOCK)
+    front_shapes = [
+        ((8, chans), F32), ((8, chans), F32), ((8, chans), F32), ((dm, 128), BF16), ((dm, 256), BF16), ((7, 256), F32),
+        ((ext, dm), BF16), ((length, 1), F32), ((ext, 256), F32), ((ext, 256), F32), (pos, BF16), (pos, F32), (sq, F32),
+        (pos, BF16), (pos, F32), (sq, F32), (sq, F32), (sq, F32), (pos, F32), (pos, F32), (sq, F32), (sq, F32),
+        (sq, F32), (sq, F32), ((128, 128), F32), (pos, F32), ((length, 256), F32),
+    ]
+    (
+        info, taps, gain, skip, wdt_all, wbc, taps_bc, normed, rs, bcm, dsl, bmap, bk, bkt, cmap, ce, cet, gmat, gmat_t,
+        colt, rows, coltt, rowst, et, wt, dpt, a_dt, sig,
+    ) = pl.pallas_call(
+        functools.partial(front_kernel, length, hl),
+        out_shape=[sds((8,), jnp.int32)] + [sds(*v) for v in front_shapes],
+        in_specs=[SMEM] + [VMEM] * 10,
+        out_specs=[SMEM] + [VMEM] * len(front_shapes),
+        scratch_shapes=[
+            pltpu.VMEM((ext, 256), jnp.int32), pltpu.VMEM((ext, 256), F32), pltpu.VMEM((128, 128), F32),
+            pltpu.VMEM((ext, dm), BF16),
+        ],
+        compiler_params=params(False),
+        cost_estimate=cost(8),
+        name="front",
+    )(starts, live, x, edge, pre_gain.reshape(1, dm), wdt, wdt_other, w_bc, conv_bc, small_own, small_other)
+
+    state_spec = pl.BlockSpec((1, nb + 1, 128, 128), lambda j: (j, 0, 0, 0))
+    bnd_spec = pl.BlockSpec((1, 64, 128), lambda j: (j, 0, 0))
+    far_spec = pl.BlockSpec((1, 64, 128), lambda j: ((j + hp) % pairs, 0, 0))
+    state_shape = sds((pairs, nb + 1, 128, 128), BF16)
+    bnd_shape = sds((pairs, 64, 128), BF16)
+    act_shape = sds((length, chans), BF16)
+    own_spec = pl.BlockSpec((dm, 128), lambda j: (0, jnp.minimum(j, hp - 1)))
+    other_spec = pl.BlockSpec((dm, 128), lambda j: (0, jnp.maximum(j - hp, 0)))
+
+    def vals(other, weights, before):
+        first = hp if other else 0
+        extra = [sds((dm, ch), BF16)] if other else []
+        specs = [SMEM, whole((ext, dm), 1)]
+        if other:
+            specs += [whole((quarter, ch), 1)] * 4
+        else:
+            specs += [columns(dm)]
+        specs += [columns(8, first), whole(sq, 1), whole(sq, 1), whole((128, 128), 1)] + [ANY] * len(before)
+        scratch = [pltpu.VMEM((ext, 128), F32), pltpu.VMEM((ext, 128), jnp.int32)]
+        if other:
+            scratch.append(pltpu.VMEM((hp, dm, 128), BF16))
+        return pl.pallas_call(
+            functools.partial(vals_kernel, length, other),
+            grid=(hp,),
+            out_shape=[act_shape, sds((ext, chans), BF16), act_shape, state_shape, bnd_shape] + extra,
+            in_specs=specs,
+            out_specs=[
+                columns(length, first), columns(ext, first), columns(length, first),
+                pl.BlockSpec((1, nb + 1, 128, 128), lambda j: (j + first, 0, 0, 0)),
+                pl.BlockSpec((1, 64, 128), lambda j: (j + first, 0, 0)),
+            ] + [whole((dm, ch), 1)] * other,
+            scratch_shapes=scratch,
+            input_output_aliases={len(specs) - len(before) + i: i for i in range(len(before))},
+            compiler_params=params(True),
+            cost_estimate=cost(8),
+            name="vals_other" if other else "vals_own",
+        )(info, normed, *weights, taps, wt, bkt, dpt, *before)
+
+    own_vals = vals(False, (wv,), ())
+    xc, vm, ds, s_loc, bnd, wv_other = vals(True, wv_pieces, own_vals)
+
+    y, s_true = pl.pallas_call(
+        functools.partial(scan_kernel, length),
+        grid=(pairs,),
+        out_shape=[act_shape, state_shape],
+        in_specs=[
+            SMEM, columns(length), state_spec, far_spec, whole((128, 128), 1), whole(pos, 1), whole(sq, 1), whole(pos, 1),
+            whole(sq, 1), columns(8),
+        ],
+        out_specs=[columns(length), state_spec],
+        compiler_params=params(True),
+        cost_estimate=cost(19),
+        name="scan",
+    )(info, xc, s_loc, swap(bnd), dpt, colt, rowst, ce, gmat, skip)
+
+    tile_spec = pl.BlockSpec((BLOCK, chans), lambda i: (i, 0))
+    gw_shape = (2, dm // 2, dm + ch)
+    out, gy, keep_a, send_a, ggate, ggain, wg_other = pl.pallas_call(
+        functools.partial(gate_kernel, nb),
+        grid=(nb,),
+        out_shape=[
+            sds((length, dm), BF16), act_shape, sds(gw_shape, BF16), sds(gw_shape, BF16), act_shape, sds((8, chans), F32),
+            sds((dm, ch), BF16),
+        ],
+        in_specs=[
+            whole((length, dm), 1), whole((length, dm), 1), whole((ext, dm), 1), tile_spec, whole((ch, dm), 1),
+            whole((dm, ch), 1),
+        ] + [whole((quarter, dm + ch), 1)] * 4 + [whole((8, chans), 1)],
+        out_specs=[
+            pl.BlockSpec((BLOCK, dm), lambda i: (i, 0)), tile_spec, whole(gw_shape, 1), whole(gw_shape, 1),
+            whole((length, chans), 1), whole((8, chans), 1), whole((dm, ch), 1),
+        ],
+        scratch_shapes=[pltpu.VMEM((length, chans), BF16), pltpu.VMEM((dm, dm + ch), BF16)],
+        compiler_params=params(True),
+        cost_estimate=cost(22),
+        name="gated",
+    )(x, g, normed, y, wo, wg, *wog_pieces, gain)
+
+    def meet(keep, got):
+        cols = keep.shape[-1]
+        keep = keep.reshape(2, wide // 4, 2, share, cols)
+        got = got.reshape(2, wide // 4, 2, share, cols)
+
+        def piece(half, xx):
+            return total(pick(keep[half], 1, xx), pick(got[half], 1, xx)).astype(BF16)
+
+        return piece(0, xbit), piece(0, 1 - xbit), piece(1, xbit), piece(1, 1 - xbit)
+
+    def plane(mine, to_x, to_y, to_d):
+        return total(mine, flip(to_x, 2, wide), swap(to_y), cross(to_d, 2, wide)).astype(mine.dtype)
+
+    def depth(v):
+        parts = [pick(v, 0, zbits)]
+        for k in (1, 2, 3):
+            parts.append(flip(pick(v, 0, zbits ^ k), 4 * k, wide))
+        return total(*parts)
+
+    a_pieces = meet(keep_a, flip(send_a, 1, wide))
+
+    gs_loc, gbnd = pl.pallas_call(
+        functools.partial(gstate_kernel, length),
+        grid=(pairs,),
+        out_shape=[state_shape, bnd_shape],
+        in_specs=[SMEM, columns(length), whole(sq, 1), whole(sq, 1), whole((128, 128), 1)],
+        out_specs=[state_spec, bnd_spec],
+        compiler_params=params(True),
+        cost_estimate=cost(9),
+        name="gstate",
+    )(info, gy, et, cet, dpt)
+
+    gs_loc, gbnd, *a_pieces = lax.optimization_barrier((gs_loc, gbnd, *a_pieces))
+    a_plane = plane(*a_pieces)
+
+    gmix, ggt, gb, gct, ksum, rsum, phi, gskip = pl.pallas_call(
+        functools.partial(gscan_kernel, length),
+        grid=(pairs,),
+        out_shape=[
+            act_shape, sds(sq, F32), sds(sq, F32), sds(sq, F32), sds(pos, F32), sds(sq, F32), sds((16, chans), F32),
+            sds((8, chans), F32),
+        ],
+        in_specs=[
+            SMEM, columns(length), columns(length), columns(length), state_spec, state_spec, far_spec, whole((128, 128), 1),
+            whole(pos, 1), whole(sq, 1), whole(sq, 1), whole(sq, 1), whole(pos, 1), whole(sq, 1), columns(8),
+        ],
+        out_specs=[
+            columns(length), whole(sq, 1), whole(sq, 1), whole(sq, 1), whole(pos, 1), whole(sq, 1), columns(16), columns(8),
+        ],
+        scratch_shapes=[pltpu.VMEM((nb + 1, 128, 128), BF16)],
+        compiler_params=params(True),
+        cost_estimate=cost(35),
+        name="gscan",
+    )(info, xc, ds, gy, s_true, gs_loc, swap(gbnd), dpt, rows, coltt, et, gmat_t, bk, cet, skip)
+
+    gmix, ggt, a_plane = lax.optimization_barrier((gmix, ggt, a_plane))
+    wa = depth(a_plane)
+    edge_x = swap(jnp.where(left, gmix[length - HALO :], gmix[:HALO]))
+
+    gmb, gv, small = pl.pallas_call(
+        functools.partial(join_kernel, length, heads),
+        out_shape=[sds((ext, 256), F32), sds(pos, BF16), sds((16, 128), F32)],
+        in_specs=[SMEM] + [VMEM] * 12,
+        out_specs=[VMEM] * 3,
+        scratch_shapes=[pltpu.VMEM((ext, 128), F32), pltpu.VMEM((ext, 256), F32)],
+        compiler_params=params(False),
+        cost_estimate=cost(6),
+        name="join",
+    )(info, ggt, gb, gct, ksum, rsum, phi, bmap, cmap, bk, dsl, a_dt, sig)
+
+    lo = HALO // 2
+    edge_bc = swap(jnp.where(left, gmb[length + lo : length + lo + HALO], gmb[lo : lo + HALO]))
+
+    keep_b, send_b, gtaps, keep_bc, send_bc, gtaps_bc, grad_in, gpre = pl.pallas_call(
+        functools.partial(back_kernel, length, pairs),
+        grid=(pairs,),
+        out_shape=[
+            sds((2, dm // 2, ch), BF16), sds((2, dm // 2, ch), BF16), sds((8, chans), F32), sds((2, dm // 2, 384), BF16),
+            sds((2, dm // 2, 384), BF16), sds((8, 256), F32), sds((length, dm), F32), sds((8, dm), F32),
+        ],
+        in_specs=[
+            SMEM, columns(length), pl.BlockSpec((HALO, 128), lambda j: (0, (j + hp) % pairs)), columns(ext), own_spec, own_spec,
+            other_spec, other_spec, columns(length), whole((ext, dm), 1), columns(8), whole((ext, 256), 1),
+            whole((HALO, 256), 1), whole((ext, 256), 1), whole((7, 256), 1), whole(pos, 1), whole((dm, 128), 1),
+            whole((dm, 256), 1), whole((length, dm), 1), whole((length, dm), 1), whole((length, 1), 1), whole((1, dm), 1),
+        ],
+        out_specs=[
+            pl.BlockSpec((1, dm // 2, 128), lambda j: (j // hp, 0, j % hp)),
+            pl.BlockSpec((1, dm // 2, 128), lambda j: (j // hp, 0, j % hp)), columns(8), whole((2, dm // 2, 384), 1),
+            whole((2, dm // 2, 384), 1), whole((8, 256), 1), whole((length, dm), 1), whole((8, dm), 1),
+        ],
+        scratch_shapes=[
+            pltpu.VMEM((length, dm), F32), pltpu.VMEM((ext, 128), F32), pltpu.VMEM((ext, 128), F32),
+            pltpu.VMEM((ext, 128), jnp.int32),
+        ],
+        compiler_params=params(True),
+        cost_estimate=cost(24),
+        name="back",
+    )(
+        info, gmix, edge_x, vm, wv, wg, wv_other, wg_other, ggate, normed, taps, gmb, edge_bc, bcm, taps_bc, gv, wdt_all, wbc,
+        x, g, rs, pre_gain.reshape(1, dm),
+    )
+
+    keep_b, send_b, wa = lax.optimization_barrier((keep_b, send_b, wa))
+
+    keep_bb = jnp.concatenate([keep_b, keep_bc], axis=2)
+    send_bb = jnp.concatenate([send_b, send_bc], axis=2)
+    wb = depth(plane(*meet(keep_bb, flip(send_bb, 1, wide))))
+
+    small = jnp.pad(small, ((0, 0), (0, ch - 128)))
+    common = jnp.concatenate([gpre, jnp.pad(gtaps_bc, ((0, 0), (0, dm - 256)))], axis=0)
+    own_rows = jnp.concatenate([gtaps[:, :ch], ggain[:, :ch], gskip[:, :ch], small[:8], common], axis=0)
+    far_rows = jnp.concatenate([gtaps[:, ch:], ggain[:, ch:], gskip[:, ch:], small[8:], common], axis=0)
+    tiny = jnp.stack([own_rows, far_rows])
+    tiny = tiny + flip(tiny, 1, wide)
+    tiny = plane(tiny[0], tiny[0], tiny[1], tiny[1])
+    tiny = total(tiny, *[flip(tiny, 4 * k, wide) for k in (1, 2, 3)])
+
+    def part(v, dim):
+        size = v.shape[dim] // wide
+        return lax.dynamic_slice_in_dim(v, w * size, size, dim)
+
+    gate_part = wa[:, dm:].reshape(share, hl, HD)
+    vals_part = wb[:, :ch].reshape(share, hl, HD)
+    bc_part = pack_columns(wb[:, ch : ch + 256])
+    dt_cols = wb[:, ch + 256 :]
+    dt_part = jnp.stack([dt_cols[:, 0:hl], dt_cols[:, 64 : 64 + hl]], axis=2)
+    g_w_heads = jnp.concatenate([gate_part, vals_part, dt_part], axis=2)
+    g_w_out = jnp.transpose(wa[:, :dm].reshape(share, hl, HD), (1, 2, 0))
+    return (
+        out[None],
+        grad_in[None],
+        part(tiny[32], 0),
+        g_w_heads,
+        bc_part,
+        part(tiny[0:7].reshape(7, hl, HD), 2),
+        part(pack_columns(tiny[40:47, :256]), 1),
+        jnp.stack([tiny[24, 0:hl], tiny[24, 64 : 64 + hl]], axis=1),
+        tiny[25, 0:hl] + tiny[25, 64 : 64 + hl],
+        jnp.sum(tiny[16].reshape(hl, HD), axis=1),
+        part(tiny[8].reshape(hl, HD), 1),
+        g_w_out,
+    )
+
+
 def solution(mesh):
+    body = shards
+    if mesh.shape["narrow"] == 2 and mesh.shape["wide"] == 16:
+        body = functools.partial(split_positions, mesh.shape["wide"])
     return jax.shard_map(
-        shards,
+        body,
         mesh=mesh,
         in_specs=(
             P("wide", "narrow", None),

time: 1360 us -> 285 us (0.21); the launches traced: 1340 us -> 283 us
  waiting for transfers between devices: 332 us -> 39.2 us
  other arithmetic: 296 us -> 13.5 us
  matrix products: 275 us -> 0 us
  local copies, waits for them, and re-layouts: 310 us -> 37.5 us
  Pallas kernels: 0 us -> 149 us
  blocking collectives: 81.4 us -> 0 us
  starting transfers between devices: 1.13 us -> 42.8 us
  loops' own time: 27.1 us -> 0 us
  between operations: 17.9 us -> 1.27 us
    reduce_scatter x6 -> x0, waiting for transfers between devices: 310 us -> none  [the longest x1 115 us: shards(): lax.psum_scatter(g_w_heads, 'wide', scatter_dimension=0, tiled=True)]
    dot_general x33 -> x0, matrix products: 275 us -> none  [the longest x6 108 us: ssd_forward(): intra = jnp.einsum('rbtsh,rbshp->rbthp', mix, xb, precision=prec)]
    pallas_call x0 -> x10, Pallas kernels: none -> 149 us  [the longest x1 35.6 us: split_positions(): pl.pallas_call(functools.partial(gscan_kernel, length), grid=(pairs,), ou...]
    reduce_sum x32 -> x1, other arithmetic: 76.5 us -> 0.63 us  [split_positions(): jnp.sum(tiny[16].reshape(hl, HD), axis=1)]
    dynamic_update_slice x80 -> x0, other arithmetic: 73.4 us -> none  [ssd_forward(): _, (before, seg_before) = lax.scan(carry_step, init, items)]
    unnamed x1 -> x0, blocking collectives: 61.4 us -> none
    rev x11 -> x0, local copies, waits for them, and re-layouts: 61 us -> none  [flip(): return jnp.flip(v, axis=1)]
    mul x38 -> x0, other arithmetic: 53.6 us -> none  [the longest x3 13.3 us: conv_doc(): taps[offset] * padded[:, offset:offset + length] * same[:, :, None]]
  transfers between devices with their start and end apart: 9 -> 36, of which waited for: 6 -> 9; matrix products, arithmetic and copies ran while one was open for 31% -> 13% of each run, Pallas kernels for 0% -> 42%
where the time goes in v1:
time: 285 us; the launch traced here: 283 us
  Pallas kernels  149 us (52%)
  starting transfers between devices  42.8 us (15%)
  waiting for transfers between devices  39.2 us (14%)
  local copies, waits for them, and re-layouts  37.5 us (13%)
  other arithmetic  13.5 us (5%)
    pallas_call x1, Pallas kernels, split_positions(): pl.pallas_call(functools.partial(gscan_kernel, length), grid=(pairs,), ou...  35.6 us
    ppermute x21, waiting for transfers between devices, flip(): return lax.ppermute(v, 'wide', [(i, i ^ bit) for i in range(wide)])  26.3 us
    pallas_call x1, Pallas kernels, split_positions(): pl.pallas_call(functools.partial(back_kernel, length, pairs), grid=(pairs...  24.9 us
    pallas_call x1, Pallas kernels, split_positions(): pl.pallas_call(functools.partial(gate_kernel, nb), grid=(nb,), out_shape=...  24.1 us
    ppermute x21, starting transfers between devices, flip(): return lax.ppermute(v, 'wide', [(i, i ^ bit) for i in range(wide)])  22.7 us
    pallas_call x1, Pallas kernels, split_positions(): pl.pallas_call(functools.partial(scan_kernel, length), grid=(pairs,), out...  19.7 us
    pallas_call x2, Pallas kernels, vals(): pl.pallas_call(functools.partial(vals_kernel, length, other), grid=(hp,),...  18.6 us
    ppermute x12, starting transfers between devices, swap(): return lax.ppermute(v, 'narrow', [(0, 1), (1, 0)])  15.8 us
  transfers between devices with their start and end apart: 36, of which 9 were waited for; matrix products, arithmetic and copies ran while one was open for 13% of the time, Pallas kernels for 42%

profile of v1, /device:TPU:0, one launch (start us, length us, event | category | flops | bytes accessed | tf_op | source)
XLA Modules:
  0.0 283.2 jit_solution(2398493775577760621)
XLA Ops:
  0.7 1.8 fusion.22
  3.1 0.8 constant_dynamic-slice_fusion.7
  4.0 3.0 %collective-permute-start.3 = (bf16[192,768]{1,0:T(8,128)(2,1)}, bf16[192,768]{1,0:T(8,128)(2,1)}, u32[]{:S(2)}, u32[]{:S(2)}) collective-permute-start(bf16[192,768]{1,0:T(8,128)(2,1)} %constant_dynamic-slice_fusion.7), channel_id=1, source_target_pairs={{0,1},{1,0},{2,3},{3,2},{4,5},{5,4},{6,7},{7,6},{8,9},{9,8},{10,11... | collective-permute-start | bytes 884744 | tf_op jit(solution)/shard_map/ppermute | solution.py:921
  6.9 1.4 select_bitcast_fusion
  8.3 0.9 slice.179
  9.3 0.8 copy.195.wdt_a
  10.1 2.0 collective-permute-start.1
  12.1 1.4 copy.193.conv
  14.2 1.7 small.1.small_a
  16.6 1.2 fusion.7
  17.8 2.1 collective-permute-start.8
  20.5 1.5 collective-permute-start.4
  22.0 8.7 %front.1 = (s32[8]{0:T(128)}, f32[8,1536]{1,0:T(8,128)}, f32[8,1536]{1,0:T(8,128)}, f32[8,1536]{1,0:T(8,128)}, bf16[768,128]{1,0:T(8,128)(2,1)}, /*index=5*/bf16...) custom-call(s32[1,4]{1,0:T(1,128)} %starts.1, ...), custom_call_target="tpu_custom_call" | custom-call | flops 8800000000 | bytes 8000000 | tf_op jit(solution)/shard_map/front/pallas_call | solution.py:1002
  31.3 8.8 %vals_own.1 = (bf16[640,1536]{1,0:T(8,128)(2,1)}, bf16[672,1536]{1,0:T(8,128)(2,1)}, bf16[640,1536]{1,0:T(8,128)(2,1)}, bf16[12,6,128,128]{3,2,1,0:T(8,128)(2,1)}, bf16[12,64,128]{2,1,0:T(8,128)(2,1)}) custom-call(s32[8]{0:T(128)} %get-tuple-element.94.info, bf16[672,768]{1,0:T(8,128)(2,1)} %get-tuple-element.93.normed, bf16[768,768]{1,0:T(8,128)(2,1)} %copy-done.1, ...), custom_call_target="tpu_custom_call" | custom-call | flops 8800000000 | bytes 8000000 | tf_op jit(solution)/shard_map/vals_own/pallas_call | solution.py:1037
  40.1 2.0 collective-permute-start.9
  42.9 9.8 %vals_other.1 = (bf16[640,1536]{1,0:T(8,128)(2,1)}, bf16[672,1536]{1,0:T(8,128)(2,1)}, bf16[640,1536]{1,0:T(8,128)(2,1)}, bf16[12,6,128,128]{3,2,1,0:T(8,128)(2,...) custom-call(s32[8]{0:T(128)} %get-tuple-element.94.info, ...), custom_call_target="tpu_custom_call", output_to_operand_aliasing={{0}: (10, {}), {1}: (11, {}), {2}: (12, {}), {3}: (13, {}),... | custom-call | flops 8800000000 | bytes 8000000 | tf_op jit(solution)/shard_map/vals_other/pallas_call | solution.py:1037
  52.7 1.6 collective-permute-start.7
  54.3 1.4 collective-permute-done.9.p1
  55.7 3.9 %collective-permute-done.7.s0_ref = bf16[12,64,128]{2,1,0:T(8,128)(2,1)S(1)} collective-permute-done((bf16[12,64,128]{2,1,0:T(8,128)(2,1)}, bf16[12,64,128]{2,1,0:T(8,128)(2,1)S(1)}, u32[]{:S(2)}, u32[]{:S(2)}) %collective-permute-start.7) | collective-permute-done | bytes 196640 | tf_op jit(solution)/shard_map/ppermute | solution.py:921
  60.3 19.7 %scan.1 = (bf16[640,1536]{1,0:T(8,128)(2,1)}, bf16[12,6,128,128]{3,2,1,0:T(8,128)(2,1)}) custom-call(s32[8]{0:T(128)} %get-tuple-element.94.info, bf16[640,1536]{1,0:T(8,128)(2,1)} %get-tuple-element.104.xc_ref, bf16[12,6,128,128]{3,2,1,0:T(8,128)(2,1)} %get-tuple-element.105.s_ref, bf16[12,64,128]{2,1,0:T(8,128)(2,1)} %copy-done.22, ...), custom_call_target="tpu_custom_call" | custom-call | flops 20899999744 | bytes 19000000 | tf_op jit(solution)/shard_map/scan/pallas_call | solution.py:1057
  80.0 0.8 copy-done.15
  81.0 24.1 %gated.1 = (bf16[640,768]{1,0:T(8,128)(2,1)}, bf16[640,1536]{1,0:T(8,128)(2,1)}, bf16[2,384,1536]{2,1,0:T(8,128)(2,1)}, bf16[2,384,1536]{2,1,0:T(8,128)(2,1)}, b...) custom-call(bf16[640,768]{1,0:T(8,128)(2,1)} %bitcast.129, bf16[640,768]{1,0:T(8,128)(2,1)} %bitcast.131, ...), custom_call_target="tpu_custom_call" | custom-call | flops 24199999488 | bytes 22000000 | tf_op jit(solution)/shard_map/gated/pallas_call | solution.py:1073
  105.3 1.8 fusion.23
  107.0 9.2 %gstate.1 = (bf16[12,6,128,128]{3,2,1,0:T(8,128)(2,1)}, bf16[12,64,128]{2,1,0:T(8,128)(2,1)}) custom-call(s32[8]{0:T(128)} %get-tuple-element.94.info, bf16[640,1536]{1,0:T(8,128)(2,1)} %get-tuple-element.116.gy_ref, f32[5,128,128]{2,1,0:T(8,128)} %get-tuple-element.118.et, f32[5,128,128]{2,1,0:T(8,128)} %get-tuple-element.119.cet, ...), custom_call_target="tpu_custom_call" | custom-call | flops 9900000256 | bytes 9000000 | tf_op jit(solution)/shard_map/gstate/pallas_call | solution.py:1115
  117.3 1.5 collective-permute-start.13
  119.8 2.5 collective-permute-start.16
  122.3 2.7 collective-permute-done.13.gs0_ref
  125.7 35.6 %gscan.1 = (bf16[640,1536]{1,0:T(8,128)(2,1)}, f32[5,128,128]{2,1,0:T(8,128)}, f32[5,128,128]{2,1,0:T(8,128)}, f32[5,128,128]{2,1,0:T(8,128)}, f32[640,128]{1,0:...) custom-call(s32[8]{0:T(128)} %get-tuple-element.94.info, ...), custom_call_target="tpu_custom_call" | custom-call | flops 38499999744 | bytes 35000000 | tf_op jit(solution)/shard_map/gscan/pallas_call | solution.py:1129
  161.6 6.4 %join.1 = (f32[672,256]{1,0:T(8,128)}, bf16[640,128]{1,0:T(8,128)(2,1)}, f32[16,128]{1,0:T(8,128)}) custom-call(s32[8]{0:T(128)} %get-tuple-element.94.info, f32[5,128,128]{2,1,0:T(8,128)} %get-tuple-element.141.ggt, f32[5,128,128]{2,1,0:T(8,128)} %get-tuple-element.142.gb, f32[5,128,128]{2,1,0:T(8,128)} %get-tuple-element.143.gct, ...), custom_call_target="tpu_custom_call" | custom-call | flops 6600000000 | bytes 6000000 | tf_op jit(solution)/shard_map/join/pallas_call | solution.py:1153
  168.8 1.5 collective-permute-start.18
  170.3 0.8 slice_select_fusion
  171.6 1.6 collective-permute-start.26
  173.3 2.6 collective-permute-start.27
  176.8 24.9 %back.1 = (bf16[2,384,768]{2,1,0:T(8,128)(2,1)}, bf16[2,384,768]{2,1,0:T(8,128)(2,1)}, f32[8,1536]{1,0:T(8,128)}, bf16[2,384,384]{2,1,0:T(8,128)(2,1)}, bf16[2,3...) custom-call(s32[8]{0:T(128)} %get-tuple-element.94.info, ...), custom_call_target="tpu_custom_call" | custom-call | flops 26400000000 | bytes 24000000 | tf_op jit(solution)/shard_map/back/pallas_call | solution.py:1167
  201.7 0.9 constant_dynamic-update-slice_fusion.4
  202.7 0.7 constant_dynamic-update-slice_fusion
  204.4 1.4 pad_maximum_fusion
  207.1 1.6 collective-permute-start.21
  209.0 1.6 collective-permute-start.20
  210.8 7.0 %collective-permute-done.20 = f32[48,768]{1,0:T(8,128)S(1)} collective-permute-done((f32[48,768]{1,0:T(8,128)S(1)}, f32[48,768]{1,0:T(8,128)S(1)}, u32[]{:S(2)}, u32[]{:S(2)}) %collective-permute-start.20) | collective-permute-done | bytes 147488 | tf_op jit(solution)/shard_map/ppermute | solution.py:925
  219.1 3.5 %collective-permute-start.24 = (f32[48,768]{1,0:T(8,128)}, f32[48,768]{1,0:T(8,128)}, u32[]{:S(2)}, u32[]{:S(2)}) collective-permute-start(f32[48,768]{1,0:T(8,128)} %add_add_fusion.1), channel_id=1, source_target_pairs={{0,16},{2,18},{4,20},{6,22},{8,24},{10,26},{12,28},{14,30},{16,0},... | collective-permute-start | bytes 442376 | tf_op jit(solution)/shard_map/ppermute | solution.py:925
  223.5 1.8 reshape.121
  225.3 1.8 reshape.124
  227.1 1.8 copy.225
  228.9 5.1 %collective-permute-done.24 = f32[48,768]{1,0:T(8,128)} collective-permute-done((f32[48,768]{1,0:T(8,128)}, f32[48,768]{1,0:T(8,128)}, u32[]{:S(2)}, u32[]{:S(2)}) %collective-permute-start.24) | collective-permute-done | bytes 147488 | tf_op jit(solution)/shard_map/ppermute | solution.py:925
  234.0 1.2 add_add_fusion
  236.4 1.4 reshape.123
  237.8 1.5 constant_dynamic-slice_fusion.1
  239.4 1.5 copy.224
  240.9 1.9 slice_reduce_fusion
  243.7 0.8 reshape_squeeze.6
  245.0 1.4 fusion.20
  247.5 1.6 collective-permute-start.31
  249.1 1.4 collective-permute-start.32
  251.1 0.8 fusion.29
  252.6 7.2 %collective-permute-done.30 = bf16[4,48,1152]{2,1,0:T(8,128)(2,1)S(1)} collective-permute-done((bf16[4,48,1152]{2,1,0:T(8,128)(2,1)S(1)}, bf16[4,48,1152]{2,1,0:T(8,128)(2,1)S(1)}, u32[]{:S(2)}, u32[]{:S(2)}) %collective-permute-start.30) | collective-permute-done | bytes 442400 | tf_op jit(solution)/shard_map/ppermute | solution.py:925
  259.9 4.9 %collective-permute-done.31 = bf16[4,48,1152]{2,1,0:T(8,128)(2,1)S(1)} collective-permute-done((bf16[4,48,1152]{2,1,0:T(8,128)(2,1)S(1)}, bf16[4,48,1152]{2,1,0:T(8,128)(2,1)S(1)}, u32[]{:S(2)}, u32[]{:S(2)}) %collective-permute-start.31) | collective-permute-done | bytes 442400 | tf_op jit(solution)/shard_map/ppermute | solution.py:921
  264.8 1.3 collective-permute-done.32
  266.5 3.9 %collective-permute-start.33 = (bf16[48,1152]{1,0:T(8,128)(2,1)S(1)}, bf16[48,1152]{1,0:T(8,128)(2,1)S(1)}, u32[]{:S(2)}, u32[]{:S(2)}) collective-permute-start(bf16[48,1152]{1,0:T(8,128)(2,1)S(1)} %get-tuple-element.255), channel_id=1, source_target_pairs={{0,8},{2,10},{4,12},{6,14},{8,0},{10,2},{12,4},{14,6},{16,24},{18,... | collective-permute-start | bytes 331784 | tf_op jit(solution)/shard_map/ppermute | solution.py:925
  270.4 1.2 collective-permute-start.34
  271.6 1.4 collective-permute-start.35
  273.0 1.3 fusion.19
  274.2 5.5 %collective-permute-done.34 = bf16[48,1152]{1,0:T(8,128)(2,1)S(1)} collective-permute-done((bf16[48,1152]{1,0:T(8,128)(2,1)S(1)}, bf16[48,1152]{1,0:T(8,128)(2,1)S(1)}, u32[]{:S(2)}, u32[]{:S(2)}) %collective-permute-start.34) | collective-permute-done | bytes 110624 | tf_op jit(solution)/shard_map/ppermute | solution.py:925
  281.3 1.2 copy.223
  (137 shorter events, 22.8 us)
Async XLA Ops:
  2.5 11.1 %copy-start.12 = (f32[12,2]{0,1:T(2,128)S(1)}, f32[12,2]{0,1:T(2,128)}, u32[]{:S(2)}) copy-start(f32[12,2]{0,1:T(2,128)} %param.20) | copy-start | bytes 292
  3.1 13.4 %copy-start.1 = (bf16[768,768]{1,0:T(8,128)(2,1)}, bf16[768,768]{1,0:T(8,128)(2,1)S(1)}, u32[]{:S(2)}) copy-start(bf16[768,768]{1,0:T(8,128)(2,1)S(1)} %copy.196.refs_0_.wv_a) | copy-start | bytes 3538948
  4.0 16.5 %collective-permute-start.3 = (bf16[192,768]{1,0:T(8,128)(2,1)}, bf16[192,768]{1,0:T(8,128)(2,1)}, u32[]{:S(2)}, u32[]{:S(2)}) collective-permute-start(bf16[192,768]{1,0:T(8,128)(2,1)} %constant_dynamic-slice_fusion.7), channel_id=1, source_target_pairs={{0,1},{1,0},{2,3},{3,2},{4,5},{5,4},{6,7},{7,6},{8,9},{9,8},{10,11... | collective-permute-start | bytes 884744 | tf_op jit(solution)/shard_map/ppermute | solution.py:921
  8.3 13.7 %collective-permute-start = (bf16[16,768]{1,0:T(8,128)(2,1)}, bf16[16,768]{1,0:T(8,128)(2,1)}, u32[]{:S(2)}, u32[]{:S(2)}) collective-permute-start(bf16[16,768]{1,0:T(8,128)(2,1)} %select_bitcast_fusion), channel_id=1, source_target_pairs={{0,1},{1,0},{2,3},{3,2},{4,5},{5,4},{6,7},{7,6},{8,9},{9,8},{10,11... | collective-permute-start | bytes 73736 | tf_op jit(solution)/shard_map/ppermute | solution.py:921
  10.1 11.9 %collective-permute-start.1 = (bf16[768,24]{1,0:T(8,128)(2,1)}, bf16[768,24]{1,0:T(8,128)(2,1)}, u32[]{:S(2)}, u32[]{:S(2)}) collective-permute-start(bf16[768,24]{1,0:T(8,128)(2,1)} %copy.195.wdt_a), channel_id=1, source_target_pairs={{0,1},{1,0},{2,3},{3,2},{4,5},{5,4},{6,7},{7,6},{8,9},{9,8},{10,11... | collective-permute-start | bytes 110600 | tf_op jit(solution)/shard_map/ppermute | solution.py:921
  15.9 6.1 %collective-permute-start.2 = (f32[32,768]{1,0:T(8,128)}, f32[32,768]{1,0:T(8,128)}, u32[]{:S(2)}, u32[]{:S(2)}) collective-permute-start(f32[32,768]{1,0:T(8,128)} %small.1.small_a), channel_id=1, source_target_pairs={{0,1},{1,0},{2,3},{3,2},{4,5},{5,4},{6,7},{7,6},{8,9},{9,8},{10,11... | collective-permute-start | bytes 294920 | tf_op jit(solution)/shard_map/ppermute | solution.py:921
  16.5 1.3 copy-start
  16.5 3.4 %copy-start.11 = (f32[768]{0:T(1024)S(1)}, f32[768]{0:T(1024)}, u32[]{:S(2)}) copy-start(f32[768]{0:T(1024)} %param.15) | copy-start | bytes 9220
  17.8 22.3 %collective-permute-start.8 = (bf16[192,1536]{1,0:T(8,128)(2,1)S(1)}, bf16[192,1536]{1,0:T(8,128)(2,1)S(1)}, u32[]{:S(2)}, u32[]{:S(2)}) collective-permute-start(bf16[192,1536]{1,0:T(8,128)(2,1)S(1)} %fusion.7), channel_id=1, source_target_pairs={{0,1},{1,0},{2,3},{3,2},{4,5},{5,4},{6,7},{7,6},{8,9},{9,8},{10,11... | collective-permute-start | bytes 1769480 | tf_op jit(solution)/shard_map/ppermute | solution.py:921
  20.5 10.3 %collective-permute-start.4 = (bf16[192,768]{1,0:T(8,128)(2,1)}, bf16[192,768]{1,0:T(8,128)(2,1)S(1)}, u32[]{:S(2)}, u32[]{:S(2)}) collective-permute-start(bf16[192,768]{1,0:T(8,128)(2,1)} %collective-permute-done.3.refs_0_), channel_id=1, source_target_pairs={{0,4},{2,6},{4,0},{6,2},{8,12},{10,14},{12,8},{14,10},{16,20},{18,... | collective-permute-start | bytes 884744 | tf_op jit(solution)/shard_map/ppermute | solution.py:925
  30.7 11.4 %collective-permute-start.5 = (bf16[192,768]{1,0:T(8,128)(2,1)}, bf16[192,768]{1,0:T(8,128)(2,1)S(1)}, u32[]{:S(2)}, u32[]{:S(2)}) collective-permute-start(bf16[192,768]{1,0:T(8,128)(2,1)} %collective-permute-done.3.refs_0_), channel_id=1, source_target_pairs={{0,2},{2,0},{4,6},{6,4},{8,10},{10,8},{12,14},{14,12},{16,18},{18,... | collective-permute-start | bytes 884744 | tf_op jit(solution)/shard_map/ppermute | solution.py:925
  30.8 9.3 %copy-start.17 = (bf16[192,768]{1,0:T(8,128)(2,1)}, bf16[192,768]{1,0:T(8,128)(2,1)S(1)}, u32[]{:S(2)}) copy-start(bf16[192,768]{1,0:T(8,128)(2,1)S(1)} %collective-permute-done.4.refs_1_) | copy-start | bytes 884740
  30.8 11.3 %collective-permute-start.6 = (bf16[192,768]{1,0:T(8,128)(2,1)S(1)}, bf16[192,768]{1,0:T(8,128)(2,1)S(1)}, u32[]{:S(2)}, u32[]{:S(2)}) collective-permute-start(bf16[192,768]{1,0:T(8,128)(2,1)S(1)} %collective-permute-done.4.refs_1_), channel_id=1, source_target_pairs={{0,2},{2,0},{4,6},{6,4},{8,10},{10,8},{12,14},{14,12},{16,18},{18,... | collective-permute-start | bytes 884744 | tf_op jit(solution)/shard_map/ppermute | solution.py:925
  40.1 14.2 %copy-start.13 = (bf16[192,1536]{1,0:T(8,128)(2,1)}, bf16[192,1536]{1,0:T(8,128)(2,1)S(1)}, u32[]{:S(2)}) copy-start(bf16[192,1536]{1,0:T(8,128)(2,1)S(1)} %collective-permute-done.8.p0) | copy-start | bytes 1769476
  40.1 15.6 %collective-permute-start.9 = (bf16[192,1536]{1,0:T(8,128)(2,1)S(1)}, bf16[192,1536]{1,0:T(8,128)(2,1)S(1)}, u32[]{:S(2)}, u32[]{:S(2)}) collective-permute-start(bf16[192,1536]{1,0:T(8,128)(2,1)S(1)} %collective-permute-done.8.p0), channel_id=1, source_target_pairs={{0,4},{2,6},{4,0},{6,2},{8,12},{10,14},{12,8},{14,10},{16,20},{18,... | collective-permute-start | bytes 1769480 | tf_op jit(solution)/shard_map/ppermute | solution.py:925
  42.1 0.7 copy-start.18
  42.1 0.8 copy-start.19
  52.7 6.9 %collective-permute-start.7 = (bf16[12,64,128]{2,1,0:T(8,128)(2,1)}, bf16[12,64,128]{2,1,0:T(8,128)(2,1)S(1)}, u32[]{:S(2)}, u32[]{:S(2)}) collective-permute-start(bf16[12,64,128]{2,1,0:T(8,128)(2,1)} %get-tuple-element.106), channel_id=1, source_target_pairs={{0,1},{1,0},{2,3},{3,2},{4,5},{5,4},{6,7},{7,6},{8,9},{9,8},{10,11... | collective-permute-start | bytes 589832 | tf_op jit(solution)/shard_map/ppermute | solution.py:921
  54.3 25.7 %collective-permute-start.10 = (bf16[192,1536]{1,0:T(8,128)(2,1)S(1)}, bf16[192,1536]{1,0:T(8,128)(2,1)S(1)}, u32[]{:S(2)}, u32[]{:S(2)}) collective-permute-start(bf16[192,1536]{1,0:T(8,128)(2,1)S(1)} %collective-permute-done.8.p0), channel_id=1, source_target_pairs={{0,2},{2,0},{4,6},{6,4},{8,10},{10,8},{12,14},{14,12},{16,18},{18,... | collective-permute-start | bytes 1769480 | tf_op jit(solution)/shard_map/ppermute | solution.py:925
  55.7 24.3 %copy-start.14 = (bf16[192,1536]{1,0:T(8,128)(2,1)}, bf16[192,1536]{1,0:T(8,128)(2,1)S(1)}, u32[]{:S(2)}) copy-start(bf16[192,1536]{1,0:T(8,128)(2,1)S(1)} %collective-permute-done.9.p1) | copy-start | bytes 1769476
  55.7 24.3 %collective-permute-start.11 = (bf16[192,1536]{1,0:T(8,128)(2,1)S(1)}, bf16[192,1536]{1,0:T(8,128)(2,1)S(1)}, u32[]{:S(2)}, u32[]{:S(2)}) collective-permute-start(bf16[192,1536]{1,0:T(8,128)(2,1)S(1)} %collective-permute-done.9.p1), channel_id=1, source_target_pairs={{0,2},{2,0},{4,6},{6,4},{8,10},{10,8},{12,14},{14,12},{16,18},{18,... | collective-permute-start | bytes 1769480 | tf_op jit(solution)/shard_map/ppermute | solution.py:925
  59.6 0.7 copy-start.22
  80.0 0.8 copy-start.15
  80.0 1.0 copy-start.16
  105.1 11.1 %collective-permute-start.12 = (bf16[2,384,1536]{2,1,0:T(8,128)(2,1)}, bf16[2,384,1536]{2,1,0:T(8,128)(2,1)S(1)}, u32[]{:S(2)}, u32[]{:S(2)}) collective-permute-start(bf16[2,384,1536]{2,1,0:T(8,128)(2,1)} %get-tuple-element.123), channel_id=1, source_target_pairs={{0,2},{2,0},{4,6},{6,4},{8,10},{10,8},{12,14},{14,12},{16,18},{18,... | collective-permute-start | bytes 7077896 | tf_op jit(solution)/shard_map/ppermute | solution.py:925
  116.4 0.9 copy-start.20
  117.3 7.7 %collective-permute-start.13 = (bf16[12,64,128]{2,1,0:T(8,128)(2,1)S(1)}, bf16[12,64,128]{2,1,0:T(8,128)(2,1)S(1)}, u32[]{:S(2)}, u32[]{:S(2)}) collective-permute-start(bf16[12,64,128]{2,1,0:T(8,128)(2,1)S(1)} %copy-done.20), channel_id=1, source_target_pairs={{0,1},{1,0},{2,3},{3,2},{4,5},{5,4},{6,7},{7,6},{8,9},{9,8},{10,11... | collective-permute-start | bytes 589832 | tf_op jit(solution)/shard_map/ppermute | solution.py:921
  118.8 42.5 %collective-permute-start.14 = (bf16[4,48,1536]{2,1,0:T(8,128)(2,1)S(1)}, bf16[4,48,1536]{2,1,0:T(8,128)(2,1)S(1)}, u32[]{:S(2)}, u32[]{:S(2)}) collective-permute-start(bf16[4,48,1536]{2,1,0:T(8,128)(2,1)S(1)} %get-tuple-element.133), channel_id=1, source_target_pairs={{0,4},{2,6},{4,0},{6,2},{8,12},{10,14},{12,8},{14,10},{16,20},{18,... | collective-permute-start | bytes 1769480 | tf_op jit(solution)/shard_map/ppermute | solution.py:925
  119.3 41.9 %collective-permute-start.15 = (bf16[4,48,1536]{2,1,0:T(8,128)(2,1)S(1)}, bf16[4,48,1536]{2,1,0:T(8,128)(2,1)S(1)}, u32[]{:S(2)}, u32[]{:S(2)}) collective-permute-start(bf16[4,48,1536]{2,1,0:T(8,128)(2,1)S(1)} %get-tuple-element.134), channel_id=1, source_target_pairs={{0,1},{1,0},{2,3},{3,2},{4,5},{5,4},{6,7},{7,6},{8,9},{9,8},{10,11... | collective-permute-start | bytes 1769480 | tf_op jit(solution)/shard_map/ppermute | solution.py:921
  119.8 41.5 %collective-permute-start.16 = (bf16[4,48,1536]{2,1,0:T(8,128)(2,1)S(1)}, bf16[4,48,1536]{2,1,0:T(8,128)(2,1)S(1)}, u32[]{:S(2)}, u32[]{:S(2)}) collective-permute-start(bf16[4,48,1536]{2,1,0:T(8,128)(2,1)S(1)} %get-tuple-element.135), channel_id=1, source_target_pairs={{0,5},{1,4},{2,7},{3,6},{4,1},{5,0},{6,3},{7,2},{8,13},{9,12},{10,... | collective-permute-start | bytes 1769480 | tf_op jit(solution)/shard_map/ppermute | solution.py:930
  125.0 0.7 copy-start.21
  168.8 7.3 %collective-permute-start.18 = (f32[16,256]{1,0:T(8,128)S(1)}, f32[16,256]{1,0:T(8,128)S(1)}, u32[]{:S(2)}, u32[]{:S(2)}) collective-permute-start(f32[16,256]{1,0:T(8,128)S(1)} %slice_select_fusion.1), channel_id=1, source_target_pairs={{0,1},{1,0},{2,3},{3,2},{4,5},{5,4},{6,7},{7,6},{8,9},{9,8},{10,11... | collective-permute-start | bytes 49160 | tf_op jit(solution)/shard_map/ppermute | solution.py:921
  171.1 5.0 %collective-permute-start.17 = (bf16[16,1536]{1,0:T(8,128)(2,1)S(1)}, bf16[16,1536]{1,0:T(8,128)(2,1)S(1)}, u32[]{:S(2)}, u32[]{:S(2)}) collective-permute-start(bf16[16,1536]{1,0:T(8,128)(2,1)S(1)} %slice_select_fusion), channel_id=1, source_target_pairs={{0,1},{1,0},{2,3},{3,2},{4,5},{5,4},{6,7},{7,6},{8,9},{9,8},{10,11... | collective-permute-start | bytes 147464 | tf_op jit(solution)/shard_map/ppermute | solution.py:921
  171.6 32.6 %collective-permute-start.26 = (bf16[48,1536]{1,0:T(8,128)(2,1)S(1)}, bf16[48,1536]{1,0:T(8,128)(2,1)S(1)}, u32[]{:S(2)}, u32[]{:S(2)}) collective-permute-start(bf16[48,1536]{1,0:T(8,128)(2,1)S(1)} %get-tuple-element.252), channel_id=1, source_target_pairs={{0,8},{2,10},{4,12},{6,14},{8,0},{10,2},{12,4},{14,6},{16,24},{18,... | collective-permute-start | bytes 442376 | tf_op jit(solution)/shard_map/ppermute | solution.py:925
  173.3 30.9 %collective-permute-start.27 = (bf16[48,1536]{1,0:T(8,128)(2,1)S(1)}, bf16[48,1536]{1,0:T(8,128)(2,1)S(1)}, u32[]{:S(2)}, u32[]{:S(2)}) collective-permute-start(bf16[48,1536]{1,0:T(8,128)(2,1)S(1)} %get-tuple-element.254), channel_id=1, source_target_pairs={{0,16},{2,18},{4,20},{6,22},{8,24},{10,26},{12,28},{14,30},{16,0},... | collective-permute-start | bytes 442376 | tf_op jit(solution)/shard_map/ppermute | solution.py:925
  175.9 28.4 %collective-permute-start.28 = (bf16[48,1536]{1,0:T(8,128)(2,1)S(1)}, bf16[48,1536]{1,0:T(8,128)(2,1)S(1)}, u32[]{:S(2)}, u32[]{:S(2)}) collective-permute-start(bf16[48,1536]{1,0:T(8,128)(2,1)S(1)} %get-tuple-element.253), channel_id=1, source_target_pairs={{0,24},{2,26},{4,28},{6,30},{8,16},{10,18},{12,20},{14,22},{16,8},... | collective-permute-start | bytes 442376 | tf_op jit(solution)/shard_map/ppermute | solution.py:925
  176.1 0.6 copy-start.24
  176.1 0.6 copy-start.23
  176.8 25.9 %copy-start.8 = (f32[8,1536]{1,0:T(8,128)S(1)}, f32[8,1536]{1,0:T(8,128)}, u32[]{:S(2)}) copy-start(f32[8,1536]{1,0:T(8,128)} %get-tuple-element.161) | copy-start | bytes 147460
  176.8 25.9 %copy-start.9 = (f32[8,1536]{1,0:T(8,128)S(1)}, f32[8,1536]{1,0:T(8,128)}, u32[]{:S(2)}) copy-start(f32[8,1536]{1,0:T(8,128)} %get-tuple-element.162) | copy-start | bytes 147460
  176.8 25.9 %copy-start.10 = (f32[16,128]{1,0:T(8,128)S(1)}, f32[16,128]{1,0:T(8,128)}, u32[]{:S(2)}) copy-start(f32[16,128]{1,0:T(8,128)} %get-tuple-element.163) | copy-start | bytes 24580
  201.7 2.6 copy-start.3
  201.7 2.6 copy-start.5
  204.1 2.8 %collective-permute-start.19 = (f32[2,48,768]{2,1,0:T(8,128)S(1)}, f32[2,48,768]{2,1,0:T(8,128)S(1)}, u32[]{:S(2)}, u32[]{:S(2)}) collective-permute-start(f32[2,48,768]{2,1,0:T(8,128)S(1)} %pad_maximum_fusion.2), channel_id=1, source_target_pairs={{0,2},{2,0},{4,6},{6,4},{8,10},{10,8},{12,14},{14,12},{16,18},{18,... | collective-permute-start | bytes 884744 | tf_op jit(solution)/shard_map/ppermute | solution.py:925
  204.4 1.9 copy-start.4
  205.7 1.2 copy-start.6
  205.7 40.7 %collective-permute-start.29 = (bf16[2,384,1152]{2,1,0:T(8,128)(2,1)}, bf16[2,384,1152]{2,1,0:T(8,128)(2,1)S(1)}, u32[]{:S(2)}, u32[]{:S(2)}) collective-permute-start(bf16[2,384,1152]{2,1,0:T(8,128)(2,1)} %pad_maximum_fusion), channel_id=1, source_target_pairs={{0,2},{2,0},{4,6},{6,4},{8,10},{10,8},{12,14},{14,12},{16,18},{18,... | collective-permute-start | bytes 5308424 | tf_op jit(solution)/shard_map/ppermute | solution.py:925
  207.1 10.7 %collective-permute-start.21 = (f32[48,768]{1,0:T(8,128)S(1)}, f32[48,768]{1,0:T(8,128)S(1)}, u32[]{:S(2)}, u32[]{:S(2)}) collective-permute-start(f32[48,768]{1,0:T(8,128)S(1)} %get-tuple-element.261), channel_id=1, source_target_pairs={{0,1},{1,0},{2,3},{3,2},{4,5},{5,4},{6,7},{7,6},{8,9},{9,8},{10,11... | collective-permute-start | bytes 442376 | tf_op jit(solution)/shard_map/ppermute | solution.py:921
  208.6 9.1 %collective-permute-start.22 = (f32[48,768]{1,0:T(8,128)S(1)}, f32[48,768]{1,0:T(8,128)S(1)}, u32[]{:S(2)}, u32[]{:S(2)}) collective-permute-start(f32[48,768]{1,0:T(8,128)S(1)} %get-tuple-element.261), channel_id=1, source_target_pairs={{0,5},{1,4},{2,7},{3,6},{4,1},{5,0},{6,3},{7,2},{8,13},{9,12},{10,... | collective-permute-start | bytes 442376 | tf_op jit(solution)/shard_map/ppermute | solution.py:930
  209.0 8.7 %collective-permute-start.20 = (f32[48,768]{1,0:T(8,128)S(1)}, f32[48,768]{1,0:T(8,128)S(1)}, u32[]{:S(2)}, u32[]{:S(2)}) collective-permute-start(f32[48,768]{1,0:T(8,128)S(1)} %get-tuple-element.260), channel_id=1, source_target_pairs={{0,4},{2,6},{4,0},{6,2},{8,12},{10,14},{12,8},{14,10},{16,20},{18,... | collective-permute-start | bytes 442376 | tf_op jit(solution)/shard_map/ppermute | solution.py:925
  218.4 10.4 %collective-permute-start.23 = (f32[48,768]{1,0:T(8,128)}, f32[48,768]{1,0:T(8,128)}, u32[]{:S(2)}, u32[]{:S(2)}) collective-permute-start(f32[48,768]{1,0:T(8,128)} %add_add_fusion.1), channel_id=1, source_target_pairs={{0,8},{2,10},{4,12},{6,14},{8,0},{10,2},{12,4},{14,6},{16,24},{18,... | collective-permute-start | bytes 442376 | tf_op jit(solution)/shard_map/ppermute | solution.py:925
  219.1 14.9 %collective-permute-start.24 = (f32[48,768]{1,0:T(8,128)}, f32[48,768]{1,0:T(8,128)}, u32[]{:S(2)}, u32[]{:S(2)}) collective-permute-start(f32[48,768]{1,0:T(8,128)} %add_add_fusion.1), channel_id=1, source_target_pairs={{0,16},{2,18},{4,20},{6,22},{8,24},{10,26},{12,28},{14,30},{16,0},... | collective-permute-start | bytes 442376 | tf_op jit(solution)/shard_map/ppermute | solution.py:925
  222.6 11.4 %collective-permute-start.25 = (f32[48,768]{1,0:T(8,128)}, f32[48,768]{1,0:T(8,128)}, u32[]{:S(2)}, u32[]{:S(2)}) collective-permute-start(f32[48,768]{1,0:T(8,128)} %add_add_fusion.1), channel_id=1, source_target_pairs={{0,24},{2,26},{4,28},{6,30},{8,16},{10,18},{12,20},{14,22},{16,8},... | collective-permute-start | bytes 442376 | tf_op jit(solution)/shard_map/ppermute | solution.py:925
  235.1 0.7 copy-start.7
  246.7 13.2 %collective-permute-start.30 = (bf16[4,48,1152]{2,1,0:T(8,128)(2,1)S(1)}, bf16[4,48,1152]{2,1,0:T(8,128)(2,1)S(1)}, u32[]{:S(2)}, u32[]{:S(2)}) collective-permute-start(bf16[4,48,1152]{2,1,0:T(8,128)(2,1)S(1)} %fusion.9), channel_id=1, source_target_pairs={{0,4},{2,6},{4,0},{6,2},{8,12},{10,14},{12,8},{14,10},{16,20},{18,... | collective-permute-start | bytes 1327112 | tf_op jit(solution)/shard_map/ppermute | solution.py:925
  247.5 17.3 %collective-permute-start.31 = (bf16[4,48,1152]{2,1,0:T(8,128)(2,1)S(1)}, bf16[4,48,1152]{2,1,0:T(8,128)(2,1)S(1)}, u32[]{:S(2)}, u32[]{:S(2)}) collective-permute-start(bf16[4,48,1152]{2,1,0:T(8,128)(2,1)S(1)} %get-tuple-element.250), channel_id=1, source_target_pairs={{0,1},{1,0},{2,3},{3,2},{4,5},{5,4},{6,7},{7,6},{8,9},{9,8},{10,11... | collective-permute-start | bytes 1327112 | tf_op jit(solution)/shard_map/ppermute | solution.py:921
  249.1 17.0 %collective-permute-start.32 = (bf16[4,48,1152]{2,1,0:T(8,128)(2,1)S(1)}, bf16[4,48,1152]{2,1,0:T(8,128)(2,1)S(1)}, u32[]{:S(2)}, u32[]{:S(2)}) collective-permute-start(bf16[4,48,1152]{2,1,0:T(8,128)(2,1)S(1)} %get-tuple-element.251), channel_id=1, source_target_pairs={{0,5},{1,4},{2,7},{3,6},{4,1},{5,0},{6,3},{7,2},{8,13},{9,12},{10,... | collective-permute-start | bytes 1327112 | tf_op jit(solution)/shard_map/ppermute | solution.py:930
  266.5 7.8 %collective-permute-start.33 = (bf16[48,1152]{1,0:T(8,128)(2,1)S(1)}, bf16[48,1152]{1,0:T(8,128)(2,1)S(1)}, u32[]{:S(2)}, u32[]{:S(2)}) collective-permute-start(bf16[48,1152]{1,0:T(8,128)(2,1)S(1)} %get-tuple-element.255), channel_id=1, source_target_pairs={{0,8},{2,10},{4,12},{6,14},{8,0},{10,2},{12,4},{14,6},{16,24},{18,... | collective-permute-start | bytes 331784 | tf_op jit(solution)/shard_map/ppermute | solution.py:925
  270.4 9.3 %collective-permute-start.34 = (bf16[48,1152]{1,0:T(8,128)(2,1)S(1)}, bf16[48,1152]{1,0:T(8,128)(2,1)S(1)}, u32[]{:S(2)}, u32[]{:S(2)}) collective-permute-start(bf16[48,1152]{1,0:T(8,128)(2,1)S(1)} %get-tuple-element.257), channel_id=1, source_target_pairs={{0,16},{2,18},{4,20},{6,22},{8,24},{10,26},{12,28},{14,30},{16,0},... | collective-permute-start | bytes 331784 | tf_op jit(solution)/shard_map/ppermute | solution.py:925
  271.6 8.1 %collective-permute-start.35 = (bf16[48,1152]{1,0:T(8,128)(2,1)S(1)}, bf16[48,1152]{1,0:T(8,128)(2,1)S(1)}, u32[]{:S(2)}, u32[]{:S(2)}) collective-permute-start(bf16[48,1152]{1,0:T(8,128)(2,1)S(1)} %get-tuple-element.256), channel_id=1, source_target_pairs={{0,24},{2,26},{4,28},{6,30},{8,16},{10,18},{12,20},{14,22},{16,8},... | collective-permute-start | bytes 331784 | tf_op jit(solution)/shard_map/ppermute | solution.py:925
  274.2 6.7 %copy-start.2 = (f32[48,12,64]{2,1,0:T(8,128)S(1)}, f32[48,12,64]{2,1,0:T(8,128)}, u32[]{:S(2)}) copy-start(f32[48,12,64]{2,1,0:T(8,128)} %reshape.121) | copy-start | bytes 442372

commit v2 on v1

--- a/solution.py
+++ b/solution.py
@@ -479,8 +479,9 @@
         for i in range(2):
             h = 2 * j + i
             w = jnp.where(top, wt[b, pl.ds(h, 1), :], wt[b, pl.ds(64 + h, 1), :])
-            got.append(mm((bkt[b] * w).astype(BF16), xc[blk, :]))
-        loc.append(jnp.where(lane < 64, got[0], got[1]))
+            got.append((bkt[b] * w).astype(BF16))
+        got = mm(jnp.concatenate(got, axis=0), xc[blk, :])
+        loc.append(jnp.where(lane < 64, got[0:BLOCK, :], got[BLOCK:, :]))
     state = jnp.zeros((64, 128), F32)
     s_o[0, 0, 0:64, :] = state.astype(BF16)
     for b in range(nb):
@@ -522,8 +523,9 @@
             mix = jnp.exp(jnp.minimum(diff, 60.0)) * g[b]
             ct = ce[blk, :] * jnp.exp(jnp.where(first, cf, cb))
             lhs = jnp.concatenate([mix.astype(BF16), ct.astype(BF16)], axis=1)
-            got.append(mm(lhs, rhs))
-        y = jnp.where(first, got[0], got[1]) + skip[0:1, :] * xb.astype(F32)
+            got.append(lhs)
+        got = mm(jnp.concatenate(got, axis=0), rhs)
+        y = jnp.where(first, got[0:BLOCK, :], got[BLOCK:, :]) + skip[0:1, :] * xb.astype(F32)
         y_o[blk, :] = y.astype(BF16)
 
 
@@ -605,8 +607,9 @@
         for i in range(2):
             h = 2 * j + i
             e = jnp.where(top, et[b, pl.ds(h, 1), :], et[b, pl.ds(64 + h, 1), :])
-            got.append(mm((cet[b] * e).astype(BF16), gy))
-        loc.append(jnp.where(lane < 64, got[0], got[1]))
+            got.append((cet[b] * e).astype(BF16))
+        got = mm(jnp.concatenate(got, axis=0), gy)
+        loc.append(jnp.where(lane < 64, got[0:BLOCK, :], got[BLOCK:, :]))
     state = jnp.zeros((64, 128), F32)
     gs_o[0, nb, 0:64, :] = state.astype(BF16)
     for b in range(nb - 1, -1, -1):
@@ -666,8 +669,11 @@
         gskip = gskip + jnp.sum(gyf * xb.astype(F32), axis=0, keepdims=True)
         rhs = jnp.concatenate([gy, gst_s[b + 1, 0:64, :], gst_s[b, 64:128, :]], axis=0)
         left = jnp.concatenate([xb, st_ref[0, b, 0:64, :], st_ref[0, b + 1, 64:128, :]], axis=0)
-        lane2 = iota((2 * BLOCK, 128), 1)
+        first2 = iota((2 * BLOCK, 128), 1) < 64
+        none = jnp.zeros_like(left)
+        big2 = nt(jnp.concatenate([jnp.where(first2, left, none), jnp.where(first2, none, left)], axis=0), rhs)
         got = []
+        sum_ge, sum_gct, sum_gb = [], [], []
         for i in range(2):
             h = 2 * j + i
             mine = pltpu.roll(rows_ref[blk, :], 128 - h, 1)
@@ -678,34 +684,37 @@
             mt = et_m * gt[b]
             endf = dpt[pl.ds(h, 1), :][:, 48 + b : 49 + b]
             endb = dpt[pl.ds(64 + h, 1), :][:, 48 + b : 49 + b]
-            w = jnp.exp(jnp.minimum(jnp.where(first, cf + endf, cb + endb), 60.0))
+            w = jnp.exp(jnp.minimum(jnp.where(first, cf, cb) + jnp.where(first[0:1, :], endf, endb), 60.0))
             bt = bk[blk, :] * w
-            lhs_b = jnp.where((lane2 < 64) == (i == 0), left, jnp.zeros_like(left))
-            big = nt(lhs_b, rhs)
+            big = big2[2 * BLOCK * i : 2 * BLOCK * (i + 1), :]
             gmt = big[0:BLOCK, 0:BLOCK]
             gbt = big[0:BLOCK, BLOCK:]
             gctt = big[BLOCK:, 0:BLOCK]
             ge = gmt * et_m
-            ggt_o[b] += ge
+            sum_ge.append(ge)
             q = gmt * mt
             qf = jnp.where(later, q, 0.0)
-            qb = q - qf
             e = jnp.where(top, et[b, pl.ds(h, 1), :], et[b, pl.ds(64 + h, 1), :])
             gce = gctt * e
-            gct_o[b] += gce
+            sum_gct.append(gce)
             ct = gce * cet[b]
-            r_o[b, pl.ds(h, 1), :] = jnp.sum(qf, axis=0, keepdims=True) + jnp.sum(ct[0:64, :], axis=0, keepdims=True)
-            r_o[b, pl.ds(64 + h, 1), :] = jnp.sum(qb, axis=0, keepdims=True) + jnp.sum(
-                ct[64:128, :], axis=0, keepdims=True
-            )
-            gb_o[b] += gbt * w
-            u = gbt * bt
+            rf = jnp.sum(qf, axis=0, keepdims=True)
+            rall = jnp.sum(q, axis=0, keepdims=True)
+            r_o[b, pl.ds(h, 1), :] = rf + jnp.sum(ct[0:64, :], axis=0, keepdims=True)
+            r_o[b, pl.ds(64 + h, 1), :] = rall - rf + jnp.sum(ct[64:128, :], axis=0, keepdims=True)
+            gbw = gbt * w
+            sum_gb.append(gbw)
+            u = gbw * bk[blk, :]
             kf = jnp.sum(qf + jnp.where(first, u, 0.0), axis=1, keepdims=True)
-            kb = jnp.sum(qb + jnp.where(first, 0.0, u), axis=1, keepdims=True)
+            kb = jnp.sum(q + u, axis=1, keepdims=True) - kf
             k_o[blk, :] += jnp.where(lane == h, kf, jnp.where(lane == 64 + h, kb, 0.0))
             lhs = jnp.concatenate([mt.astype(BF16), bt.astype(BF16)], axis=1)
-            got.append(mm(lhs, rhs))
-        gx = jnp.where(first, got[0], got[1]) + skip[0:1, :] * gyf
+            got.append(lhs)
+        ggt_o[b] += sum_ge[0] + sum_ge[1]
+        gct_o[b] += sum_gct[0] + sum_gct[1]
+        gb_o[b] += sum_gb[0] + sum_gb[1]
+        got = mm(jnp.concatenate(got, axis=0), rhs)
+        gx = jnp.where(first, got[0:BLOCK, :], got[BLOCK:, :]) + skip[0:1, :] * gyf
         gmix_o[blk, :] = (gx * ds_ref[blk, :].astype(F32)).astype(BF16)
     gskip_o[...] = jnp.broadcast_to(gskip, (8, 128))
 
@@ -782,8 +791,8 @@
 
 
 def back_kernel(
-    length, steps, info, gmix, edge, vm, wv_a, wg_a, wv_b, wg_b, ggate, normed, taps, gmb, edge_bc, bcm, taps_bc, gv, wdt, wbc, x_ref, g_ref, rs, pre,
-    keep_o, send_o, gtaps_o, keepbc_o, sendbc_o, gtapsbc_o, gin_o, gpre_o, acc_s, ext_s, vm_s, seg_s,
+    length, steps, info, gmix, edge, vm, wv_a, wg_a, wv_b, wg_b, ggate, normed, taps, gmb, edge_bc, bcm, taps_bc, gv, wdt, wbc, x_ref, g_ref, rs, pre, ggain, gskip, small,
+    keep_o, send_o, tiny_o, gin_o, acc_s, ext_s, vm_s, seg_s,
 ):
     j = pl.program_id(0)
     ext = length + 2 * HALO
@@ -798,26 +807,30 @@
     seg0 = seg_s[own, :]
     live = iota((length, 128), 0) + off < count
 
-    def back_conv(grad, data, tap, gtap):
+    def back_conv(grad, data, tap):
         total = grad[own, :] * tap[3:4, :]
         mine = grad[own, :]
-        gtap[3:4, :] = jnp.sum(mine * data[own, :], axis=0, keepdims=True)
+        gtap = [None] * 7
+        gtap[3] = jnp.sum(mine * data[own, :], axis=0, keepdims=True)
         for k in (0, 1, 2, 4, 5, 6):
             lo = HALO + 3 - k
             same = seg_s[lo : lo + length, :] == seg0
             total = total + jnp.where(same, grad[lo : lo + length, :], 0.0) * tap[k : k + 1, :]
             up = HALO + k - 3
             same = seg_s[up : up + length, :] == seg0
-            gtap[k : k + 1, :] = jnp.sum(
+            gtap[k] = jnp.sum(
                 jnp.where(same, data[up : up + length, :], 0.0) * mine, axis=0, keepdims=True
             )
-        gtap[7:8, :] = jnp.zeros((1, 128), F32)
-        return jnp.where(live, total, 0.0)
+        return jnp.where(live, total, 0.0), gtap
 
     @pl.when(j == 0)
     def _():
         no = normed[own, :]
         both = []
+        tiny_o[...] = jnp.zeros_like(tiny_o)
+        for half in range(2):
+            tiny_o[half, 10:11, 0:128] = small[8 * half : 8 * half + 1, :]
+            tiny_o[half, 10:11, 128:256] = small[8 * half + 1 : 8 * half + 2, :]
         for k in range(2):
             cols = slice(k * 128, (k + 1) * 128)
             ext_s[...] = gmb[:, cols]
@@ -827,13 +840,18 @@
             ext_s[lo : lo + HALO, :] += jnp.where(info[7] == 1, got, 0.0)
             ext_s[hi : hi + HALO, :] += jnp.where(info[7] == 1, 0.0, got)
             vm_s[...] = bcm[:, cols]
-            gbc = back_conv(ext_s, vm_s, taps_bc.at[:, cols], gtapsbc_o.at[:, cols])
+            gbc, gtap = back_conv(ext_s, vm_s, taps_bc.at[:, cols])
+            for t in range(7):
+                at = (t % 3) * 256 + k * 128
+                for half in range(2):
+                    tiny_o[half, 11 + t // 3 : 12 + t // 3, at : at + 128] = gtap[t]
             both.append(gbc.astype(BF16))
         gbc = jnp.concatenate(both + [gv[...]], axis=1)
         gw = tn(no, gbc)
-        by_core(gw, keepbc_o.at[0], sendbc_o.at[0])
+        ch = keep_o.shape[2] - 384
+        by_core(gw, keep_o.at[0, :, ch:], send_o.at[0, :, ch:])
         turned = pltpu.roll(gw[:, 256:], 128 - steps, 1)
-        by_core(jnp.concatenate([gw[:, 0:256], turned], axis=1), keepbc_o.at[1], sendbc_o.at[1])
+        by_core(jnp.concatenate([gw[:, 0:256], turned], axis=1), keep_o.at[1, :, ch:], send_o.at[1, :, ch:])
         acc_s[...] = nt(gbc[:, 0:256], wbc[...]) + nt(gv[...], wdt[...])
 
     ext_s[own, :] = gmix[...].astype(F32)
@@ -842,8 +860,15 @@
     ext_s[0:HALO, :] = jnp.where(right, halo, 0.0)
     ext_s[HALO + length : ext, :] = jnp.where(right, 0.0, halo)
     vm_s[...] = vm[...].astype(F32)
-    gvals = back_conv(ext_s, vm_s, taps, gtaps_o).astype(BF16)
-    by_core(tn(normed[own, :], gvals), keep_o.at[0], send_o.at[0])
+    gvals, gtap = back_conv(ext_s, vm_s, taps)
+    gvals = gvals.astype(BF16)
+    half = j // (steps // 2)
+    here = pl.ds(pl.multiple_of((j % (steps // 2)) * 128, 128), 128)
+    by_core(tn(normed[own, :], gvals), keep_o.at[half, :, here], send_o.at[half, :, here])
+    for t in range(7):
+        tiny_o[half, t : t + 1, here] = gtap[t]
+    tiny_o[half, 7:8, here] = ggain[0:1, :]
+    tiny_o[half, 8:9, here] = gskip[0:1, :]
     both = jnp.concatenate([gvals, ggate[...]], axis=1)
     mine = j < steps // 2
     weights = jnp.concatenate(
@@ -859,7 +884,80 @@
         wp = gn * pre[...]
         mean = jnp.mean(wp * x, axis=1, keepdims=True)
         gin_o[...] = g_ref[...].astype(F32) + r * wp - x * (r * r * r * mean)
-        gpre_o[...] = jnp.broadcast_to(jnp.sum(gn * x * r, axis=0, keepdims=True), gpre_o.shape)
+        gpre = jnp.sum(gn * x * r, axis=0, keepdims=True)
+        for half in range(2):
+            tiny_o[half, 9:10, 0 : gpre.shape[1]] = gpre
+
+
+def collect_kernel(
+    keep, send, tiny, out_o, tiny_o,
+    core_s, mine_s, piece_s, got_s, zsend_s, zgot_s, tcore_s, tsum_s, tgot_s, tz_s, tzgot_s,
+    core_out, core_in, plane_out, plane_in, z_out, z_in,
+):
+    w = lax.axis_index("wide")
+    n = lax.axis_index("narrow")
+    c, xx, z = w % 2, (w // 2) % 2, w // 4
+    share = out_o.shape[0]
+    core = (w + 1 - 2 * c, n)
+    over_x = (w + 2 - 4 * xx, n)
+    over_y = (w, 1 - n)
+    over_d = (w + 2 - 4 * xx, 1 - n)
+    steps = (2, 1, 3)
+    over_z = [(((z + d) % 4) * 4 + w % 4, n) for d in steps]
+    mesh_ids = pl.DeviceIdType.MESH
+    barrier = pltpu.get_barrier_semaphore()
+    for other in [core, over_x, over_y, over_d] + over_z:
+        pl.semaphore_signal(barrier, inc=1, device_id=other, device_id_type=mesh_ids)
+    pl.semaphore_wait(barrier, 7)
+
+    def copy(src, dst, out_sem, in_sem, other):
+        got = pltpu.make_async_remote_copy(
+            src_ref=src, dst_ref=dst, send_sem=out_sem, recv_sem=in_sem, device_id=other, device_id_type=mesh_ids
+        )
+        got.start()
+        return got
+
+    rows = [pl.ds(pl.multiple_of(((z + d) % 4) * (2 * share), 2 * share), 2 * share) for d in steps + (0,)]
+    first = [copy(tiny, tcore_s, core_out.at[4], core_in.at[4], core)]
+    for i in range(4):
+        first.append(copy(send.at[:, rows[i], :], core_s.at[i], core_out.at[i], core_in.at[i], core))
+    ways = (over_x, over_y, over_d)
+    first[0].wait()
+    tsum_s[...] = tiny[...] + tcore_s[...]
+    second = [[]]
+    for k, other in enumerate(ways):
+        half = 0 if k == 0 else 1
+        second[0].append(copy(tsum_s.at[half], tgot_s.at[k], plane_out.at[4, k], plane_in.at[4, k], other))
+    for i in range(4):
+        first[i + 1].wait()
+        both = keep[:, rows[i], :].astype(F32) + core_s[i].astype(F32)
+        low, high = both[:, 0:share, :], both[:, share:, :]
+        near = jnp.where(xx == 0, low, high)
+        far = jnp.where(xx == 0, high, low)
+        mine_s[i] = near[0]
+        piece_s[i, 0] = far[0].astype(BF16)
+        piece_s[i, 1] = near[1].astype(BF16)
+        piece_s[i, 2] = far[1].astype(BF16)
+        second.append(
+            [copy(piece_s.at[i, k], got_s.at[i, k], plane_out.at[i, k], plane_in.at[i, k], ways[k]) for k in range(3)]
+        )
+    for one in second[0]:
+        one.wait()
+    tsum = tsum_s[0] + tgot_s[0] + tgot_s[1] + tgot_s[2]
+    tz_s[...] = tsum
+    third = [copy(tz_s, tzgot_s.at[k], z_out.at[1, k], z_in.at[1, k], over_z[k]) for k in range(3)]
+    total = None
+    for i in range(4):
+        for one in second[i + 1]:
+            one.wait()
+        total = mine_s[i] + got_s[i, 0].astype(F32) + got_s[i, 1].astype(F32) + got_s[i, 2].astype(F32)
+        if i < 3:
+            zsend_s[i] = total.astype(BF16)
+            third.append(copy(zsend_s.at[i], zgot_s.at[i], z_out.at[0, i], z_in.at[0, i], over_z[i]))
+    for one in third:
+        one.wait()
+    out_o[...] = total + zgot_s[0].astype(F32) + zgot_s[1].astype(F32) + zgot_s[2].astype(F32)
+    tiny_o[...] = tsum + tzgot_s[0] + tzgot_s[1] + tzgot_s[2]
 
 
 def whole(shape, grid):
@@ -1164,23 +1262,21 @@
     lo = HALO // 2
     edge_bc = swap(jnp.where(left, gmb[length + lo : length + lo + HALO], gmb[lo : lo + HALO]))
 
-    keep_b, send_b, gtaps, keep_bc, send_bc, gtaps_bc, grad_in, gpre = pl.pallas_call(
+    keep_b, send_b, tiny, grad_in = pl.pallas_call(
         functools.partial(back_kernel, length, pairs),
         grid=(pairs,),
         out_shape=[
-            sds((2, dm // 2, ch), BF16), sds((2, dm // 2, ch), BF16), sds((8, chans), F32), sds((2, dm // 2, 384), BF16),
-            sds((2, dm // 2, 384), BF16), sds((8, 256), F32), sds((length, dm), F32), sds((8, dm), F32),
+            sds((2, dm // 2, ch + 384), BF16), sds((2, dm // 2, ch + 384), BF16), sds((2, 16, ch), F32), sds((length, dm), F32),
         ],
         in_specs=[
             SMEM, columns(length), pl.BlockSpec((HALO, 128), lambda j: (0, (j + hp) % pairs)), columns(ext), own_spec, own_spec,
             other_spec, other_spec, columns(length), whole((ext, dm), 1), columns(8), whole((ext, 256), 1),
             whole((HALO, 256), 1), whole((ext, 256), 1), whole((7, 256), 1), whole(pos, 1), whole((dm, 128), 1),
             whole((dm, 256), 1), whole((length, dm), 1), whole((length, dm), 1), whole((length, 1), 1), whole((1, dm), 1),
+            columns(8), columns(8), whole((16, 128), 1),
         ],
         out_specs=[
-            pl.BlockSpec((1, dm // 2, 128), lambda j: (j // hp, 0, j % hp)),
-            pl.BlockSpec((1, dm // 2, 128), lambda j: (j // hp, 0, j % hp)), columns(8), whole((2, dm // 2, 384), 1),
-            whole((2, dm // 2, 384), 1), whole((8, 256), 1), whole((length, dm), 1), whole((8, dm), 1),
+            whole((2, dm // 2, ch + 384), 1), whole((2, dm // 2, ch + 384), 1), whole((2, 16, ch), 1), whole((length, dm), 1),
         ],
         scratch_shapes=[
             pltpu.VMEM((length, dm), F32), pltpu.VMEM((ext, 128), F32), pltpu.VMEM((ext, 128), F32),
@@ -1191,23 +1287,39 @@
         name="back",
     )(
         info, gmix, edge_x, vm, wv, wg, wv_other, wg_other, ggate, normed, taps, gmb, edge_bc, bcm, taps_bc, gv, wdt_all, wbc,
-        x, g, rs, pre_gain.reshape(1, dm),
+        x, g, rs, pre_gain.reshape(1, dm), ggain, gskip, small,
     )
 
     keep_b, send_b, wa = lax.optimization_barrier((keep_b, send_b, wa))
 
-    keep_bb = jnp.concatenate([keep_b, keep_bc], axis=2)
-    send_bb = jnp.concatenate([send_b, send_bc], axis=2)
-    wb = depth(plane(*meet(keep_bb, flip(send_bb, 1, wide))))
-
-    small = jnp.pad(small, ((0, 0), (0, ch - 128)))
-    common = jnp.concatenate([gpre, jnp.pad(gtaps_bc, ((0, 0), (0, dm - 256)))], axis=0)
-    own_rows = jnp.concatenate([gtaps[:, :ch], ggain[:, :ch], gskip[:, :ch], small[:8], common], axis=0)
-    far_rows = jnp.concatenate([gtaps[:, ch:], ggain[:, ch:], gskip[:, ch:], small[8:], common], axis=0)
-    tiny = jnp.stack([own_rows, far_rows])
-    tiny = tiny + flip(tiny, 1, wide)
-    tiny = plane(tiny[0], tiny[0], tiny[1], tiny[1])
-    tiny = total(tiny, *[flip(tiny, 4 * k, wide) for k in (1, 2, 3)])
+    cols = ch + 384
+    wb, tiny = pl.pallas_call(
+        collect_kernel,
+        out_shape=[sds((share, cols), F32), sds((16, ch), F32)],
+        in_specs=[VMEM] * 3,
+        out_specs=[VMEM] * 2,
+        scratch_shapes=[
+            pltpu.VMEM((4, 2, 2 * share, cols), BF16),
+            pltpu.VMEM((4, share, cols), F32),
+            pltpu.VMEM((4, 3, share, cols), BF16),
+            pltpu.VMEM((4, 3, share, cols), BF16),
+            pltpu.VMEM((3, share, cols), BF16),
+            pltpu.VMEM((3, share, cols), BF16),
+            pltpu.VMEM((2, 16, ch), F32),
+            pltpu.VMEM((2, 16, ch), F32),
+            pltpu.VMEM((3, 16, ch), F32),
+            pltpu.VMEM((16, ch), F32),
+            pltpu.VMEM((3, 16, ch), F32),
+            pltpu.SemaphoreType.DMA((5,)),
+            pltpu.SemaphoreType.DMA((5,)),
+            pltpu.SemaphoreType.DMA((5, 3)),
+            pltpu.SemaphoreType.DMA((5, 3)),
+            pltpu.SemaphoreType.DMA((2, 3)),
+            pltpu.SemaphoreType.DMA((2, 3)),
+        ],
+        compiler_params=pltpu.CompilerParams(collective_id=0, has_side_effects=True, vmem_limit_bytes=VMEM_LIMIT),
+        name="collect",
+    )(keep_b, send_b, tiny)
 
     def part(v, dim):
         size = v.shape[dim] // wide
@@ -1220,18 +1332,19 @@
     dt_part = jnp.stack([dt_cols[:, 0:hl], dt_cols[:, 64 : 64 + hl]], axis=2)
     g_w_heads = jnp.concatenate([gate_part, vals_part, dt_part], axis=2)
     g_w_out = jnp.transpose(wa[:, :dm].reshape(share, hl, HD), (1, 2, 0))
+    taps_rows = tiny[11:14].reshape(3, 3, 256).reshape(9, 256)[:7]
     return (
         out[None],
         grad_in[None],
-        part(tiny[32], 0),
+        part(tiny[9], 0),
         g_w_heads,
         bc_part,
         part(tiny[0:7].reshape(7, hl, HD), 2),
-        part(pack_columns(tiny[40:47, :256]), 1),
-        jnp.stack([tiny[24, 0:hl], tiny[24, 64 : 64 + hl]], axis=1),
-        tiny[25, 0:hl] + tiny[25, 64 : 64 + hl],
-        jnp.sum(tiny[16].reshape(hl, HD), axis=1),
-        part(tiny[8].reshape(hl, HD), 1),
+        part(pack_columns(taps_rows), 1),
+        jnp.stack([tiny[10, 0:hl], tiny[10, 64 : 64 + hl]], axis=1),
+        tiny[10, 128 : 128 + hl] + tiny[10, 192 : 192 + hl],
+        jnp.sum(tiny[8].reshape(hl, HD), axis=1),
+        part(tiny[7].reshape(hl, HD), 1),
         g_w_out,
     )
 

time: 285 us -> 247 us (0.87)
  waiting for transfers between devices: 39.2 us -> 8.06 us
  Pallas kernels: 149 us -> 178 us
  starting transfers between devices: 42.8 us -> 24.2 us
  local copies, waits for them, and re-layouts: 37.5 us -> 24.9 us
  other arithmetic: 13.5 us -> 9.53 us
    pallas_call x0 -> x1, Pallas kernels: none -> 31.8 us  [split_positions(): pl.pallas_call(collect_kernel, out_shape=[sds((share, cols), F32), sds((1...]
    ppermute x21 -> x11, waiting for transfers between devices: 26.3 us -> 1.54 us  [flip(): return lax.ppermute(v, 'wide', [(i, i ^ bit) for i in range(wide)])]
    ppermute x21 -> x11, starting transfers between devices: 22.7 us -> 9.06 us  [flip(): return lax.ppermute(v, 'wide', [(i, i ^ bit) for i in range(wide)])]
    ppermute x12 -> x10, waiting for transfers between devices: 11.6 us -> 6.52 us  [swap(): return lax.ppermute(v, 'narrow', [(0, 1), (1, 0)])]
    unnamed x62 -> x38, local copies, waits for them, and re-layouts: 14.3 us -> 9.51 us
    ppermute x12 -> x10, starting transfers between devices: 15.8 us -> 12.6 us  [swap(): return lax.ppermute(v, 'narrow', [(0, 1), (1, 0)])]
  transfers between devices with their start and end apart: 36 -> 22, of which waited for: 9 -> 3; matrix products, arithmetic and copies ran while one was open for 13% -> 4% of each run, Pallas kernels for 42% -> 47%
where the time goes in v2:
time: 247 us; the launch traced here: 245 us
  Pallas kernels  178 us (72%)
  local copies, waits for them, and re-layouts  24.9 us (10%)
  starting transfers between devices  24.2 us (10%)
  other arithmetic  9.53 us (4%)
  waiting for transfers between devices  8.06 us (3%)
    pallas_call x1, Pallas kernels, split_positions(): pl.pallas_call(functools.partial(gscan_kernel, length), grid=(pairs,), ou...  33 us
    pallas_call x1, Pallas kernels, split_positions(): pl.pallas_call(collect_kernel, out_shape=[sds((share, cols), F32), sds((1...  31.8 us
    pallas_call x1, Pallas kernels, split_positions(): pl.pallas_call(functools.partial(back_kernel, length, pairs), grid=(pairs...  25 us
    pallas_call x1, Pallas kernels, split_positions(): pl.pallas_call(functools.partial(gate_kernel, nb), grid=(nb,), out_shape=...  24 us
    pallas_call x1, Pallas kernels, split_positions(): pl.pallas_call(functools.partial(scan_kernel, length), grid=(pairs,), out...  19.4 us
    pallas_call x2, Pallas kernels, vals(): pl.pallas_call(functools.partial(vals_kernel, length, other), grid=(hp,),...  18.4 us
    ppermute x10, starting transfers between devices, swap(): return lax.ppermute(v, 'narrow', [(0, 1), (1, 0)])  12.6 us
    unnamed x38, local copies, waits for them, and re-layouts  9.51 us
  transfers between devices with their start and end apart: 22, of which 3 were waited for; matrix products, arithmetic and copies ran while one was open for 4% of the time, Pallas kernels for 47%

profile of v2, /device:TPU:0, one launch (start us, length us, event | category | flops | bytes accessed | tf_op | source)
XLA Modules:
  0.0 245.4 jit_solution(1644645966418972658)
XLA Ops:
  0.7 1.8 fusion.11
  2.5 0.6 copy.51.refs_0_.wv_a
  3.1 0.8 constant_dynamic-slice_fusion.3
  3.9 3.0 %collective-permute-start.3 = (bf16[192,768]{1,0:T(8,128)(2,1)}, bf16[192,768]{1,0:T(8,128)(2,1)}, u32[]{:S(2)}, u32[]{:S(2)}) collective-permute-start(bf16[192,768]{1,0:T(8,128)(2,1)} %constant_dynamic-slice_fusion.3), channel_id=1, source_target_pairs={{0,1},{1,0},{2,3},{3,2},{4,5},{5,4},{6,7},{7,6},{8,9},{9,8},{10,11... | collective-permute-start | bytes 884744 | tf_op jit(solution)/shard_map/ppermute | solution.py:1019
  6.9 1.4 select_bitcast_fusion
  8.3 0.9 slice.130
  9.2 0.8 copy.50.wdt_a
  10.1 2.0 collective-permute-start.1
  12.1 1.4 copy.48.conv
  13.5 0.7 copy.49.dtb
  14.2 1.7 small.1.small_a
  15.9 0.6 copy.54.wg_a
  16.5 1.2 fusion.4
  17.8 2.1 collective-permute-start.8
  19.9 0.6 reshape.86.gain.pre
  20.5 1.5 collective-permute-start.4
  22.0 8.7 %front.1 = (s32[8]{0:T(128)}, f32[8,1536]{1,0:T(8,128)}, f32[8,1536]{1,0:T(8,128)}, f32[8,1536]{1,0:T(8,128)}, bf16[768,128]{1,0:T(8,128)(2,1)}, /*index=5*/bf16...) custom-call(s32[1,4]{1,0:T(1,128)} %starts.1, ...), custom_call_target="tpu_custom_call" | custom-call | flops 8800000000 | bytes 8000000 | tf_op jit(solution)/shard_map/front/pallas_call | solution.py:1100
  30.8 0.5 collective-permute-start.6
  31.3 8.7 %vals_own.1 = (bf16[640,1536]{1,0:T(8,128)(2,1)}, bf16[672,1536]{1,0:T(8,128)(2,1)}, bf16[640,1536]{1,0:T(8,128)(2,1)}, bf16[12,6,128,128]{3,2,1,0:T(8,128)(2,1)}, bf16[12,64,128]{2,1,0:T(8,128)(2,1)}) custom-call(s32[8]{0:T(128)} %get-tuple-element.92.info, bf16[672,768]{1,0:T(8,128)(2,1)} %get-tuple-element.91.normed, bf16[768,768]{1,0:T(8,128)(2,1)} %copy-done.1, ...), custom_call_target="tpu_custom_call" | custom-call | flops 8800000000 | bytes 8000000 | tf_op jit(solution)/shard_map/vals_own/pallas_call | solution.py:1135
  40.0 1.9 collective-permute-start.9
  42.0 0.7 copy-done.9
  42.8 9.6 %vals_other.1 = (bf16[640,1536]{1,0:T(8,128)(2,1)}, bf16[672,1536]{1,0:T(8,128)(2,1)}, bf16[640,1536]{1,0:T(8,128)(2,1)}, bf16[12,6,128,128]{3,2,1,0:T(8,128)(2,...) custom-call(s32[8]{0:T(128)} %get-tuple-element.92.info, ...), custom_call_target="tpu_custom_call", output_to_operand_aliasing={{0}: (10, {}), {1}: (11, {}), {2}: (12, {}), {3}: (13, {}),... | custom-call | flops 8800000000 | bytes 8000000 | tf_op jit(solution)/shard_map/vals_other/pallas_call | solution.py:1135
  52.5 1.6 collective-permute-start.7
  54.1 1.5 collective-permute-done.9.p1
  55.6 3.8 %collective-permute-done.7.s0_ref = bf16[12,64,128]{2,1,0:T(8,128)(2,1)S(1)} collective-permute-done((bf16[12,64,128]{2,1,0:T(8,128)(2,1)}, bf16[12,64,128]{2,1,0:T(8,128)(2,1)S(1)}, u32[]{:S(2)}, u32[]{:S(2)}) %collective-permute-start.7) | collective-permute-done | bytes 196640 | tf_op jit(solution)/shard_map/ppermute | solution.py:1019
  59.4 0.7 copy-done.13
  60.0 19.4 %scan.1 = (bf16[640,1536]{1,0:T(8,128)(2,1)}, bf16[12,6,128,128]{3,2,1,0:T(8,128)(2,1)}) custom-call(s32[8]{0:T(128)} %get-tuple-element.92.info, bf16[640,1536]{1,0:T(8,128)(2,1)} %get-tuple-element.102.xc_ref, bf16[12,6,128,128]{3,2,1,0:T(8,128)(2,1)} %get-tuple-element.103.s_ref, bf16[12,64,128]{2,1,0:T(8,128)(2,1)} %copy-done.13, ...), custom_call_target="tpu_custom_call" | custom-call | flops 20899999744 | bytes 19000000 | tf_op jit(solution)/shard_map/scan/pallas_call | solution.py:1155
  79.5 0.8 copy-done.6
  80.4 24.0 %gated.1 = (bf16[640,768]{1,0:T(8,128)(2,1)}, bf16[640,1536]{1,0:T(8,128)(2,1)}, bf16[2,384,1536]{2,1,0:T(8,128)(2,1)}, bf16[2,384,1536]{2,1,0:T(8,128)(2,1)}, b...) custom-call(bf16[640,768]{1,0:T(8,128)(2,1)} %bitcast.71, bf16[640,768]{1,0:T(8,128)(2,1)} %bitcast.73, ...), custom_call_target="tpu_custom_call" | custom-call | flops 24199999488 | bytes 22000000 | tf_op jit(solution)/shard_map/gated/pallas_call | solution.py:1171
  104.6 1.8 fusion.12
  106.4 9.2 %gstate.1 = (bf16[12,6,128,128]{3,2,1,0:T(8,128)(2,1)}, bf16[12,64,128]{2,1,0:T(8,128)(2,1)}) custom-call(s32[8]{0:T(128)} %get-tuple-element.92.info, bf16[640,1536]{1,0:T(8,128)(2,1)} %get-tuple-element.114.gy_ref, f32[5,128,128]{2,1,0:T(8,128)} %get-tuple-element.116.et, f32[5,128,128]{2,1,0:T(8,128)} %get-tuple-element.117.cet, ...), custom_call_target="tpu_custom_call" | custom-call | flops 9900000256 | bytes 9000000 | tf_op jit(solution)/shard_map/gstate/pallas_call | solution.py:1213
  115.8 0.7 fusion.1
  116.7 1.5 collective-permute-start.13
  118.2 0.5 collective-permute-start.14
  119.1 2.6 %collective-permute-start.16 = (bf16[4,48,1536]{2,1,0:T(8,128)(2,1)S(1)}, bf16[4,48,1536]{2,1,0:T(8,128)(2,1)S(1)}, u32[]{:S(2)}, u32[]{:S(2)}) collective-permute-start(bf16[4,48,1536]{2,1,0:T(8,128)(2,1)S(1)} %get-tuple-element.133), channel_id=1, source_target_pairs={{0,5},{1,4},{2,7},{3,6},{4,1},{5,0},{6,3},{7,2},{8,13},{9,12},{10,... | collective-permute-start | bytes 1769480 | tf_op jit(solution)/shard_map/ppermute | solution.py:1028
  121.7 2.7 %collective-permute-done.13.gs0_ref = bf16[12,64,128]{2,1,0:T(8,128)(2,1)S(1)} collective-permute-done((bf16[12,64,128]{2,1,0:T(8,128)(2,1)S(1)}, bf16[12,64,128]{2,1,0:T(8,128)(2,1)S(1)}, u32[]{:S(2)}, u32[]{:S(2)}) %collective-permute-start.13) | collective-permute-done | bytes 196640 | tf_op jit(solution)/shard_map/ppermute | solution.py:1019
  124.4 0.7 copy-done.12
  125.1 33.0 %gscan.1 = (bf16[640,1536]{1,0:T(8,128)(2,1)}, f32[5,128,128]{2,1,0:T(8,128)}, f32[5,128,128]{2,1,0:T(8,128)}, f32[5,128,128]{2,1,0:T(8,128)}, f32[640,128]{1,0:...) custom-call(s32[8]{0:T(128)} %get-tuple-element.92.info, ...), custom_call_target="tpu_custom_call" | custom-call | flops 38499999744 | bytes 35000000 | tf_op jit(solution)/shard_map/gscan/pallas_call | solution.py:1227
  158.4 6.4 %join.1 = (f32[672,256]{1,0:T(8,128)}, bf16[640,128]{1,0:T(8,128)(2,1)}, f32[16,128]{1,0:T(8,128)}) custom-call(s32[8]{0:T(128)} %get-tuple-element.92.info, f32[5,128,128]{2,1,0:T(8,128)} %get-tuple-element.139.ggt, f32[5,128,128]{2,1,0:T(8,128)} %get-tuple-element.140.gb, f32[5,128,128]{2,1,0:T(8,128)} %get-tuple-element.141.gct, ...), custom_call_target="tpu_custom_call" | custom-call | flops 6600000000 | bytes 6000000 | tf_op jit(solution)/shard_map/join/pallas_call | solution.py:1251
  164.8 0.7 slice_select_fusion.1
  165.6 1.5 collective-permute-start.18
  167.1 0.8 slice_select_fusion
  167.9 0.5 collective-permute-start.17
  168.5 1.6 collective-permute-start.19
  170.1 2.6 %collective-permute-start.20 = (bf16[48,1536]{1,0:T(8,128)(2,1)S(1)}, bf16[48,1536]{1,0:T(8,128)(2,1)S(1)}, u32[]{:S(2)}, u32[]{:S(2)}) collective-permute-start(bf16[48,1536]{1,0:T(8,128)(2,1)S(1)} %get-tuple-element.196), channel_id=1, source_target_pairs={{0,16},{2,18},{4,20},{6,22},{8,24},{10,26},{12,28},{14,30},{16,0},... | collective-permute-start | bytes 442376 | tf_op jit(solution)/shard_map/ppermute | solution.py:1023
  173.0 0.6 copy-done.15
  173.6 25.0 %back.1 = (bf16[2,384,1152]{2,1,0:T(8,128)(2,1)}, bf16[2,384,1152]{2,1,0:T(8,128)(2,1)}, f32[2,16,768]{2,1,0:T(8,128)}, f32[640,768]{1,0:T(8,128)}) custom-call(s32[8]{0:T(128)} %get-tuple-element.92.info, bf16[640,1536]{1,0:T(8,128)(2,1)} %get-tuple-element.134.gmix, bf16[16,1536]{1,0:T(8,128)(2,1)} %copy-done.14, bf16[672,1536]{1,0:T(8,128)(2,1)} %get-tuple-element.135.vm, ...), custom_call_target="tpu_custom_call" | custom-call | flops 26400000000 | bytes 24000000 | tf_op jit(solution)/shard_map/back/pallas_call | solution.py:1265
  198.7 31.8 %collect.1 = (f32[48,1152]{1,0:T(8,128)}, f32[16,768]{1,0:T(8,128)}) custom-call(bf16[2,384,1152]{2,1,0:T(8,128)(2,1)} %get-tuple-element.164.keep, bf16[2,384,1152]{2,1,0:T(8,128)(2,1)} %get-tuple-element.165.send, f32[2,16,768]{2,1,0:T(8,128)} %get-tuple-element.166.tiny), custom_call_target="tpu_custom_call" | custom-call | tf_op jit(solution)/shard_map/collect/pallas_call | solution.py:1296
  230.4 1.3 add_bitcast_fusion
  231.8 0.7 slice.151
  232.5 0.9 fusion.15
  233.4 0.9 slice.143
  234.3 0.9 slice_bitcast_fusion.1
  235.2 0.7 slice.150
  236.0 0.8 slice_reduce_fusion
  238.4 1.2 copy.68
  239.6 0.8 copy.70
  240.6 0.7 copy.69
  241.5 0.7 copy.79
  242.2 0.6 pad_maximum_fusion.2
  242.8 0.6 reduce_sum.9
  243.4 0.6 fusion.10
  244.0 0.7 pad_maximum_fusion.1
  244.7 0.7 fusion.9
  (73 shorter events, 4.0 us)
Async XLA Ops:
  2.5 11.1 %copy-start.3 = (f32[12,2]{0,1:T(2,128)S(1)}, f32[12,2]{0,1:T(2,128)}, u32[]{:S(2)}) copy-start(f32[12,2]{0,1:T(2,128)} %param.20) | copy-start | bytes 292
  3.1 13.4 %copy-start.1 = (bf16[768,768]{1,0:T(8,128)(2,1)}, bf16[768,768]{1,0:T(8,128)(2,1)S(1)}, u32[]{:S(2)}) copy-start(bf16[768,768]{1,0:T(8,128)(2,1)S(1)} %copy.51.refs_0_.wv_a) | copy-start | bytes 3538948
  3.9 16.5 %collective-permute-start.3 = (bf16[192,768]{1,0:T(8,128)(2,1)}, bf16[192,768]{1,0:T(8,128)(2,1)}, u32[]{:S(2)}, u32[]{:S(2)}) collective-permute-start(bf16[192,768]{1,0:T(8,128)(2,1)} %constant_dynamic-slice_fusion.3), channel_id=1, source_target_pairs={{0,1},{1,0},{2,3},{3,2},{4,5},{5,4},{6,7},{7,6},{8,9},{9,8},{10,11... | collective-permute-start | bytes 884744 | tf_op jit(solution)/shard_map/ppermute | solution.py:1019
  8.3 13.7 %collective-permute-start = (bf16[16,768]{1,0:T(8,128)(2,1)}, bf16[16,768]{1,0:T(8,128)(2,1)}, u32[]{:S(2)}, u32[]{:S(2)}) collective-permute-start(bf16[16,768]{1,0:T(8,128)(2,1)} %select_bitcast_fusion), channel_id=1, source_target_pairs={{0,1},{1,0},{2,3},{3,2},{4,5},{5,4},{6,7},{7,6},{8,9},{9,8},{10,11... | collective-permute-start | bytes 73736 | tf_op jit(solution)/shard_map/ppermute | solution.py:1019
  10.1 11.9 %collective-permute-start.1 = (bf16[768,24]{1,0:T(8,128)(2,1)}, bf16[768,24]{1,0:T(8,128)(2,1)}, u32[]{:S(2)}, u32[]{:S(2)}) collective-permute-start(bf16[768,24]{1,0:T(8,128)(2,1)} %copy.50.wdt_a), channel_id=1, source_target_pairs={{0,1},{1,0},{2,3},{3,2},{4,5},{5,4},{6,7},{7,6},{8,9},{9,8},{10,11... | collective-permute-start | bytes 110600 | tf_op jit(solution)/shard_map/ppermute | solution.py:1019
  15.9 6.1 %collective-permute-start.2 = (f32[32,768]{1,0:T(8,128)}, f32[32,768]{1,0:T(8,128)}, u32[]{:S(2)}, u32[]{:S(2)}) collective-permute-start(f32[32,768]{1,0:T(8,128)} %small.1.small_a), channel_id=1, source_target_pairs={{0,1},{1,0},{2,3},{3,2},{4,5},{5,4},{6,7},{7,6},{8,9},{9,8},{10,11... | collective-permute-start | bytes 294920 | tf_op jit(solution)/shard_map/ppermute | solution.py:1019
  16.5 1.3 copy-start
  16.5 3.4 %copy-start.2 = (f32[768]{0:T(1024)S(1)}, f32[768]{0:T(1024)}, u32[]{:S(2)}) copy-start(f32[768]{0:T(1024)} %param.15) | copy-start | bytes 9220
  17.8 22.2 %collective-permute-start.8 = (bf16[192,1536]{1,0:T(8,128)(2,1)S(1)}, bf16[192,1536]{1,0:T(8,128)(2,1)S(1)}, u32[]{:S(2)}, u32[]{:S(2)}) collective-permute-start(bf16[192,1536]{1,0:T(8,128)(2,1)S(1)} %fusion.4), channel_id=1, source_target_pairs={{0,1},{1,0},{2,3},{3,2},{4,5},{5,4},{6,7},{7,6},{8,9},{9,8},{10,11... | collective-permute-start | bytes 1769480 | tf_op jit(solution)/shard_map/ppermute | solution.py:1019
  20.5 10.3 %collective-permute-start.4 = (bf16[192,768]{1,0:T(8,128)(2,1)}, bf16[192,768]{1,0:T(8,128)(2,1)S(1)}, u32[]{:S(2)}, u32[]{:S(2)}) collective-permute-start(bf16[192,768]{1,0:T(8,128)(2,1)} %collective-permute-done.3.refs_0_), channel_id=1, source_target_pairs={{0,4},{2,6},{4,0},{6,2},{8,12},{10,14},{12,8},{14,10},{16,20},{18,... | collective-permute-start | bytes 884744 | tf_op jit(solution)/shard_map/ppermute | solution.py:1023
  30.7 11.3 %collective-permute-start.5 = (bf16[192,768]{1,0:T(8,128)(2,1)}, bf16[192,768]{1,0:T(8,128)(2,1)S(1)}, u32[]{:S(2)}, u32[]{:S(2)}) collective-permute-start(bf16[192,768]{1,0:T(8,128)(2,1)} %collective-permute-done.3.refs_0_), channel_id=1, source_target_pairs={{0,2},{2,0},{4,6},{6,4},{8,10},{10,8},{12,14},{14,12},{16,18},{18,... | collective-permute-start | bytes 884744 | tf_op jit(solution)/shard_map/ppermute | solution.py:1023
  30.8 9.2 %copy-start.8 = (bf16[192,768]{1,0:T(8,128)(2,1)}, bf16[192,768]{1,0:T(8,128)(2,1)S(1)}, u32[]{:S(2)}) copy-start(bf16[192,768]{1,0:T(8,128)(2,1)S(1)} %collective-permute-done.4.refs_1_) | copy-start | bytes 884740
  30.8 11.2 %collective-permute-start.6 = (bf16[192,768]{1,0:T(8,128)(2,1)S(1)}, bf16[192,768]{1,0:T(8,128)(2,1)S(1)}, u32[]{:S(2)}, u32[]{:S(2)}) collective-permute-start(bf16[192,768]{1,0:T(8,128)(2,1)S(1)} %collective-permute-done.4.refs_1_), channel_id=1, source_target_pairs={{0,2},{2,0},{4,6},{6,4},{8,10},{10,8},{12,14},{14,12},{16,18},{18,... | collective-permute-start | bytes 884744 | tf_op jit(solution)/shard_map/ppermute | solution.py:1023
  40.0 14.0 %copy-start.4 = (bf16[192,1536]{1,0:T(8,128)(2,1)}, bf16[192,1536]{1,0:T(8,128)(2,1)S(1)}, u32[]{:S(2)}) copy-start(bf16[192,1536]{1,0:T(8,128)(2,1)S(1)} %collective-permute-done.8.p0) | copy-start | bytes 1769476
  40.0 15.6 %collective-permute-start.9 = (bf16[192,1536]{1,0:T(8,128)(2,1)S(1)}, bf16[192,1536]{1,0:T(8,128)(2,1)S(1)}, u32[]{:S(2)}, u32[]{:S(2)}) collective-permute-start(bf16[192,1536]{1,0:T(8,128)(2,1)S(1)} %collective-permute-done.8.p0), channel_id=1, source_target_pairs={{0,4},{2,6},{4,0},{6,2},{8,12},{10,14},{12,8},{14,10},{16,20},{18,... | collective-permute-start | bytes 1769480 | tf_op jit(solution)/shard_map/ppermute | solution.py:1023
  42.0 0.7 copy-start.9
  42.0 0.8 copy-start.10
  52.5 6.9 %collective-permute-start.7 = (bf16[12,64,128]{2,1,0:T(8,128)(2,1)}, bf16[12,64,128]{2,1,0:T(8,128)(2,1)S(1)}, u32[]{:S(2)}, u32[]{:S(2)}) collective-permute-start(bf16[12,64,128]{2,1,0:T(8,128)(2,1)} %get-tuple-element.104), channel_id=1, source_target_pairs={{0,1},{1,0},{2,3},{3,2},{4,5},{5,4},{6,7},{7,6},{8,9},{9,8},{10,11... | collective-permute-start | bytes 589832 | tf_op jit(solution)/shard_map/ppermute | solution.py:1019
  54.0 25.4 %collective-permute-start.10 = (bf16[192,1536]{1,0:T(8,128)(2,1)S(1)}, bf16[192,1536]{1,0:T(8,128)(2,1)S(1)}, u32[]{:S(2)}, u32[]{:S(2)}) collective-permute-start(bf16[192,1536]{1,0:T(8,128)(2,1)S(1)} %collective-permute-done.8.p0), channel_id=1, source_target_pairs={{0,2},{2,0},{4,6},{6,4},{8,10},{10,8},{12,14},{14,12},{16,18},{18,... | collective-permute-start | bytes 1769480 | tf_op jit(solution)/shard_map/ppermute | solution.py:1023
  55.6 23.9 %copy-start.5 = (bf16[192,1536]{1,0:T(8,128)(2,1)}, bf16[192,1536]{1,0:T(8,128)(2,1)S(1)}, u32[]{:S(2)}) copy-start(bf16[192,1536]{1,0:T(8,128)(2,1)S(1)} %collective-permute-done.9.p1) | copy-start | bytes 1769476
  55.6 23.9 %collective-permute-start.11 = (bf16[192,1536]{1,0:T(8,128)(2,1)S(1)}, bf16[192,1536]{1,0:T(8,128)(2,1)S(1)}, u32[]{:S(2)}, u32[]{:S(2)}) collective-permute-start(bf16[192,1536]{1,0:T(8,128)(2,1)S(1)} %collective-permute-done.9.p1), channel_id=1, source_target_pairs={{0,2},{2,0},{4,6},{6,4},{8,10},{10,8},{12,14},{14,12},{16,18},{18,... | collective-permute-start | bytes 1769480 | tf_op jit(solution)/shard_map/ppermute | solution.py:1023
  59.4 0.7 copy-start.13
  79.4 0.8 copy-start.6
  79.5 1.0 copy-start.7
  104.5 11.1 %collective-permute-start.12 = (bf16[2,384,1536]{2,1,0:T(8,128)(2,1)}, bf16[2,384,1536]{2,1,0:T(8,128)(2,1)S(1)}, u32[]{:S(2)}, u32[]{:S(2)}) collective-permute-start(bf16[2,384,1536]{2,1,0:T(8,128)(2,1)} %get-tuple-element.121), channel_id=1, source_target_pairs={{0,2},{2,0},{4,6},{6,4},{8,10},{10,8},{12,14},{14,12},{16,18},{18,... | collective-permute-start | bytes 7077896 | tf_op jit(solution)/shard_map/ppermute | solution.py:1023
  115.7 0.9 copy-start.11
  116.7 7.7 %collective-permute-start.13 = (bf16[12,64,128]{2,1,0:T(8,128)(2,1)S(1)}, bf16[12,64,128]{2,1,0:T(8,128)(2,1)S(1)}, u32[]{:S(2)}, u32[]{:S(2)}) collective-permute-start(bf16[12,64,128]{2,1,0:T(8,128)(2,1)S(1)} %copy-done.11), channel_id=1, source_target_pairs={{0,1},{1,0},{2,3},{3,2},{4,5},{5,4},{6,7},{7,6},{8,9},{9,8},{10,11... | collective-permute-start | bytes 589832 | tf_op jit(solution)/shard_map/ppermute | solution.py:1019
  118.2 39.9 %collective-permute-start.14 = (bf16[4,48,1536]{2,1,0:T(8,128)(2,1)S(1)}, bf16[4,48,1536]{2,1,0:T(8,128)(2,1)S(1)}, u32[]{:S(2)}, u32[]{:S(2)}) collective-permute-start(bf16[4,48,1536]{2,1,0:T(8,128)(2,1)S(1)} %get-tuple-element.131), channel_id=1, source_target_pairs={{0,4},{2,6},{4,0},{6,2},{8,12},{10,14},{12,8},{14,10},{16,20},{18,... | collective-permute-start | bytes 1769480 | tf_op jit(solution)/shard_map/ppermute | solution.py:1023
  118.7 39.4 %collective-permute-start.15 = (bf16[4,48,1536]{2,1,0:T(8,128)(2,1)S(1)}, bf16[4,48,1536]{2,1,0:T(8,128)(2,1)S(1)}, u32[]{:S(2)}, u32[]{:S(2)}) collective-permute-start(bf16[4,48,1536]{2,1,0:T(8,128)(2,1)S(1)} %get-tuple-element.132), channel_id=1, source_target_pairs={{0,1},{1,0},{2,3},{3,2},{4,5},{5,4},{6,7},{7,6},{8,9},{9,8},{10,11... | collective-permute-start | bytes 1769480 | tf_op jit(solution)/shard_map/ppermute | solution.py:1019
  119.1 39.0 %collective-permute-start.16 = (bf16[4,48,1536]{2,1,0:T(8,128)(2,1)S(1)}, bf16[4,48,1536]{2,1,0:T(8,128)(2,1)S(1)}, u32[]{:S(2)}, u32[]{:S(2)}) collective-permute-start(bf16[4,48,1536]{2,1,0:T(8,128)(2,1)S(1)} %get-tuple-element.133), channel_id=1, source_target_pairs={{0,5},{1,4},{2,7},{3,6},{4,1},{5,0},{6,3},{7,2},{8,13},{9,12},{10,... | collective-permute-start | bytes 1769480 | tf_op jit(solution)/shard_map/ppermute | solution.py:1028
  124.4 0.7 copy-start.12
  165.6 7.3 %collective-permute-start.18 = (f32[16,256]{1,0:T(8,128)S(1)}, f32[16,256]{1,0:T(8,128)S(1)}, u32[]{:S(2)}, u32[]{:S(2)}) collective-permute-start(f32[16,256]{1,0:T(8,128)S(1)} %slice_select_fusion.1), channel_id=1, source_target_pairs={{0,1},{1,0},{2,3},{3,2},{4,5},{5,4},{6,7},{7,6},{8,9},{9,8},{10,11... | collective-permute-start | bytes 49160 | tf_op jit(solution)/shard_map/ppermute | solution.py:1019
  167.9 5.0 %collective-permute-start.17 = (bf16[16,1536]{1,0:T(8,128)(2,1)S(1)}, bf16[16,1536]{1,0:T(8,128)(2,1)S(1)}, u32[]{:S(2)}, u32[]{:S(2)}) collective-permute-start(bf16[16,1536]{1,0:T(8,128)(2,1)S(1)} %slice_select_fusion), channel_id=1, source_target_pairs={{0,1},{1,0},{2,3},{3,2},{4,5},{5,4},{6,7},{7,6},{8,9},{9,8},{10,11... | collective-permute-start | bytes 147464 | tf_op jit(solution)/shard_map/ppermute | solution.py:1019
  168.5 30.1 %collective-permute-start.19 = (bf16[48,1536]{1,0:T(8,128)(2,1)S(1)}, bf16[48,1536]{1,0:T(8,128)(2,1)S(1)}, u32[]{:S(2)}, u32[]{:S(2)}) collective-permute-start(bf16[48,1536]{1,0:T(8,128)(2,1)S(1)} %get-tuple-element.194), channel_id=1, source_target_pairs={{0,8},{2,10},{4,12},{6,14},{8,0},{10,2},{12,4},{14,6},{16,24},{18,... | collective-permute-start | bytes 442376 | tf_op jit(solution)/shard_map/ppermute | solution.py:1023
  170.1 28.4 %collective-permute-start.20 = (bf16[48,1536]{1,0:T(8,128)(2,1)S(1)}, bf16[48,1536]{1,0:T(8,128)(2,1)S(1)}, u32[]{:S(2)}, u32[]{:S(2)}) collective-permute-start(bf16[48,1536]{1,0:T(8,128)(2,1)S(1)} %get-tuple-element.196), channel_id=1, source_target_pairs={{0,16},{2,18},{4,20},{6,22},{8,24},{10,26},{12,28},{14,30},{16,0},... | collective-permute-start | bytes 442376 | tf_op jit(solution)/shard_map/ppermute | solution.py:1023
  172.7 25.9 %collective-permute-start.21 = (bf16[48,1536]{1,0:T(8,128)(2,1)S(1)}, bf16[48,1536]{1,0:T(8,128)(2,1)S(1)}, u32[]{:S(2)}, u32[]{:S(2)}) collective-permute-start(bf16[48,1536]{1,0:T(8,128)(2,1)S(1)} %get-tuple-element.195), channel_id=1, source_target_pairs={{0,24},{2,26},{4,28},{6,30},{8,16},{10,18},{12,20},{14,22},{16,8},... | collective-permute-start | bytes 442376 | tf_op jit(solution)/shard_map/ppermute | solution.py:1023
  172.9 0.6 copy-start.15
  172.9 0.6 copy-start.14

commit v3 on v2

--- a/solution.py
+++ b/solution.py
@@ -227,7 +227,6 @@
 F32 = jnp.float32
 BF16 = jnp.bfloat16
 LOGZERO = -1e30
-VMEM_LIMIT = 56 * 2**20
 
 
 def mm(a, b, dims=((1,), (0,)), precision=None):
@@ -254,8 +253,50 @@
 
 
 def silu_parts(v):
-    sg = 1.0 / (1.0 + jnp.exp(-v))
-    return v * sg, sg * (1.0 + v * (1.0 - sg))
+    sg = 0.5 * jnp.tanh(0.5 * v) + 0.5
+    act = v * sg
+    return act, sg + act * (1.0 - sg)
+
+
+def thirds(v):
+    hi = v.astype(BF16).astype(F32)
+    rest = v - hi
+    mid = rest.astype(BF16).astype(F32)
+    return hi, mid, rest - mid
+
+
+def column_terms(values):
+    sub = iota((16, 128), 0)
+    v = jnp.ones((16, 128), F32)
+    for k, value in enumerate(values):
+        v = jnp.where((sub >= 3 * k) & (sub < 3 * k + 3), value, v)
+    hi, mid, low = thirds(v)
+    part = sub % 3
+    out = jnp.where(part == 0, hi, jnp.where(part == 1, mid, low))
+    return jnp.where(sub < 3 * len(values), out, 1.0).astype(BF16)
+
+
+def row_base(count, places):
+    sub = iota((16, 384), 0)
+    lane = iota((16, 384), 1)
+    out = jnp.zeros((16, 384), F32)
+    for k, spans in enumerate(places):
+        for lo, hi in spans:
+            out = jnp.where((sub >= 3 * k) & (sub < 3 * k + 3) & (lane >= lo) & (lane < hi), 1.0, out)
+    return out
+
+
+def row_terms(count, base, one, two):
+    sub = iota((16, 128), 0)
+    part = sub - 3 * count
+    made = []
+    for k, value in enumerate((one, two)):
+        hi, mid, low = thirds(jnp.broadcast_to(value, (16, 128)))
+        here = base[:, 128 * k : 128 * (k + 1)]
+        made.append(
+            jnp.where(part == 0, hi, jnp.where(part == 1, mid, jnp.where(part == 2, low, here))).astype(BF16)
+        )
+    return jnp.concatenate(made + [base[:, 256:].astype(BF16)], axis=1)
 
 
 def conv_taps(src, seg_src, taps, first, rows):
@@ -269,9 +310,8 @@
 
 
 def front_kernel(
-    length, hl, starts, live_ref, x_in, edge, gain, wdt_a, wdt_b, wbc_ref, taps_ref, small_a, small_b,
-    info, taps_o, gain_o, skip_o, wdt, wbc, taps, normed_o, rs_o, bcm_o, dsl_o, b_o, bk_o, bkt_o, c_o, ce_o, cet_o, g_o, gt_o,
-    colt_o, rows_o, coltt_o, rowst_o, et_o, wt_o, dpt_o, dt_o, sig_o, seg_s, maps_s, cum_s, x_s,
+    length, hl, starts, live_ref, x_in, gain, wbc_ref, taps_ref, small_a, small_b,
+    info, taps_o, gain_o, skip_o, wdt, wbc, taps, normed_o, rs_o, bcm_o, dsl_o, maps_o, ta_o, tb_o, tc_o, dpt_o, sig_o, seg_s, maps_s, cum_s, x_s,
 ):
     nb = length // BLOCK
     ext = length + 2 * HALO
@@ -286,28 +326,31 @@
     info[6] = live_ref.shape[1]
     info[7] = n
     ch = small_a.shape[1]
-    taps_o[:, 0:ch] = small_a[0:8, :]
-    taps_o[:, ch : 2 * ch] = small_b[0:8, :]
-    gain_o[:, 0:ch] = small_a[8:16, :]
-    gain_o[:, ch : 2 * ch] = small_b[8:16, :]
-    skip_o[:, 0:ch] = small_a[16:24, :]
-    skip_o[:, ch : 2 * ch] = small_b[16:24, :]
-    src = iota((2 * hl, 128), 0)
-    dst = iota((2 * hl, 128), 1)
+    for k, small in enumerate((small_a, small_b)):
+        cols = slice(k * ch, (k + 1) * ch)
+        taps_o[:, cols] = small[0:8, :]
+        gain_o[:, cols] = jnp.broadcast_to(small[7:8, :], (8, ch))
+        skip_o[:, cols] = jnp.broadcast_to(small[8:9, :], (8, ch))
+    dst = iota((128, 2 * hl), 0)
+    src = iota((128, 2 * hl), 1)
     place = (src % 2) * 64 + src // 2
-    one = jnp.float32(1.0)
-    at_a = jnp.where(dst == place, one, 0.0).astype(BF16)
-    at_b = jnp.where(dst == place + hl, one, 0.0).astype(BF16)
-    wdt[...] = (mm(wdt_a[...], at_a) + mm(wdt_b[...], at_b)).astype(BF16)
+    at_a = jnp.where(dst == place, 1.0, 0.0).astype(BF16)
+    at_b = jnp.where(dst == place + hl, 1.0, 0.0).astype(BF16)
+    own_steps = small_a[16 : 16 + 2 * hl, :].astype(BF16)
+    far_steps = small_b[16 : 16 + 2 * hl, :].astype(BF16)
+    wdt[...] = (mm(at_a, own_steps) + mm(at_b, far_steps)).astype(BF16)
     wbc[...] = pack_columns(wbc_ref[...])
     taps[...] = pack_columns(taps_ref[...])
 
-    bias = small_a[24:25, 0:128] + pltpu.roll(small_b[24:25, 0:128], hl, 1)
-    alog = small_a[25:26, 0:128] + pltpu.roll(small_b[25:26, 0:128], hl, 1)
-    zero_edge = jnp.zeros((HALO, dm), BF16)
-    x_s[0:HALO, :] = jnp.where(n == 1, edge[...], zero_edge)
+    bias = small_a[9:10, 0:128] + pltpu.roll(small_b[9:10, 0:128], hl, 1)
+    alog = small_a[9:10, 128:256] + pltpu.roll(small_b[9:10, 128:256], hl, 1)
+    edge = small_b[16 + 2 * hl : 24 + 2 * hl, :]
+    zero_edge = jnp.zeros((8, dm), F32)
+    before = jnp.concatenate([zero_edge, jnp.where(n == 1, edge, 0.0)], axis=0)
+    behind = jnp.concatenate([jnp.where(n == 1, 0.0, edge), zero_edge], axis=0)
+    x_s[0:HALO, :] = before.astype(BF16)
     x_s[HALO : HALO + length, :] = x_in[...]
-    x_s[HALO + length : ext, :] = jnp.where(n == 1, zero_edge, edge[...])
+    x_s[HALO + length : ext, :] = behind.astype(BF16)
     x = x_s[...].astype(F32)
     rs = lax.rsqrt(jnp.mean(x * x, axis=1, keepdims=True) + EPS)
     normed = (x * rs * gain[...]).astype(BF16)
@@ -335,9 +378,9 @@
     cprev = jnp.where(segp == segx, maps_s[HALO - 1 : HALO - 1 + length, 128:256], 0.0)
     cnext = jnp.where(segn == segx, maps_s[HALO + 1 : HALO + 1 + length, 128:256], 0.0)
     cmap = jnp.where(fwd, cprev, cnext)
-    b_o[...] = bmap.astype(BF16)
-    c_o[...] = cmap.astype(BF16)
-    raw = mm(normed[own, :], wdt[...]) + bias
+    maps_o[:, 0:128] = bmap.astype(BF16)
+    maps_o[:, 128:256] = cmap.astype(BF16)
+    raw = nt(normed[own, :], wdt[...]) + bias
     softp = jnp.maximum(raw, 0.0) + jnp.log(1.0 + jnp.exp(-jnp.abs(raw)))
     softp = jnp.where(raw < -15.0, jnp.exp(jnp.minimum(raw, 0.0)), softp)
     pos128 = iota((length, 128), 0) + off
@@ -347,7 +390,7 @@
     ratio = jnp.where(m, jnp.where(raw < -15.0, 1.0, sg / jnp.maximum(softp, 1e-30)), 0.0)
     rate = -jnp.exp(alog)
     a = dt * rate
-    dt_o[...] = a
+    sig_o[:, 256:384] = a
     sig_o[:, 0:128] = sg * rate
     sig_o[:, 128:256] = ratio
     tri = (iota((BLOCK, BLOCK), 0) >= iota((BLOCK, BLOCK), 1)).astype(F32)
@@ -365,13 +408,9 @@
         end = cum[BLOCK - 1 : BLOCK, :]
         colt = jnp.where(fwdb, cx, end - cum)
         rows = jnp.where(fwdb, logdt[blk, :] - cum, cx + logdt[blk, :] - end)
-        colt_o[blk, :] = colt
-        rows_o[blk, :] = rows
-        coltt = colt.T
-        coltt_o[b] = coltt
-        et_o[b] = jnp.exp(coltt)
-        rowst_o[b] = rows.T
-        wt_o[b] = jnp.exp(jnp.minimum(rows + end, 60.0)).T
+        tb_o[0, b] = colt.T
+        tb_o[1, b] = rows.T
+        ta_o[0, b] = jnp.minimum(rows + end, 60.0).T
         first_pos = off + b * BLOCK
         sp = seg_at(info, sub + first_pos)
         st = seg_at(info, ln + first_pos)
@@ -383,10 +422,10 @@
         keep = jnp.where(fwdb, (sp == last).astype(F32), (sp == begin).astype(F32))
         ce = cmap[blk, :] * enter
         bk = bmap[blk, :] * keep
-        ce_o[blk, :] = ce
-        bk_o[blk, :] = bk
-        cet_o[b] = ce.T
-        bkt_o[b] = bk.T
+        tb_o[3, b] = ce
+        tc_o[1, b] = bk
+        tc_o[2, b] = ce.T
+        ta_o[1, b] = bk.T
         chain = jnp.where(fwdb[0:1, :], (last == before).astype(F32)[0:1, :], (begin == after).astype(F32)[0:1, :])
         dvals.append(jnp.exp(end) * chain)
         ends.append(end)
@@ -398,8 +437,8 @@
         high = same & (sub < ln)
         bf = jnp.where(fwdb, bb, zero)
         br = jnp.where(fwdb, zero, bb)
-        g_o[b] = jnp.where(low, nt(cb, bf), jnp.where(high, nt(cb, br), 0.0))
-        gt_o[b] = jnp.where(high, nt(bf, cb), jnp.where(low, nt(br, cb), 0.0))
+        tb_o[2, b] = jnp.where(low, nt(cb, bf), jnp.where(high, nt(cb, br), 0.0))
+        tc_o[0, b] = jnp.where(high, nt(bf, cb), jnp.where(low, nt(br, cb), 0.0))
     ones = jnp.ones((1, 128), F32)
     prefix, suffix = [ones], [ones]
     for b in range(nb):
@@ -441,8 +480,8 @@
     j = pl.program_id(0)
     step = j
     if other:
-        p0, p1, p2, p3, taps, wt, bkt, dpt = refs[:8]
-        xc_o, vm_o, ds_o, s_o, bnd_o, wvo_o, vm_s, seg_s, wall_s = refs[13:]
+        p0, p1, p2, p3, taps, ta, dpt = refs[:7]
+        xc_o, vm_o, ds_o, s_o, bnd_o, wvo_o, vm_s, seg_s, wall_s = refs[11:]
         j = j + pl.num_programs(0)
 
         @pl.when(step == 0)
@@ -453,7 +492,7 @@
 
         wv = wall_s[step]
     else:
-        wv_ref, taps, wt, bkt, dpt, xc_o, vm_o, ds_o, s_o, bnd_o, vm_s, seg_s = refs
+        wv_ref, taps, ta, dpt, xc_o, vm_o, ds_o, s_o, bnd_o, vm_s, seg_s = refs
         wv = wv_ref[...]
     off, count = info[5], info[4]
 
@@ -478,8 +517,8 @@
         got = []
         for i in range(2):
             h = 2 * j + i
-            w = jnp.where(top, wt[b, pl.ds(h, 1), :], wt[b, pl.ds(64 + h, 1), :])
-            got.append((bkt[b] * w).astype(BF16))
+            w = jnp.exp(jnp.where(top, ta[0, b, pl.ds(h, 1), :], ta[0, b, pl.ds(64 + h, 1), :]))
+            got.append((ta[1, b] * w).astype(BF16))
         got = mm(jnp.concatenate(got, axis=0), xc[blk, :])
         loc.append(jnp.where(lane < 64, got[0:BLOCK, :], got[BLOCK:, :]))
     state = jnp.zeros((64, 128), F32)
@@ -496,14 +535,16 @@
     bnd_o[0] = jnp.where(info[7] == 0, end_f, state).astype(BF16)
 
 
-def scan_kernel(length, info, xc_ref, s_ref, s0_ref, dpt, colt, rowst, ce, g, skip, y_o, st_o):
+def scan_kernel(length, first_pair, info, xc_ref, s_ref, s0_ref, dpt, tb, skip, *refs):
     nb = length // BLOCK
-    j = pl.program_id(0)
+    y_o, st_o = refs[-2:]
+    j = pl.program_id(0) + first_pair
     right = (info[7] == 1).astype(F32)
     s0 = s0_ref[0].astype(F32)
     lane = iota((BLOCK, 128), 1)
     first = lane < 64
     low = iota((BLOCK, BLOCK), 0) > lane
+    base = row_base(2, [[(0, 128), (256, 320)], [(128, 256), (320, 384)]])
     for i in range(nb + 1):
         f = s_ref[0, i, 0:64, :].astype(F32) + pair_rows(dpt, j, 16, i, 0) * (s0 * right)
         r = s_ref[0, i, 64:128, :].astype(F32) + pair_rows(dpt, j, 16, i, 1) * (s0 * (1.0 - right))
@@ -516,12 +557,11 @@
         got = []
         for i in range(2):
             h = 2 * j + i
-            mine = pltpu.roll(colt[blk, :], 128 - h, 1)
-            cf = jnp.broadcast_to(mine[:, 0:1], (BLOCK, 128))
-            cb = jnp.broadcast_to(mine[:, 64:65], (BLOCK, 128))
-            diff = jnp.where(low, cf + rowst[b, pl.ds(h, 1), :], cb + rowst[b, pl.ds(64 + h, 1), :])
-            mix = jnp.exp(jnp.minimum(diff, 60.0)) * g[b]
-            ct = ce[blk, :] * jnp.exp(jnp.where(first, cf, cb))
+            terms = column_terms([tb[0, b, pl.ds(h, 1), :], tb[0, b, pl.ds(64 + h, 1), :]])
+            expo = tn(terms, row_terms(2, base, tb[1, b, pl.ds(h, 1), :], tb[1, b, pl.ds(64 + h, 1), :]))
+            diff = jnp.where(low, expo[:, 0:128], expo[:, 128:256])
+            mix = jnp.exp(jnp.minimum(diff, 60.0)) * tb[2, b]
+            ct = tb[3, b] * jnp.exp(expo[:, 256:])
             lhs = jnp.concatenate([mix.astype(BF16), ct.astype(BF16)], axis=1)
             got.append(lhs)
         got = mm(jnp.concatenate(got, axis=0), rhs)
@@ -539,64 +579,78 @@
 
 def gate_kernel(
     tiles, x_ref, g_ref, normed, y_ref, wout_a, wg_a, p0, p1, p2, p3, gain,
-    out_o, gy_o, keep_o, send_o, ggate_o, ggain_o, wgo_o, hn_s, other_s,
+    out_o, gy_o, keep_o, send_o, ggate_o, ggain_o, wgo_o, hn_s, other_s, gated_s, act_s, dact_s, ghn_s,
 ):
-    i = pl.program_id(0)
     dm = x_ref.shape[1]
-
-    @pl.when(i == 0)
-    def _():
-        assemble(other_s, (p0, p1, p2, p3))
-        wgo_o[...] = other_s[:, dm:]
-
-    wout = (wout_a[...], other_s[:, 0:dm])
-
     chans = y_ref.shape[1]
     half = chans // 2
-    y = y_ref[...].astype(F32)
-    nrows = normed[pl.ds(pl.multiple_of(i * BLOCK + HALO, HALO), BLOCK), :]
-    gate = jnp.concatenate([mm(nrows, wg_a[...]), mm(nrows, other_s[:, dm:])], axis=1)
-    act, dact = silu_parts(gate)
-    gated = y * act
-    inv = lax.rsqrt(jnp.sum(gated * gated, axis=1, keepdims=True) * (1.0 / chans) + EPS)
-    nrm = gated * inv
-    gainv = gain[0:1, :]
-    hn = (nrm * gainv).astype(BF16)
-    rows = pl.ds(pl.multiple_of(i * BLOCK, BLOCK), BLOCK)
-    hn_s[rows, :] = hn
-    branch = mm(hn[:, 0:half], wout[0]) + mm(hn[:, half:], wout[1])
-    out_o[...] = (x_ref[rows, :].astype(F32) + branch).astype(BF16)
-    g = g_ref[rows, :]
-    ghn = jnp.concatenate([nt(g, wout[0]), nt(g, wout[1])], axis=1)
-
-    @pl.when(i == 0)
-    def _():
-        ggain_o[...] = jnp.zeros_like(ggain_o)
-
-    ggain_o[0:1, :] += jnp.sum(ghn * nrm, axis=0, keepdims=True)
-    wgt = ghn * gainv
-    cross = jnp.sum(wgt * gated, axis=1, keepdims=True) * (1.0 / chans)
-    ggated = inv * wgt - gated * (inv * inv * inv * cross)
-    gy_o[...] = (ggated * act).astype(BF16)
-    ggate_o[rows, :] = (ggated * y * dact).astype(BF16)
-
-    @pl.when(i == tiles - 1)
-    def _():
-        length = g_ref.shape[0]
-        gt = g_ref[...].T
-        nt_ = normed[HALO : HALO + length, :].T
-        for k in range(2):
-            for p in range(half // 256):
-                cols = slice(k * half + p * 256, k * half + (p + 1) * 256)
-                dst = slice(p * 256, (p + 1) * 256)
-                dst2 = slice(half + p * 256, half + (p + 1) * 256)
-                by_core(mm(gt, hn_s[:, cols]), keep_o.at[k, :, dst], send_o.at[k, :, dst])
-                by_core(mm(nt_, ggate_o[:, cols]), keep_o.at[k, :, dst2], send_o.at[k, :, dst2])
-
-
-def gstate_kernel(length, info, gy_ref, et, cet, dpt, gs_o, bnd_o):
+    step = 256
+    assemble(other_s, (p0, p1, p2, p3))
+    wgo_o[...] = other_s[:, dm:]
+    ggain_o[...] = jnp.zeros_like(ggain_o)
+
+    @pl.loop(0, tiles)
+    def _(i):
+        start = pl.multiple_of(i * BLOCK, BLOCK)
+        rows = pl.ds(start, BLOCK)
+        nrows = normed[pl.ds(pl.multiple_of(start + HALO, HALO), BLOCK), :]
+        squares = jnp.zeros((BLOCK, 128), F32)
+        for lo in range(0, chans, step):
+            wg = wg_a[:, lo : lo + step] if lo < half else other_s[:, dm + lo - half : dm + lo - half + step]
+            gates = mm(nrows, wg)
+            for at in range(0, step, 128):
+                cols = slice(lo + at, lo + at + 128)
+                act, dact = silu_parts(gates[:, at : at + 128])
+                gated = y_ref[rows, cols].astype(F32) * act
+                squares = squares + gated * gated
+                gated_s[:, cols] = gated
+                act_s[:, cols] = act
+                dact_s[:, cols] = dact
+        inv = lax.rsqrt(jnp.sum(squares, axis=1, keepdims=True) * (1.0 / chans) + EPS)
+        inv = jnp.broadcast_to(inv, (BLOCK, 128))
+        g = g_ref[rows, :]
+        across = jnp.zeros((BLOCK, 128), F32)
+        for lo in range(0, chans, step):
+            wo = wout_a[lo : lo + step, :] if lo < half else other_s[lo - half : lo - half + step, 0:dm]
+            ghns = nt(g, wo)
+            for at in range(0, step, 128):
+                cols = slice(lo + at, lo + at + 128)
+                gainv = gain[0:1, cols]
+                gated = gated_s[:, cols]
+                nrm = gated * inv
+                hn_s[rows, cols] = (nrm * gainv).astype(BF16)
+                ghn = ghns[:, at : at + 128]
+                ggain_o[0:1, cols] += jnp.sum(ghn * nrm, axis=0, keepdims=True)
+                wgt = ghn * gainv
+                ghn_s[:, cols] = wgt
+                across = across + wgt * gated
+        cross = jnp.sum(across, axis=1, keepdims=True) * (1.0 / chans)
+        cross = jnp.broadcast_to(cross, (BLOCK, 128)) * (inv * inv * inv)
+        hn = hn_s[rows, :]
+        branch = mm(hn[:, 0:half], wout_a[...]) + mm(hn[:, half:], other_s[:, 0:dm])
+        out_o[rows, :] = (x_ref[rows, :].astype(F32) + branch).astype(BF16)
+        for lo in range(0, chans, 128):
+            cols = slice(lo, lo + 128)
+            ggated = inv * ghn_s[:, cols] - gated_s[:, cols] * cross
+            gy_o[rows, cols] = (ggated * act_s[:, cols]).astype(BF16)
+            ggate_o[rows, cols] = (ggated * y_ref[rows, cols].astype(F32) * dact_s[:, cols]).astype(BF16)
+
+    length = g_ref.shape[0]
+    gt = g_ref[...].T
+    nt_ = normed[HALO : HALO + length, :].T
+    for k in range(2):
+        for p in range(half // 256):
+            cols = slice(k * half + p * 256, k * half + (p + 1) * 256)
+            dst = slice(p * 256, (p + 1) * 256)
+            dst2 = slice(half + p * 256, half + (p + 1) * 256)
+            by_core(mm(gt, hn_s[:, cols]), keep_o.at[k, :, dst], send_o.at[k, :, dst])
+            by_core(mm(nt_, ggate_o[:, cols]), keep_o.at[k, :, dst2], send_o.at[k, :, dst2])
+
+
+def gstate_kernel(length, first_pair, info, gy_ref, coltt, cet, dpt, *refs):
     nb = length // BLOCK
-    j = pl.program_id(0)
+    gs_o, bnd_o = refs[-2:]
+    j = pl.program_id(0) + first_pair
     lane = iota((BLOCK, 128), 1)
     top = iota((BLOCK, 128), 0) < 64
     loc = []
@@ -606,7 +660,7 @@
         got = []
         for i in range(2):
             h = 2 * j + i
-            e = jnp.where(top, et[b, pl.ds(h, 1), :], et[b, pl.ds(64 + h, 1), :])
+            e = jnp.exp(jnp.where(top, coltt[b, pl.ds(h, 1), :], coltt[b, pl.ds(64 + h, 1), :]))
             got.append((cet[b] * e).astype(BF16))
         got = mm(jnp.concatenate(got, axis=0), gy)
         loc.append(jnp.where(lane < 64, got[0:BLOCK, :], got[BLOCK:, :]))
@@ -625,11 +679,13 @@
 
 
 def gscan_kernel(
-    length, info, xc_ref, ds_ref, gy_ref, st_ref, gs_ref, gs0_ref, dpt, rows_ref, coltt, et, gt, bk, cet, skip,
-    gmix_o, ggt_o, gb_o, gct_o, k_o, r_o, phi_o, gskip_o, gst_s,
+    length, first_pair, info, xc_ref, ds_ref, gy_ref, st_ref, gs_ref, gs0_ref, dpt, rowst, wt, coltt, tc, skip,
+    *refs,
 ):
     nb = length // BLOCK
-    j = pl.program_id(0)
+    gmix_o, ggt_o, gb_o, gct_o, k_o, r_o, phi_o, gskip_o, edge_o, gst_s = refs[-10:]
+    step = pl.program_id(0)
+    j = step + first_pair
     right = (info[7] == 1).astype(F32)
     s0 = gs0_ref[0].astype(F32)
     sub = iota((BLOCK, BLOCK), 0)
@@ -638,13 +694,12 @@
     later = lane > sub
     top = sub < 64
 
-    @pl.when(j == 0)
+    @pl.when(step == 0)
     def _():
-        ggt_o[...] = jnp.zeros_like(ggt_o)
-        gb_o[...] = jnp.zeros_like(gb_o)
-        gct_o[...] = jnp.zeros_like(gct_o)
-        k_o[...] = jnp.zeros_like(k_o)
-        r_o[...] = jnp.zeros_like(r_o)
+        for k, acc in enumerate((ggt_o, gb_o, gct_o, k_o, r_o)):
+            acc[...] = jnp.zeros_like(acc) if first_pair else refs[3 + k][...]
+
+    base = row_base(4, [[(0, 128)], [(128, 256)], [(256, 320)], [(320, 384)]])
 
     phi_o[...] = jnp.zeros_like(phi_o)
     for i in range(nb + 1):
@@ -673,19 +728,16 @@
         none = jnp.zeros_like(left)
         big2 = nt(jnp.concatenate([jnp.where(first2, left, none), jnp.where(first2, none, left)], axis=0), rhs)
         got = []
-        sum_ge, sum_gct, sum_gb = [], [], []
+        sum_ge, sum_gct, sum_gb, kparts = [], [], [], []
         for i in range(2):
             h = 2 * j + i
-            mine = pltpu.roll(rows_ref[blk, :], 128 - h, 1)
-            cf = jnp.broadcast_to(mine[:, 0:1], (BLOCK, 128))
-            cb = jnp.broadcast_to(mine[:, 64:65], (BLOCK, 128))
-            diff = jnp.where(later, cf + coltt[b, pl.ds(h, 1), :], cb + coltt[b, pl.ds(64 + h, 1), :])
+            terms = column_terms([v[b, pl.ds(at + h, 1), :] for v in (rowst, wt) for at in (0, 64)])
+            expo = tn(terms, row_terms(4, base, coltt[b, pl.ds(h, 1), :], coltt[b, pl.ds(64 + h, 1), :]))
+            diff = jnp.where(later, expo[:, 0:128], expo[:, 128:256])
             et_m = jnp.exp(jnp.minimum(diff, 60.0))
-            mt = et_m * gt[b]
-            endf = dpt[pl.ds(h, 1), :][:, 48 + b : 49 + b]
-            endb = dpt[pl.ds(64 + h, 1), :][:, 48 + b : 49 + b]
-            w = jnp.exp(jnp.minimum(jnp.where(first, cf, cb) + jnp.where(first[0:1, :], endf, endb), 60.0))
-            bt = bk[blk, :] * w
+            mt = et_m * tc[0, b]
+            w = jnp.exp(expo[:, 256:])
+            bt = tc[1, b] * w
             big = big2[2 * BLOCK * i : 2 * BLOCK * (i + 1), :]
             gmt = big[0:BLOCK, 0:BLOCK]
             gbt = big[0:BLOCK, BLOCK:]
@@ -694,34 +746,41 @@
             sum_ge.append(ge)
             q = gmt * mt
             qf = jnp.where(later, q, 0.0)
-            e = jnp.where(top, et[b, pl.ds(h, 1), :], et[b, pl.ds(64 + h, 1), :])
+            e = jnp.exp(jnp.where(top, coltt[b, pl.ds(h, 1), :], coltt[b, pl.ds(64 + h, 1), :]))
             gce = gctt * e
             sum_gct.append(gce)
-            ct = gce * cet[b]
+            ct = gce * tc[2, b]
             rf = jnp.sum(qf, axis=0, keepdims=True)
             rall = jnp.sum(q, axis=0, keepdims=True)
             r_o[b, pl.ds(h, 1), :] = rf + jnp.sum(ct[0:64, :], axis=0, keepdims=True)
             r_o[b, pl.ds(64 + h, 1), :] = rall - rf + jnp.sum(ct[64:128, :], axis=0, keepdims=True)
             gbw = gbt * w
             sum_gb.append(gbw)
-            u = gbw * bk[blk, :]
+            u = gbw * tc[1, b]
             kf = jnp.sum(qf + jnp.where(first, u, 0.0), axis=1, keepdims=True)
             kb = jnp.sum(q + u, axis=1, keepdims=True) - kf
-            k_o[blk, :] += jnp.where(lane == h, kf, jnp.where(lane == 64 + h, kb, 0.0))
+            kparts += [kf, kb]
             lhs = jnp.concatenate([mt.astype(BF16), bt.astype(BF16)], axis=1)
             got.append(lhs)
         ggt_o[b] += sum_ge[0] + sum_ge[1]
         gct_o[b] += sum_gct[0] + sum_gct[1]
         gb_o[b] += sum_gb[0] + sum_gb[1]
+        two = jnp.where(lane % 64 == 0, jnp.where(first, kparts[0], kparts[1]), jnp.where(first, kparts[2], kparts[3]))
+        k_o[blk, :] += pltpu.roll(jnp.where(lane % 64 < 2, two, 0.0), 2 * j, 1)
         got = mm(jnp.concatenate(got, axis=0), rhs)
         gx = jnp.where(first, got[0:BLOCK, :], got[BLOCK:, :]) + skip[0:1, :] * gyf
-        gmix_o[blk, :] = (gx * ds_ref[blk, :].astype(F32)).astype(BF16)
+        gmix = (gx * ds_ref[blk, :].astype(F32)).astype(BF16)
+        gmix_o[blk, :] = gmix
+        if b == 0:
+            edge_o[...] = gmix[0:HALO, :]
+        if b == nb - 1:
+            edge_o[...] = jnp.where(info[7] == 0, gmix[BLOCK - HALO :, :], edge_o[...])
     gskip_o[...] = jnp.broadcast_to(gskip, (8, 128))
 
 
 def join_kernel(
-    length, heads, info, ggt, gb, gct, k_ref, r_ref, phi, b_ref, c_ref, bk, dsl, a_ref, sig,
-    gmb_o, gv_o, small_o, gc_s, gm_s,
+    length, heads, info, ggt, gb, gct, k_ref, r_ref, phi, maps, dsl, sig,
+    gmb_o, gv_o, small_o, edge_o, gc_s, gm_s,
 ):
     nb = length // BLOCK
     off = info[5]
@@ -760,8 +819,8 @@
         gg = ggt[b]
         gf = jnp.where(same & high, gg, 0.0).astype(BF16)
         gr = jnp.where(same & low, gg, 0.0).astype(BF16)
-        cm = c_ref[blk, :]
-        bm = b_ref[blk, :]
+        cm = maps[blk, 128:256]
+        bm = maps[blk, 0:128]
         gm_s[ext, 0:128] = jnp.where(first, mm(gf, cm), mm(gr, cm)) + gb[b] * keep
         gc_s[ext, :] = jnp.where(first, tn(gf, bm), tn(gr, bm)) + gct[b].T * enter
         kb = k_ref[blk, :]
@@ -772,7 +831,7 @@
         gv = kb * sig[blk, 128:256] + ga * sig[blk, 0:128]
         gv_o[blk, :] = gv.astype(BF16)
         sum_bias = sum_bias + jnp.sum(gv, axis=0, keepdims=True)
-        sum_rate = sum_rate + jnp.sum(ga * a_ref[blk, :], axis=0, keepdims=True)
+        sum_rate = sum_rate + jnp.sum(ga * sig[blk, 256:384], axis=0, keepdims=True)
     small_o[...] = jnp.zeros_like(small_o)
     small_o[0:1, :] = sum_bias
     small_o[1:2, :] = sum_rate
@@ -788,11 +847,32 @@
     from_prev = jnp.where(seg0 == segp, gc_s[lo - 1 : lo - 1 + mid, :], 0.0)
     gm_s[lo : lo + mid, 128:256] = jnp.where(iota((mid, 128), 1) < 64, from_next, from_prev)
     gmb_o[...] = gm_s[...] * dsl[...]
+    lo = HALO // 2
+    edge_o[...] = jnp.where(
+        info[7] == 0, gmb_o[length + lo : length + lo + HALO, :], gmb_o[lo : lo + HALO, :]
+    )
+
+
+def back_conv(length, seg_s, live, grad, data, tap):
+    own = slice(HALO, HALO + length)
+    seg0 = seg_s[own, :]
+    mine = grad[own, :]
+    total = mine * tap[3:4, :]
+    gtap = [None] * 7
+    gtap[3] = jnp.sum(mine * data[own, :], axis=0, keepdims=True)
+    for k in (0, 1, 2, 4, 5, 6):
+        lo = HALO + 3 - k
+        same = seg_s[lo : lo + length, :] == seg0
+        total = total + jnp.where(same, grad[lo : lo + length, :], 0.0) * tap[k : k + 1, :]
+        up = HALO + k - 3
+        same = seg_s[up : up + length, :] == seg0
+        gtap[k] = jnp.sum(jnp.where(same, data[up : up + length, :], 0.0) * mine, axis=0, keepdims=True)
+    return jnp.where(live, total, 0.0), gtap
 
 
 def back_kernel(
-    length, steps, info, gmix, edge, vm, wv_a, wg_a, wv_b, wg_b, ggate, normed, taps, gmb, edge_bc, bcm, taps_bc, gv, wdt, wbc, x_ref, g_ref, rs, pre, ggain, gskip, small,
-    keep_o, send_o, tiny_o, gin_o, acc_s, ext_s, vm_s, seg_s,
+    length, steps, info, gmix, edge_a, edge_b, vm, wv_a, wg_a, wv_b, wg_b, ggate, normed, taps, ggain, gskip,
+    keep_o, send_o, tiny_o, acc_o, ext_s, vm_s, seg_s,
 ):
     j = pl.program_id(0)
     ext = length + 2 * HALO
@@ -802,65 +882,18 @@
     @pl.when(j == 0)
     def _():
         seg_s[...] = seg_at(info, iota((ext, 128), 0) + (off - HALO))
-        ext_s[...] = jnp.zeros_like(ext_s)
-
-    seg0 = seg_s[own, :]
+        tiny_o[...] = jnp.zeros_like(tiny_o)
+        acc_o[...] = jnp.zeros_like(acc_o)
+
     live = iota((length, 128), 0) + off < count
-
-    def back_conv(grad, data, tap):
-        total = grad[own, :] * tap[3:4, :]
-        mine = grad[own, :]
-        gtap = [None] * 7
-        gtap[3] = jnp.sum(mine * data[own, :], axis=0, keepdims=True)
-        for k in (0, 1, 2, 4, 5, 6):
-            lo = HALO + 3 - k
-            same = seg_s[lo : lo + length, :] == seg0
-            total = total + jnp.where(same, grad[lo : lo + length, :], 0.0) * tap[k : k + 1, :]
-            up = HALO + k - 3
-            same = seg_s[up : up + length, :] == seg0
-            gtap[k] = jnp.sum(
-                jnp.where(same, data[up : up + length, :], 0.0) * mine, axis=0, keepdims=True
-            )
-        return jnp.where(live, total, 0.0), gtap
-
-    @pl.when(j == 0)
-    def _():
-        no = normed[own, :]
-        both = []
-        tiny_o[...] = jnp.zeros_like(tiny_o)
-        for half in range(2):
-            tiny_o[half, 10:11, 0:128] = small[8 * half : 8 * half + 1, :]
-            tiny_o[half, 10:11, 128:256] = small[8 * half + 1 : 8 * half + 2, :]
-        for k in range(2):
-            cols = slice(k * 128, (k + 1) * 128)
-            ext_s[...] = gmb[:, cols]
-            lo = HALO // 2
-            hi = length + lo
-            got = edge_bc[:, cols]
-            ext_s[lo : lo + HALO, :] += jnp.where(info[7] == 1, got, 0.0)
-            ext_s[hi : hi + HALO, :] += jnp.where(info[7] == 1, 0.0, got)
-            vm_s[...] = bcm[:, cols]
-            gbc, gtap = back_conv(ext_s, vm_s, taps_bc.at[:, cols])
-            for t in range(7):
-                at = (t % 3) * 256 + k * 128
-                for half in range(2):
-                    tiny_o[half, 11 + t // 3 : 12 + t // 3, at : at + 128] = gtap[t]
-            both.append(gbc.astype(BF16))
-        gbc = jnp.concatenate(both + [gv[...]], axis=1)
-        gw = tn(no, gbc)
-        ch = keep_o.shape[2] - 384
-        by_core(gw, keep_o.at[0, :, ch:], send_o.at[0, :, ch:])
-        turned = pltpu.roll(gw[:, 256:], 128 - steps, 1)
-        by_core(jnp.concatenate([gw[:, 0:256], turned], axis=1), keep_o.at[1, :, ch:], send_o.at[1, :, ch:])
-        acc_s[...] = nt(gbc[:, 0:256], wbc[...]) + nt(gv[...], wdt[...])
-
+    near = j < steps // 2
     ext_s[own, :] = gmix[...].astype(F32)
-    halo = edge[...].astype(F32)
+    halo = jnp.where(near, edge_a[...].astype(F32), edge_b[...].astype(F32))
     right = info[7] == 1
     ext_s[0:HALO, :] = jnp.where(right, halo, 0.0)
     ext_s[HALO + length : ext, :] = jnp.where(right, 0.0, halo)
     vm_s[...] = vm[...].astype(F32)
-    gvals, gtap = back_conv(ext_s, vm_s, taps)
+    gvals, gtap = back_conv(length, seg_s, live, ext_s, vm_s, taps)
     gvals = gvals.astype(BF16)
     half = j // (steps // 2)
     here = pl.ds(pl.multiple_of((j % (steps // 2)) * 128, 128), 128)
@@ -870,27 +903,95 @@
     tiny_o[half, 7:8, here] = ggain[0:1, :]
     tiny_o[half, 8:9, here] = gskip[0:1, :]
     both = jnp.concatenate([gvals, ggate[...]], axis=1)
-    mine = j < steps // 2
     weights = jnp.concatenate(
-        [jnp.where(mine, wv_a[...], wv_b[...]), jnp.where(mine, wg_a[...], wg_b[...])], axis=1
+        [jnp.where(near, wv_a[...], wv_b[...]), jnp.where(near, wg_a[...], wg_b[...])], axis=1
     )
-    acc_s[...] += nt(both, weights)
-
-    @pl.when(j == steps - 1)
-    def _():
-        x = x_ref[...].astype(F32)
-        gn = acc_s[...]
-        r = rs[...]
-        wp = gn * pre[...]
-        mean = jnp.mean(wp * x, axis=1, keepdims=True)
-        gin_o[...] = g_ref[...].astype(F32) + r * wp - x * (r * r * r * mean)
-        gpre = jnp.sum(gn * x * r, axis=0, keepdims=True)
-        for half in range(2):
-            tiny_o[half, 9:10, 0 : gpre.shape[1]] = gpre
+    acc_o[...] += nt(both, weights)
+
+
+def last_kernel(
+    length, hl, info, acc, normed, gmb, edge, bcm, taps_bc, gv, wdt, wbc, x_ref, g_ref, rs, pre, small, tiny,
+    keep_o, send_o, tiny_o, gin_o, ext_s, vm_s, seg_s,
+):
+    ext = length + 2 * HALO
+    off, count = info[5], info[4]
+    own = slice(HALO, HALO + length)
+    seg_s[...] = seg_at(info, iota((ext, 128), 0) + (off - HALO))
+    live = iota((length, 128), 0) + off < count
+    tiny_o[...] = tiny[...]
+    for half in range(2):
+        tiny_o[half, 10:11, 0:128] = small[8 * half : 8 * half + 1, :]
+        tiny_o[half, 10:11, 128:256] = small[8 * half + 1 : 8 * half + 2, :]
+    both = []
+    for k in range(2):
+        cols = slice(k * 128, (k + 1) * 128)
+        ext_s[...] = gmb[:, cols]
+        lo = HALO // 2
+        hi = length + lo
+        got = edge[:, cols]
+        ext_s[lo : lo + HALO, :] += jnp.where(info[7] == 1, got, 0.0)
+        ext_s[hi : hi + HALO, :] += jnp.where(info[7] == 1, 0.0, got)
+        vm_s[...] = bcm[:, cols]
+        gbc, gtap = back_conv(length, seg_s, live, ext_s, vm_s, taps_bc.at[:, cols])
+        for t in range(7):
+            at = (t % 3) * 256 + k * 128
+            for half in range(2):
+                tiny_o[half, 11 + t // 3 : 12 + t // 3, at : at + 128] = gtap[t]
+        both.append(gbc.astype(BF16))
+    gbc = jnp.concatenate(both + [gv[...]], axis=1)
+    gw = tn(normed[own, :], gbc)
+    by_core(gw, keep_o.at[0], send_o.at[0])
+    turned = pltpu.roll(gw[:, 256:], 128 - hl, 1)
+    by_core(jnp.concatenate([gw[:, 0:256], turned], axis=1), keep_o.at[1], send_o.at[1])
+    gn = acc[...] + nt(gbc[:, 0:256], wbc[...]) + mm(gv[...], wdt[...])
+    x = x_ref[...].astype(F32)
+    r = rs[...]
+    wp = gn * pre[...]
+    mean = jnp.mean(wp * x, axis=1, keepdims=True)
+    gin_o[...] = g_ref[...].astype(F32) + r * wp - x * (r * r * r * mean)
+    gpre = jnp.sum(gn * x * r, axis=0, keepdims=True)
+    for half in range(2):
+        tiny_o[half, 9:10, 0 : gpre.shape[1]] = gpre
+
+
+def finish_kernel(hl, tiny, conv_o, convbc_o, pre_o, bias_o, rate_o, skip_o, gain_o):
+    ch = tiny.shape[1]
+    w = lax.axis_index("wide")
+    share = pre_o.shape[1]
+    lanes = gain_o.shape[1]
+    src = iota((ch, 128), 0)
+    dst = iota((ch, 128), 1)
+    rows = tiny[...]
+    by_head = ((src == (dst // lanes) * HD + lanes * w + dst % lanes) & (dst < hl * lanes)).astype(F32)
+    got = mm(rows, by_head, precision=HIGH)
+    for h in range(hl):
+        conv_o[:, h, :] = got[0:7, h * lanes : (h + 1) * lanes]
+        gain_o[h : h + 1, :] = got[7:8, h * lanes : (h + 1) * lanes]
+    chosen = ((src == share * w + dst) & (dst < share)).astype(F32)
+    pre_o[...] = mm(rows[8:16, :], chosen, precision=HIGH)[1:2, 0:share]
+    per = (src // HD == dst).astype(F32)
+    skip_o[...] = mm(rows[8:16, :], per, precision=HIGH)[0:1, 0:hl]
+    size = convbc_o.shape[1]
+    group = (size * w) // 64
+    start = ((group % 2) * 2 + group // 2) * 64 + (size * w) % 64
+    src = iota((256, 128), 0)
+    dst = iota((256, 128), 1)
+    chosen = ((src == start + dst) & (dst < size)).astype(F32)
+    for k in range(3):
+        part = mm(rows[8:16, 256 * k : 256 * (k + 1)], chosen, precision=HIGH)
+        for r in range(3):
+            if 3 * r + k < 7:
+                convbc_o[3 * r + k : 3 * r + k + 1, :] = part[3 + r : 4 + r, 0:size]
+    both = rows[10:11, 0:128]
+    turned = jnp.broadcast_to(both, (128, 128)).T
+    bias_o[:, 0:1] = turned[0:hl, 0:1]
+    bias_o[:, 1:2] = turned[64 : 64 + hl, 0:1]
+    rate = rows[10:11, 128:256]
+    rate_o[...] = (rate + pltpu.roll(rate, 64, 1))[:, 0:hl]
 
 
 def collect_kernel(
-    keep, send, tiny, out_o, tiny_o,
+    keep, got_v, keep_bc, send_bc, tiny, out_o, tiny_o,
     core_s, mine_s, piece_s, got_s, zsend_s, zgot_s, tcore_s, tsum_s, tgot_s, tz_s, tzgot_s,
     core_out, core_in, plane_out, plane_in, z_out, z_in,
 ):
@@ -920,7 +1021,7 @@
     rows = [pl.ds(pl.multiple_of(((z + d) % 4) * (2 * share), 2 * share), 2 * share) for d in steps + (0,)]
     first = [copy(tiny, tcore_s, core_out.at[4], core_in.at[4], core)]
     for i in range(4):
-        first.append(copy(send.at[:, rows[i], :], core_s.at[i], core_out.at[i], core_in.at[i], core))
+        first.append(copy(send_bc.at[:, rows[i], :], core_s.at[i], core_out.at[i], core_in.at[i], core))
     ways = (over_x, over_y, over_d)
     first[0].wait()
     tsum_s[...] = tiny[...] + tcore_s[...]
@@ -930,14 +1031,18 @@
         second[0].append(copy(tsum_s.at[half], tgot_s.at[k], plane_out.at[4, k], plane_in.at[4, k], other))
     for i in range(4):
         first[i + 1].wait()
-        both = keep[:, rows[i], :].astype(F32) + core_s[i].astype(F32)
-        low, high = both[:, 0:share, :], both[:, share:, :]
-        near = jnp.where(xx == 0, low, high)
-        far = jnp.where(xx == 0, high, low)
-        mine_s[i] = near[0]
-        piece_s[i, 0] = far[0].astype(BF16)
-        piece_s[i, 1] = near[1].astype(BF16)
-        piece_s[i, 2] = far[1].astype(BF16)
+        chv = keep.shape[2]
+        for cols, both in (
+            (slice(0, chv), keep[:, rows[i], :].astype(F32) + got_v[:, rows[i], :].astype(F32)),
+            (slice(chv, out_o.shape[1]), keep_bc[:, rows[i], :].astype(F32) + core_s[i].astype(F32)),
+        ):
+            low, high = both[:, 0:share, :], both[:, share:, :]
+            near = jnp.where(xx == 0, low, high)
+            far = jnp.where(xx == 0, high, low)
+            mine_s[i, :, cols] = near[0]
+            piece_s[i, 0, :, cols] = far[0].astype(BF16)
+            piece_s[i, 1, :, cols] = near[1].astype(BF16)
+            piece_s[i, 2, :, cols] = far[1].astype(BF16)
         second.append(
             [copy(piece_s.at[i, k], got_s.at[i, k], plane_out.at[i, k], plane_in.at[i, k], ways[k]) for k in range(3)]
         )
@@ -980,10 +1085,10 @@
     return jax.ShapeDtypeStruct(shape, dtype)
 
 
-def params(grid):
+def params(grid, mib):
     if grid:
-        return pltpu.CompilerParams(vmem_limit_bytes=VMEM_LIMIT, dimension_semantics=("arbitrary",))
-    return pltpu.CompilerParams(vmem_limit_bytes=VMEM_LIMIT)
+        return pltpu.CompilerParams(vmem_limit_bytes=mib * 2**20, dimension_semantics=("arbitrary",))
+    return pltpu.CompilerParams(vmem_limit_bytes=mib * 2**20)
 
 
 def cost(us):
@@ -995,24 +1100,30 @@
     return jnp.concatenate([v[..., 0:n], v[..., 2 * n : 3 * n], v[..., n : 2 * n], v[..., 3 * n :]], axis=-1)
 
 
-def small_kernel(hl, conv, gain, dtb, alog, skip, out_o):
+def small_kernel(hl, conv, gain, dtb, alog, skip, wdt, x_ref, out_o):
     ch = out_o.shape[1]
-    out_o[...] = jnp.zeros_like(out_o)
+    length = x_ref.shape[0]
     lane = iota((1, 128), 1)
     wide_lane = iota((1, ch), 1)
     bias = jnp.zeros((1, 128), F32)
     rate = jnp.zeros((1, 128), F32)
     diag = jnp.zeros((1, ch), F32)
+    out_o[0:16, :] = jnp.zeros((16, ch), F32)
     for h in range(hl):
         cols = slice(h * HD, (h + 1) * HD)
         out_o[0:7, cols] = conv[:, h, :]
-        out_o[8:9, cols] = gain[h : h + 1, :]
+        out_o[7:8, cols] = gain[h : h + 1, :]
         bias = jnp.where(lane == h, dtb[h, 0], jnp.where(lane == 64 + h, dtb[h, 1], bias))
         rate = jnp.where((lane == h) | (lane == 64 + h), alog[h], rate)
         diag = jnp.where(wide_lane // HD == h, skip[h], diag)
-    out_o[16:17, :] = diag
-    out_o[24:25, 0:128] = bias
-    out_o[25:26, 0:128] = rate
+    out_o[8:9, :] = diag
+    out_o[9:10, 0:128] = bias
+    out_o[9:10, 128:256] = rate
+    pick_row = (iota((2 * hl, 2 * hl), 0) == iota((2 * hl, 2 * hl), 1)).astype(F32).astype(BF16)
+    out_o[16 : 16 + 2 * hl, :] = nt(pick_row, wdt[...])
+    n = lax.axis_index("narrow")
+    start, end = x_ref[0:HALO, :].astype(F32), x_ref[length - HALO :, :].astype(F32)
+    out_o[16 + 2 * hl :, :] = jnp.where(n == 0, end[8:16, :], start[0:8, :])
 
 
 def swap(v):
@@ -1060,17 +1171,16 @@
     xbit = (w // 2) % 2
     zbits = w // 4
 
-    edge = swap(jnp.where(left, x[length - HALO :], x[:HALO]))
+    wdt = w_heads[:, :, 2 * HD :].reshape(dm, 2 * hl)
     small_own = pl.pallas_call(
         functools.partial(small_kernel, hl),
-        out_shape=sds((32, ch), F32),
-        in_specs=[VMEM, VMEM, SMEM, SMEM, SMEM],
+        out_shape=sds((24 + 2 * hl, ch), F32),
+        in_specs=[VMEM, VMEM, SMEM, SMEM, SMEM, VMEM, VMEM],
         out_specs=VMEM,
+        cost_estimate=cost(2),
         name="small",
-    )(conv_x, norm_gain, dt_bias, a_log, skip_d)
+    )(conv_x, norm_gain, dt_bias, a_log, skip_d, wdt, x)
     small_other = swap(small_own)
-    wdt = w_heads[:, :, 2 * HD :].reshape(dm, 2 * hl)
-    wdt_other = swap(wdt)
 
     quarter = dm // 4
     q = w % 4
@@ -1089,33 +1199,32 @@
     pos = (length, 128)
     sq = (nb, BLOCK, BLOCK)
     front_shapes = [
-        ((8, chans), F32), ((8, chans), F32), ((8, chans), F32), ((dm, 128), BF16), ((dm, 256), BF16), ((7, 256), F32),
-        ((ext, dm), BF16), ((length, 1), F32), ((ext, 256), F32), ((ext, 256), F32), (pos, BF16), (pos, F32), (sq, F32),
-        (pos, BF16), (pos, F32), (sq, F32), (sq, F32), (sq, F32), (pos, F32), (pos, F32), (sq, F32), (sq, F32),
-        (sq, F32), (sq, F32), ((128, 128), F32), (pos, F32), ((length, 256), F32),
+        ((8, chans), F32), ((8, chans), F32), ((8, chans), F32), ((128, dm), BF16), ((dm, 256), BF16), ((7, 256), F32),
+        ((ext, dm), BF16), ((length, 1), F32), ((ext, 256), F32), ((ext, 256), F32), ((length, 256), BF16),
+        ((2,) + sq, F32), ((4,) + sq, F32), ((3,) + sq, F32), ((128, 128), F32), ((length, 384), F32),
     ]
     (
-        info, taps, gain, skip, wdt_all, wbc, taps_bc, normed, rs, bcm, dsl, bmap, bk, bkt, cmap, ce, cet, gmat, gmat_t,
-        colt, rows, coltt, rowst, et, wt, dpt, a_dt, sig,
+        info, taps, gain, skip, wdt_all, wbc, taps_bc, normed, rs, bcm, dsl, maps, tab_a, tab_b, tab_c, dpt, sig,
     ) = pl.pallas_call(
         functools.partial(front_kernel, length, hl),
         out_shape=[sds((8,), jnp.int32)] + [sds(*v) for v in front_shapes],
-        in_specs=[SMEM] + [VMEM] * 10,
+        in_specs=[SMEM] + [VMEM] * 7,
         out_specs=[SMEM] + [VMEM] * len(front_shapes),
         scratch_shapes=[
             pltpu.VMEM((ext, 256), jnp.int32), pltpu.VMEM((ext, 256), F32), pltpu.VMEM((128, 128), F32),
             pltpu.VMEM((ext, dm), BF16),
         ],
-        compiler_params=params(False),
+        compiler_params=params(False, 16),
         cost_estimate=cost(8),
         name="front",
-    )(starts, live, x, edge, pre_gain.reshape(1, dm), wdt, wdt_other, w_bc, conv_bc, small_own, small_other)
-
-    state_spec = pl.BlockSpec((1, nb + 1, 128, 128), lambda j: (j, 0, 0, 0))
+    )(starts, live, x, pre_gain.reshape(1, dm), w_bc, conv_bc, small_own, small_other)
+
+    def states(first):
+        return pl.BlockSpec((1, nb + 1, 128, 128), lambda j: (j + first, 0, 0, 0))
+
     bnd_spec = pl.BlockSpec((1, 64, 128), lambda j: (j, 0, 0))
-    far_spec = pl.BlockSpec((1, 64, 128), lambda j: ((j + hp) % pairs, 0, 0))
     state_shape = sds((pairs, nb + 1, 128, 128), BF16)
-    bnd_shape = sds((pairs, 64, 128), BF16)
+    bnd_shape = sds((hp, 64, 128), BF16)
     act_shape = sds((length, chans), BF16)
     own_spec = pl.BlockSpec((dm, 128), lambda j: (0, jnp.minimum(j, hp - 1)))
     other_spec = pl.BlockSpec((dm, 128), lambda j: (0, jnp.maximum(j - hp, 0)))
@@ -1128,7 +1237,7 @@
             specs += [whole((quarter, ch), 1)] * 4
         else:
             specs += [columns(dm)]
-        specs += [columns(8, first), whole(sq, 1), whole(sq, 1), whole((128, 128), 1)] + [ANY] * len(before)
+        specs += [columns(8, first), whole((2,) + sq, 1), whole((128, 128), 1)] + [ANY] * len(before)
         scratch = [pltpu.VMEM((ext, 128), F32), pltpu.VMEM((ext, 128), jnp.int32)]
         if other:
             scratch.append(pltpu.VMEM((hp, dm, 128), BF16))
@@ -1139,52 +1248,51 @@
             in_specs=specs,
             out_specs=[
                 columns(length, first), columns(ext, first), columns(length, first),
-                pl.BlockSpec((1, nb + 1, 128, 128), lambda j: (j + first, 0, 0, 0)),
-                pl.BlockSpec((1, 64, 128), lambda j: (j + first, 0, 0)),
+                states(first), bnd_spec,
             ] + [whole((dm, ch), 1)] * other,
             scratch_shapes=scratch,
             input_output_aliases={len(specs) - len(before) + i: i for i in range(len(before))},
-            compiler_params=params(True),
-            cost_estimate=cost(8),
+            compiler_params=params(True, 14),
+            cost_estimate=cost(9),
             name="vals_other" if other else "vals_own",
-        )(info, normed, *weights, taps, wt, bkt, dpt, *before)
-
-    own_vals = vals(False, (wv,), ())
-    xc, vm, ds, s_loc, bnd, wv_other = vals(True, wv_pieces, own_vals)
-
-    y, s_true = pl.pallas_call(
-        functools.partial(scan_kernel, length),
-        grid=(pairs,),
-        out_shape=[act_shape, state_shape],
-        in_specs=[
-            SMEM, columns(length), state_spec, far_spec, whole((128, 128), 1), whole(pos, 1), whole(sq, 1), whole(pos, 1),
-            whole(sq, 1), columns(8),
-        ],
-        out_specs=[columns(length), state_spec],
-        compiler_params=params(True),
-        cost_estimate=cost(19),
-        name="scan",
-    )(info, xc, s_loc, swap(bnd), dpt, colt, rowst, ce, gmat, skip)
-
-    tile_spec = pl.BlockSpec((BLOCK, chans), lambda i: (i, 0))
+        )(info, normed, *weights, taps, tab_a, dpt, *before)
+
+    *own_vals, bnd_own = vals(False, (wv,), ())
+    xc, vm, ds, s_loc, bnd_other, wv_other = vals(True, wv_pieces, own_vals)
+
+    def aliases(specs, before):
+        return {len(specs) - len(before) + i: i for i in range(len(before))}
+
+    def scan(first, s0, before):
+        specs = [
+            SMEM, columns(length, first), states(first), bnd_spec, whole((128, 128), 1), whole((4,) + sq, 1), columns(8, first),
+        ] + [ANY] * len(before)
+        return pl.pallas_call(
+            functools.partial(scan_kernel, length, first),
+            grid=(hp,),
+            out_shape=[act_shape, state_shape],
+            in_specs=specs,
+            out_specs=[columns(length, first), states(first)],
+            input_output_aliases=aliases(specs, before),
+            compiler_params=params(True, 8),
+            cost_estimate=cost(10),
+            name="scan_other" if first else "scan_own",
+        )(info, xc, s_loc, s0, dpt, tab_b, skip, *before)
+
+    y, s_true = scan(0, swap(bnd_other), scan(hp, swap(bnd_own), ()))
+
     gw_shape = (2, dm // 2, dm + ch)
     out, gy, keep_a, send_a, ggate, ggain, wg_other = pl.pallas_call(
         functools.partial(gate_kernel, nb),
-        grid=(nb,),
         out_shape=[
             sds((length, dm), BF16), act_shape, sds(gw_shape, BF16), sds(gw_shape, BF16), act_shape, sds((8, chans), F32),
             sds((dm, ch), BF16),
         ],
-        in_specs=[
-            whole((length, dm), 1), whole((length, dm), 1), whole((ext, dm), 1), tile_spec, whole((ch, dm), 1),
-            whole((dm, ch), 1),
-        ] + [whole((quarter, dm + ch), 1)] * 4 + [whole((8, chans), 1)],
-        out_specs=[
-            pl.BlockSpec((BLOCK, dm), lambda i: (i, 0)), tile_spec, whole(gw_shape, 1), whole(gw_shape, 1),
-            whole((length, chans), 1), whole((8, chans), 1), whole((dm, ch), 1),
-        ],
-        scratch_shapes=[pltpu.VMEM((length, chans), BF16), pltpu.VMEM((dm, dm + ch), BF16)],
-        compiler_params=params(True),
+        in_specs=[VMEM] * 11,
+        out_specs=[VMEM] * 7,
+        scratch_shapes=[pltpu.VMEM((length, chans), BF16), pltpu.VMEM((dm, dm + ch), BF16)]
+        + [pltpu.VMEM((BLOCK, chans), F32)] * 4,
+        compiler_params=params(False, 28),
         cost_estimate=cost(22),
         name="gated",
     )(x, g, normed, y, wo, wg, *wog_pieces, gain)
@@ -1210,96 +1318,119 @@
 
     a_pieces = meet(keep_a, flip(send_a, 1, wide))
 
-    gs_loc, gbnd = pl.pallas_call(
-        functools.partial(gstate_kernel, length),
-        grid=(pairs,),
-        out_shape=[state_shape, bnd_shape],
-        in_specs=[SMEM, columns(length), whole(sq, 1), whole(sq, 1), whole((128, 128), 1)],
-        out_specs=[state_spec, bnd_spec],
-        compiler_params=params(True),
-        cost_estimate=cost(9),
-        name="gstate",
-    )(info, gy, et, cet, dpt)
-
-    gs_loc, gbnd, *a_pieces = lax.optimization_barrier((gs_loc, gbnd, *a_pieces))
+    def table(k):
+        return pl.BlockSpec((None,) + sq, lambda j: (k, 0, 0, 0))
+
+    def gstate(first, before):
+        specs = [SMEM, columns(length, first), table(0), table(2), whole((128, 128), 1)] + [ANY] * len(before)
+        return pl.pallas_call(
+            functools.partial(gstate_kernel, length, first),
+            grid=(hp,),
+            out_shape=[state_shape, bnd_shape],
+            in_specs=specs,
+            out_specs=[states(first), bnd_spec],
+            input_output_aliases=aliases(specs, before),
+            compiler_params=params(True, 6),
+            cost_estimate=cost(5),
+            name="gstate_other" if first else "gstate_own",
+        )(info, gy, tab_b, tab_c, dpt, *before)
+
+    gs_loc, gbnd_own = gstate(0, ())
+    gs_loc, gbnd_other = gstate(hp, (gs_loc,))
+
+    gs_loc, gbnd_other, *a_pieces = lax.optimization_barrier((gs_loc, gbnd_other, *a_pieces))
     a_plane = plane(*a_pieces)
 
-    gmix, ggt, gb, gct, ksum, rsum, phi, gskip = pl.pallas_call(
-        functools.partial(gscan_kernel, length),
-        grid=(pairs,),
-        out_shape=[
-            act_shape, sds(sq, F32), sds(sq, F32), sds(sq, F32), sds(pos, F32), sds(sq, F32), sds((16, chans), F32),
-            sds((8, chans), F32),
-        ],
-        in_specs=[
-            SMEM, columns(length), columns(length), columns(length), state_spec, state_spec, far_spec, whole((128, 128), 1),
-            whole(pos, 1), whole(sq, 1), whole(sq, 1), whole(sq, 1), whole(pos, 1), whole(sq, 1), columns(8),
-        ],
-        out_specs=[
-            columns(length), whole(sq, 1), whole(sq, 1), whole(sq, 1), whole(pos, 1), whole(sq, 1), columns(16), columns(8),
-        ],
-        scratch_shapes=[pltpu.VMEM((nb + 1, 128, 128), BF16)],
-        compiler_params=params(True),
-        cost_estimate=cost(35),
-        name="gscan",
-    )(info, xc, ds, gy, s_true, gs_loc, swap(gbnd), dpt, rows, coltt, et, gmat_t, bk, cet, skip)
+    def gscan(first, gs0, before):
+        sums = [whole(sq, 1), whole(sq, 1), whole(sq, 1), whole(pos, 1), whole(sq, 1)]
+        specs = [
+            SMEM, columns(length, first), columns(length, first), columns(length, first), states(first), states(first),
+            bnd_spec, whole((128, 128), 1), table(1), table(0), table(0), whole((3,) + sq, 1), columns(8, first),
+        ]
+        at = len(specs)
+        if before:
+            specs += [ANY] * 3 + sums
+        return pl.pallas_call(
+            functools.partial(gscan_kernel, length, first),
+            grid=(hp,),
+            out_shape=[
+                act_shape, sds(sq, F32), sds(sq, F32), sds(sq, F32), sds(pos, F32), sds(sq, F32), sds((16, chans), F32),
+                sds((8, chans), F32), sds((HALO, ch), BF16),
+            ],
+            in_specs=specs,
+            out_specs=[columns(length, first)] + sums + [columns(16, first), columns(8, first), columns(HALO)],
+            scratch_shapes=[pltpu.VMEM((nb + 1, 128, 128), BF16)],
+            input_output_aliases={at: 0, at + 1: 6, at + 2: 7} if before else {},
+            compiler_params=params(True, 14),
+            cost_estimate=cost(17),
+            name="gscan_other" if first else "gscan_own",
+        )(info, xc, ds, gy, s_true, gs_loc, gs0, dpt, tab_b, tab_a, tab_b, tab_c, skip, *before)
+
+    gmix, ggt, gb, gct, ksum, rsum, phi, gskip, edge_other = gscan(hp, swap(gbnd_own), ())
+    gmix, ggt, gb, gct, ksum, rsum, phi, gskip, edge_own = gscan(
+        0, swap(gbnd_other), (gmix, phi, gskip, ggt, gb, gct, ksum, rsum)
+    )
 
     gmix, ggt, a_plane = lax.optimization_barrier((gmix, ggt, a_plane))
     wa = depth(a_plane)
-    edge_x = swap(jnp.where(left, gmix[length - HALO :], gmix[:HALO]))
-
-    gmb, gv, small = pl.pallas_call(
+
+    gmb, gv, small, edge_bc = pl.pallas_call(
         functools.partial(join_kernel, length, heads),
-        out_shape=[sds((ext, 256), F32), sds(pos, BF16), sds((16, 128), F32)],
-        in_specs=[SMEM] + [VMEM] * 12,
-        out_specs=[VMEM] * 3,
+        out_shape=[sds((ext, 256), F32), sds(pos, BF16), sds((16, 128), F32), sds((HALO, 256), F32)],
+        in_specs=[SMEM] + [VMEM] * 9,
+        out_specs=[VMEM] * 4,
         scratch_shapes=[pltpu.VMEM((ext, 128), F32), pltpu.VMEM((ext, 256), F32)],
-        compiler_params=params(False),
+        compiler_params=params(False, 10),
         cost_estimate=cost(6),
         name="join",
-    )(info, ggt, gb, gct, ksum, rsum, phi, bmap, cmap, bk, dsl, a_dt, sig)
-
-    lo = HALO // 2
-    edge_bc = swap(jnp.where(left, gmb[length + lo : length + lo + HALO], gmb[lo : lo + HALO]))
-
-    keep_b, send_b, tiny, grad_in = pl.pallas_call(
+    )(info, ggt, gb, gct, ksum, rsum, phi, maps, dsl, sig)
+
+    edge_a, edge_b = swap(edge_other), swap(edge_own)
+    edge_bc = swap(edge_bc)
+    edge_at_a = pl.BlockSpec((HALO, 128), lambda j: (0, jnp.minimum(j, hp - 1)))
+    edge_at_b = pl.BlockSpec((HALO, 128), lambda j: (0, jnp.maximum(j - hp, 0)))
+
+    sum_shape = (2, dm // 2, ch)
+    keep_v, send_v, tiny, acc = pl.pallas_call(
         functools.partial(back_kernel, length, pairs),
         grid=(pairs,),
+        out_shape=[sds(sum_shape, BF16), sds(sum_shape, BF16), sds((2, 16, ch), F32), sds((length, dm), F32)],
+        in_specs=[
+            SMEM, columns(length), edge_at_a, edge_at_b, columns(ext), own_spec, own_spec, other_spec, other_spec,
+            columns(length), whole((ext, dm), 1), columns(8), columns(8), columns(8),
+        ],
+        out_specs=[whole(sum_shape, 1), whole(sum_shape, 1), whole((2, 16, ch), 1), whole((length, dm), 1)],
+        scratch_shapes=[pltpu.VMEM((ext, 128), F32), pltpu.VMEM((ext, 128), F32), pltpu.VMEM((ext, 128), jnp.int32)],
+        compiler_params=params(True, 20),
+        cost_estimate=cost(22),
+        name="back",
+    )(info, gmix, edge_a, edge_b, vm, wv, wg, wv_other, wg_other, ggate, normed, taps, ggain, gskip)
+
+    got_v = flip(send_v, 1, wide)
+    keep_bc, send_bc, tiny, grad_in = pl.pallas_call(
+        functools.partial(last_kernel, length, hl),
         out_shape=[
-            sds((2, dm // 2, ch + 384), BF16), sds((2, dm // 2, ch + 384), BF16), sds((2, 16, ch), F32), sds((length, dm), F32),
+            sds((2, dm // 2, 384), BF16), sds((2, dm // 2, 384), BF16), sds((2, 16, ch), F32), sds((length, dm), F32),
         ],
-        in_specs=[
-            SMEM, columns(length), pl.BlockSpec((HALO, 128), lambda j: (0, (j + hp) % pairs)), columns(ext), own_spec, own_spec,
-            other_spec, other_spec, columns(length), whole((ext, dm), 1), columns(8), whole((ext, 256), 1),
-            whole((HALO, 256), 1), whole((ext, 256), 1), whole((7, 256), 1), whole(pos, 1), whole((dm, 128), 1),
-            whole((dm, 256), 1), whole((length, dm), 1), whole((length, dm), 1), whole((length, 1), 1), whole((1, dm), 1),
-            columns(8), columns(8), whole((16, 128), 1),
-        ],
-        out_specs=[
-            whole((2, dm // 2, ch + 384), 1), whole((2, dm // 2, ch + 384), 1), whole((2, 16, ch), 1), whole((length, dm), 1),
-        ],
-        scratch_shapes=[
-            pltpu.VMEM((length, dm), F32), pltpu.VMEM((ext, 128), F32), pltpu.VMEM((ext, 128), F32),
-            pltpu.VMEM((ext, 128), jnp.int32),
-        ],
-        compiler_params=params(True),
-        cost_estimate=cost(24),
-        name="back",
+        in_specs=[SMEM] + [VMEM] * 15,
+        out_specs=[VMEM] * 4,
+        scratch_shapes=[pltpu.VMEM((ext, 128), F32), pltpu.VMEM((ext, 128), F32), pltpu.VMEM((ext, 128), jnp.int32)],
+        compiler_params=params(False, 16),
+        cost_estimate=cost(6),
+        name="last",
     )(
-        info, gmix, edge_x, vm, wv, wg, wv_other, wg_other, ggate, normed, taps, gmb, edge_bc, bcm, taps_bc, gv, wdt_all, wbc,
-        x, g, rs, pre_gain.reshape(1, dm), ggain, gskip, small,
+        info, acc, normed, gmb, edge_bc, bcm, taps_bc, gv, wdt_all, wbc, x, g, rs, pre_gain.reshape(1, dm), small, tiny,
     )
-
-    keep_b, send_b, wa = lax.optimization_barrier((keep_b, send_b, wa))
+    keep_bc, got_v, wa = lax.optimization_barrier((keep_bc, got_v, wa))
 
     cols = ch + 384
     wb, tiny = pl.pallas_call(
         collect_kernel,
         out_shape=[sds((share, cols), F32), sds((16, ch), F32)],
-        in_specs=[VMEM] * 3,
+        in_specs=[VMEM] * 5,
         out_specs=[VMEM] * 2,
         scratch_shapes=[
-            pltpu.VMEM((4, 2, 2 * share, cols), BF16),
+            pltpu.VMEM((4, 2, 2 * share, 384), BF16),
             pltpu.VMEM((4, share, cols), F32),
             pltpu.VMEM((4, 3, share, cols), BF16),
             pltpu.VMEM((4, 3, share, cols), BF16),
@@ -1317,13 +1448,20 @@
             pltpu.SemaphoreType.DMA((2, 3)),
             pltpu.SemaphoreType.DMA((2, 3)),
         ],
-        compiler_params=pltpu.CompilerParams(collective_id=0, has_side_effects=True, vmem_limit_bytes=VMEM_LIMIT),
+        compiler_params=pltpu.CompilerParams(collective_id=0, has_side_effects=True, vmem_limit_bytes=16 * 2**20),
         name="collect",
-    )(keep_b, send_b, tiny)
-
-    def part(v, dim):
-        size = v.shape[dim] // wide
-        return lax.dynamic_slice_in_dim(v, w * size, size, dim)
+    )(keep_v, got_v, keep_bc, send_bc, tiny)
+
+    g_conv_x, g_conv_bc, g_pre, g_bias, g_rate, g_skip, g_gain = pl.pallas_call(
+        functools.partial(finish_kernel, hl),
+        out_shape=[
+            sds((7, hl, HD // wide), F32), sds((7, 256 // wide), F32), sds((1, share), F32), sds((hl, 2), F32),
+            sds((1, hl), F32), sds((1, hl), F32), sds((hl, HD // wide), F32),
+        ],
+        in_specs=[VMEM],
+        out_specs=[VMEM] * 7,
+        name="finish",
+    )(tiny)
 
     gate_part = wa[:, dm:].reshape(share, hl, HD)
     vals_part = wb[:, :ch].reshape(share, hl, HD)
@@ -1332,19 +1470,18 @@
     dt_part = jnp.stack([dt_cols[:, 0:hl], dt_cols[:, 64 : 64 + hl]], axis=2)
     g_w_heads = jnp.concatenate([gate_part, vals_part, dt_part], axis=2)
     g_w_out = jnp.transpose(wa[:, :dm].reshape(share, hl, HD), (1, 2, 0))
-    taps_rows = tiny[11:14].reshape(3, 3, 256).reshape(9, 256)[:7]
     return (
         out[None],
         grad_in[None],
-        part(tiny[9], 0),
+        g_pre[0],
         g_w_heads,
         bc_part,
-        part(tiny[0:7].reshape(7, hl, HD), 2),
-        part(pack_columns(taps_rows), 1),
-        jnp.stack([tiny[10, 0:hl], tiny[10, 64 : 64 + hl]], axis=1),
-        tiny[10, 128 : 128 + hl] + tiny[10, 192 : 192 + hl],
-        jnp.sum(tiny[8].reshape(hl, HD), axis=1),
-        part(tiny[7].reshape(hl, HD), 1),
+        g_conv_x,
+        g_conv_bc,
+        g_bias,
+        g_rate[0],
+        g_skip[0],
+        g_gain,
         g_w_out,
     )
 

time: 247 us -> 213 us (0.86)
  Pallas kernels: 178 us -> 139 us
  local copies, waits for them, and re-layouts: 24.9 us -> 33.6 us
  other arithmetic: 9.53 us -> 2.21 us
  waiting for transfers between devices: 8.06 us -> 10.8 us
    pallas_call x5 -> x10, Pallas kernels: 87.3 us -> 68.1 us  [the longest x2 22.3 us: gscan(): pl.pallas_call(functools.partial(gscan_kernel, length, first), grid=(hp,)...]
    unnamed x38 -> x145, local copies, waits for them, and re-layouts: 9.51 us -> 22.4 us
    ppermute x11 -> x12, waiting for transfers between devices: 1.54 us -> 8.19 us  [flip(): return lax.ppermute(v, 'wide', [(i, i ^ bit) for i in range(wide)])]
    pallas_call x1, Pallas kernels: 25 us -> 18.3 us  [split_positions(): pl.pallas_call(functools.partial(back_kernel, length, pairs), grid=(pairs...]
    pallas_call x1, Pallas kernels: 31.8 us -> 27.6 us  [split_positions(): pl.pallas_call(collect_kernel, out_shape=[sds((share, cols), F32), sds((1...]
    ppermute x10 -> x11, waiting for transfers between devices: 6.52 us -> 2.61 us  [swap(): return lax.ppermute(v, 'narrow', [(0, 1), (1, 0)])]
    pallas_call x1, Pallas kernels: 8.71 us -> 5.4 us  [split_positions(): pl.pallas_call(functools.partial(front_kernel, length, hl), out_shape=[sd...]
    select_n x3 -> x0, other arithmetic: 2.94 us -> none  [the longest x1 1.37 us: split_positions(): edge = swap(jnp.where(left, x[length - HALO:], x[:HALO]))]
  transfers between devices with their start and end apart: 22 -> 24, of which waited for: 3 -> 4; matrix products, arithmetic and copies ran while one was open for 4% -> 4% of each run, Pallas kernels for 47% -> 44%
where the time goes in v3:
time: 213 us; the launch traced here: 212 us
  Pallas kernels  139 us (65%)
  local copies, waits for them, and re-layouts  33.6 us (16%)
  starting transfers between devices  24.4 us (11%)
  waiting for transfers between devices  10.8 us (5%)
  other arithmetic  2.21 us (1%)
    pallas_call x1, Pallas kernels, split_positions(): pl.pallas_call(collect_kernel, out_shape=[sds((share, cols), F32), sds((1...  27.6 us
    unnamed x145, local copies, waits for them, and re-layouts  22.4 us
    pallas_call x2, Pallas kernels, gscan(): pl.pallas_call(functools.partial(gscan_kernel, length, first), grid=(hp,)...  22.3 us
    pallas_call x1, Pallas kernels, split_positions(): pl.pallas_call(functools.partial(back_kernel, length, pairs), grid=(pairs...  18.3 us
    pallas_call x2, Pallas kernels, vals(): pl.pallas_call(functools.partial(vals_kernel, length, other), grid=(hp,),...  15.8 us
    pallas_call x2, Pallas kernels, scan(): pl.pallas_call(functools.partial(scan_kernel, length, first), grid=(hp,),...  15.7 us
    pallas_call x1, Pallas kernels, split_positions(): pl.pallas_call(functools.partial(gate_kernel, nb), out_shape=[sds((length...  15.4 us
    ppermute x11, starting transfers between devices, swap(): return lax.ppermute(v, 'narrow', [(0, 1), (1, 0)])  13.4 us
  transfers between devices with their start and end apart: 24, of which 4 were waited for; matrix products, arithmetic and copies ran while one was open for 4% of the time, Pallas kernels for 44%

profile of v3, /device:TPU:0, one launch (start us, length us, event | category | flops | bytes accessed | tf_op | source)
XLA Modules:
  0.0 212.0 jit_solution(12507097806656650165)
XLA Ops:
  0.7 2.9 %fusion.7 = (bf16[768,12,64]{0,2,1:T(8,128)(2,1)}, bf16[768,12,64]{0,2,1:T(8,128)(2,1)S(1)}) fusion(bf16[768,12,130]{0,2,1:T(8,128)(2,1)} %param.16), kind=kLoop, calls=%fused_computation.23 | loop fusion | bytes 4718592 | tf_op jit(solution)/shard_map/slice | solution.py:1194
  3.5 0.6 copy.56.refs_0_.wv_a
  4.2 0.8 constant_dynamic-slice_fusion
  5.0 3.0 %collective-permute-start.1 = (bf16[192,768]{1,0:T(8,128)(2,1)}, bf16[192,768]{1,0:T(8,128)(2,1)}, u32[]{:S(2)}, u32[]{:S(2)}) collective-permute-start(bf16[192,768]{1,0:T(8,128)(2,1)} %constant_dynamic-slice_fusion), channel_id=1, source_target_pairs={{0,1},{1,0},{2,3},{3,2},{4,5},{5,4},{6,7},{7,6},{8,9},{9,8},{10,11... | collective-permute-start | bytes 884744 | tf_op jit(solution)/shard_map/ppermute | solution.py:1130
  8.0 0.9 slice.64
  8.9 0.7 copy.54.dtb
  9.6 0.6 copy.53.conv
  10.2 0.8 copy.55.wdt
  11.1 2.2 %small.1.small_a = f32[48,768]{1,0:T(8,128)} custom-call(f32[7,12,64]{2,1,0:T(8,128)} %copy.53.conv, f32[12,64]{1,0:T(8,128)} %gain.1, f32[12,2]{1,0:T(8,128)} %copy.54.dtb, f32[12]{0:T(128)} %alog.1, f32[12]{0:T(128)} %skip.1, bf16[768,24]{1,0:T(8,128)(2,1)} %copy.55.wdt, bf16[640,768]{1,0:T(8,128)(2,1)} %bitcast.56), custom_call_target="tpu_custom_call" | custom-call | flops 2200000000 | bytes 2000000 | tf_op jit(solution)/shard_map/small/pallas_call | solution.py:1175
  13.3 1.7 copy.59.wg_a
  15.1 2.1 collective-permute-start.7
  17.2 1.6 collective-permute-start.2
  18.8 1.6 collective-permute-done.small_b
  20.4 5.4 %front.1 = (s32[8]{0:T(128)S(1)}, f32[8,1536]{1,0:T(8,128)S(1)}, f32[8,1536]{1,0:T(8,128)S(1)}, f32[8,1536]{1,0:T(8,128)S(1)}, bf16[128,768]{1,0:T(8,128)(2,1)S(...) custom-call(s32[1,4]{1,0:T(1,128)S(1)} %copy-done.15, ...), custom_call_target="tpu_custom_call" | custom-call | flops 8800000000 | bytes 8000000 | tf_op jit(solution)/shard_map/front/pallas_call | solution.py:1208
  25.8 0.9 copy-done.22
  26.8 0.9 copy-done.35
  27.7 1.0 copy-done.37
  28.7 0.9 copy-done.41
  30.2 7.6 %vals_own.1 = (bf16[640,1536]{1,0:T(8,128)(2,1)S(1)}, bf16[672,1536]{1,0:T(8,128)(2,1)S(1)}, bf16[640,1536]{1,0:T(8,128)(2,1)S(1)}, bf16[12,6,128,128]{3,2,1,0:T(8,128)(2,1)S(1)}, bf16[6,64,128]{2,1,0:T(8,128)(2,1)S(1)}) custom-call(s32[8]{0:T(128)S(1)} %get-tuple-element.107.info, bf16[672,768]{1,0:T(8,128)(2,1)S(1)} %get-tuple-element.106.normed, ...), custom_call_target="tpu_custom_call" | custom-call | flops 9900000256 | bytes 9000000 | tf_op jit(solution)/shard_map/vals_own/pallas_call | solution.py:1244
  37.9 0.8 collective-permute-start.6
  38.7 1.3 collective-permute-start.8
  40.0 8.3 %vals_other.1 = (bf16[640,1536]{1,0:T(8,128)(2,1)S(1)}, bf16[672,1536]{1,0:T(8,128)(2,1)S(1)}, bf16[640,1536]{1,0:T(8,128)(2,1)S(1)}, bf16[12,6,128,128]{3,2,1,0...) custom-call(s32[8]{0:T(128)S(1)} %get-tuple-element.107.info, ...), custom_call_target="tpu_custom_call", output_to_operand_aliasing={{0}: (9, {}), {1}: (10, {}), {2}: (11, {}), {3}: (12, {})} | custom-call | flops 9900000256 | bytes 9000000 | tf_op jit(solution)/shard_map/vals_other/pallas_call | solution.py:1244
  48.3 1.4 collective-permute-start.5
  49.7 7.8 %scan_other.1 = (bf16[640,1536]{1,0:T(8,128)(2,1)S(1)}, bf16[12,6,128,128]{3,2,1,0:T(8,128)(2,1)S(1)}) custom-call(s32[8]{0:T(128)S(1)} %get-tuple-element.107.info, bf16[640,1536]{1,0:T(8,128)(2,1)S(1)} %get-tuple-element.115.xc_ref, bf16[12,6,128,128]{3,2,1,0:T(8,128)(2,1)S(1)} %get-tuple-element.116.s_ref, ...), custom_call_target="tpu_custom_call" | custom-call | flops 11000000512 | bytes 10000000 | tf_op jit(solution)/shard_map/scan_other/pallas_call | solution.py:1270
  57.7 7.9 %scan_own.1 = (bf16[640,1536]{1,0:T(8,128)(2,1)S(1)}, bf16[12,6,128,128]{3,2,1,0:T(8,128)(2,1)S(1)}) custom-call(s32[8]{0:T(128)S(1)} %get-tuple-element.107.info, bf16[640,1536]{1,0:T(8,128)(2,1)S(1)} %get-tuple-element.115.xc_ref, bf16[12,6,128,128]{3,2,1,0:T(8,128)(2,1)S(1)} %get-tuple-element.116.s_ref, ...), custom_call_target="tpu_custom_call", output_to_operand_aliasing={{0}: (7, {}), {1}: (8, {})} | custom-call | flops 11000000512 | bytes 10000000 | tf_op jit(solution)/shard_map/scan_own/pallas_call | solution.py:1270
  65.6 1.4 copy-done.33
  67.0 15.4 %gated.1 = (bf16[640,768]{1,0:T(8,128)(2,1)}, bf16[640,1536]{1,0:T(8,128)(2,1)S(1)}, bf16[2,384,1536]{2,1,0:T(8,128)(2,1)S(1)}, bf16[2,384,1536]{2,1,0:T(8,128)(...) custom-call(bf16[640,768]{1,0:T(8,128)(2,1)S(1)} %bitcast.58, ...), custom_call_target="tpu_custom_call" | custom-call | flops 24199999488 | bytes 22000000 | tf_op jit(solution)/shard_map/gated/pallas_call | solution.py:1285
  82.4 1.3 copy-done.16
  83.7 1.3 copy-done.56
  85.0 1.0 copy-done.58
  87.1 1.5 copy-done.17
  88.7 1.3 copy-done.20
  90.0 1.2 copy-done.23
  91.2 0.8 copy-done.54
  92.0 2.3 %gstate_own.1 = (bf16[12,6,128,128]{3,2,1,0:T(8,128)(2,1)S(1)}, bf16[6,64,128]{2,1,0:T(8,128)(2,1)S(1)}) custom-call(s32[8]{0:T(128)S(1)} %get-tuple-element.107.info, bf16[640,1536]{1,0:T(8,128)(2,1)S(1)} %copy-done.17, f32[4,5,128,128]{3,2,1,0:T(8,128)S(1)} %copy-done.20, f32[3,5,128,128]{3,2,1,0:T(8,128)S(1)} %copy-done.23, f32[128,128]{1,0:T(8,128)S(1)} %copy-done.54), custom_call_target="tpu_custom_call" | custom-call | flops 5500000256 | bytes 5000000 | tf_op jit(solution)/shard_map/gstate_own/pallas_call | solution.py:1326
  94.4 0.8 collective-permute-start.13
  95.2 2.3 %gstate_other.1 = (bf16[12,6,128,128]{3,2,1,0:T(8,128)(2,1)S(1)}, bf16[6,64,128]{2,1,0:T(8,128)(2,1)S(1)}) custom-call(s32[8]{0:T(128)S(1)} %get-tuple-element.107.info, bf16[640,1536]{1,0:T(8,128)(2,1)S(1)} %copy-done.17, f32[4,5,128,128]{3,2,1,0:T(8,128)S(1)} %copy-done.20, f32[3,5,128,128]{3,2,1,0:T(8,128)S(1)} %copy-done.23, ...), custom_call_target="tpu_custom_call", output_to_operand_aliasing={{0}: (5, {})} | custom-call | flops 5500000256 | bytes 5000000 | tf_op jit(solution)/shard_map/gstate_other/pallas_call | solution.py:1326
  97.7 1.9 fusion.9
  99.7 0.7 fusion.1
  100.4 1.4 collective-permute-start.12
  101.8 0.7 collective-permute-start.14
  102.5 0.7 collective-permute-start.15
  103.3 2.0 collective-permute-start.16
  105.4 11.2 %gscan_other.1 = (bf16[640,1536]{1,0:T(8,128)(2,1)S(1)}, f32[5,128,128]{2,1,0:T(8,128)S(1)}, f32[5,128,128]{2,1,0:T(8,128)S(1)}, f32[5,128,128]{2,1,0:T(8,128)S(...) custom-call(s32[8]{0:T(128)S(1)} %get-tuple-element.107.info, ...), custom_call_target="tpu_custom_call" | custom-call | flops 18699999232 | bytes 17000000 | tf_op jit(solution)/shard_map/gscan_other/pallas_call | solution.py:1353
  116.6 0.8 collective-permute-start.17
  117.4 11.1 %gscan_own.1 = (bf16[640,1536]{1,0:T(8,128)(2,1)S(1)}, f32[5,128,128]{2,1,0:T(8,128)S(1)}, f32[5,128,128]{2,1,0:T(8,128)S(1)}, f32[5,128,128]{2,1,0:T(8,128)S(1)...) custom-call(s32[8]{0:T(128)S(1)} %get-tuple-element.107.info, ...), custom_call_target="tpu_custom_call", output_to_operand_aliasing={{0}: (13, {}), {6}: (14, {}), {7}: (15, {})} | custom-call | flops 18699999232 | bytes 17000000 | tf_op jit(solution)/shard_map/gscan_own/pallas_call | solution.py:1353
  128.5 1.4 collective-permute-start.18
  129.9 1.0 collective-permute-done.15
  131.3 4.0 %join.1 = (f32[672,256]{1,0:T(8,128)S(1)}, bf16[640,128]{1,0:T(8,128)(2,1)S(1)}, f32[16,128]{1,0:T(8,128)S(1)}, f32[16,256]{1,0:T(8,128)S(1)}) custom-call(s32[8]{0:T(128)S(1)} %get-tuple-element.107.info, f32[5,128,128]{2,1,0:T(8,128)S(1)} %get-tuple-element.162.ggt, f32[5,128,128]{2,1,0:T(8,128)S(1)} %get-tuple-element.163.gb, ...), custom_call_target="tpu_custom_call" | custom-call | flops 6600000000 | bytes 6000000 | tf_op jit(solution)/shard_map/join/pallas_call | solution.py:1377
  135.3 1.1 collective-permute-start.19
  136.6 18.3 %back.1 = (bf16[2,384,768]{2,1,0:T(8,128)(2,1)S(1)}, bf16[2,384,768]{2,1,0:T(8,128)(2,1)S(1)}, f32[2,16,768]{2,1,0:T(8,128)S(1)}, f32[640,768]{1,0:T(8,128)S(1)}) custom-call(s32[8]{0:T(128)S(1)} %get-tuple-element.107.info, bf16[640,1536]{1,0:T(8,128)(2,1)S(1)} %get-tuple-element.152.gmix, bf16[16,768]{1,0:T(8,128)(2,1)S(1)} %collective-permute-done.17.edge_a, ...), custom_call_target="tpu_custom_call" | custom-call | flops 24199999488 | bytes 22000000 | tf_op jit(solution)/shard_map/back/pallas_call | solution.py:1394
  155.1 1.6 collective-permute-start.21
  156.7 2.5 %collective-permute-start.23 = (bf16[48,1536]{1,0:T(8,128)(2,1)S(1)}, bf16[48,1536]{1,0:T(8,128)(2,1)S(1)}, u32[]{:S(2)}, u32[]{:S(2)}) collective-permute-start(bf16[48,1536]{1,0:T(8,128)(2,1)S(1)} %get-tuple-element.235), channel_id=1, source_target_pairs={{0,24},{2,26},{4,28},{6,30},{8,16},{10,18},{12,20},{14,22},{16,8},... | collective-permute-start | bytes 442376 | tf_op jit(solution)/shard_map/ppermute | solution.py:1134
  159.4 5.5 %last.1 = (bf16[2,384,384]{2,1,0:T(8,128)(2,1)S(1)}, bf16[2,384,384]{2,1,0:T(8,128)(2,1)S(1)}, f32[2,16,768]{2,1,0:T(8,128)S(1)}, f32[640,768]{1,0:T(8,128)}) custom-call(s32[8]{0:T(128)S(1)} %get-tuple-element.107.info, f32[640,768]{1,0:T(8,128)S(1)} %get-tuple-element.161.acc, bf16[672,768]{1,0:T(8,128)(2,1)S(1)} %copy-done.26, ...), custom_call_target="tpu_custom_call" | custom-call | flops 6600000000 | bytes 6000000 | tf_op jit(solution)/shard_map/last/pallas_call | solution.py:1410
  164.8 2.2 %collective-permute-done.23 = bf16[48,1536]{1,0:T(8,128)(2,1)S(1)} collective-permute-done((bf16[48,1536]{1,0:T(8,128)(2,1)S(1)}, bf16[48,1536]{1,0:T(8,128)(2,1)S(1)}, u32[]{:S(2)}, u32[]{:S(2)}) %collective-permute-start.23) | collective-permute-done | bytes 147488 | tf_op jit(solution)/shard_map/ppermute | solution.py:1134
  167.1 5.9 %collective-permute-done.22 = bf16[48,1536]{1,0:T(8,128)(2,1)S(1)} collective-permute-done((bf16[48,1536]{1,0:T(8,128)(2,1)S(1)}, bf16[48,1536]{1,0:T(8,128)(2,1)S(1)}, u32[]{:S(2)}, u32[]{:S(2)}) %collective-permute-start.22) | collective-permute-done | bytes 147488 | tf_op jit(solution)/shard_map/ppermute | solution.py:1134
  173.1 27.6 %collect.1 = (f32[48,1152]{1,0:T(8,128)S(1)}, f32[16,768]{1,0:T(8,128)S(1)}) custom-call(bf16[2,384,768]{2,1,0:T(8,128)(2,1)S(1)} %get-tuple-element.182.keep, bf16[2,384,768]{2,1,0:T(8,128)(2,1)S(1)} %collective-permute-done.20.got_v, bf16[2,384,384]{2,1,0:T(8,128)(2,1)S(1)} %get-tuple-element.187.keep_bc, ...), custom_call_target="tpu_custom_call" | custom-call | tf_op jit(solution)/shard_map/collect/pallas_call | solution.py:1427
  201.3 2.2 %finish.1 = (f32[7,12,4]{2,1,0:T(8,128)}, f32[7,16]{1,0:T(8,128)}, f32[1,48]{1,0:T(1,128)}, f32[12,2]{1,0:T(8,128)}, f32[1,12]{1,0:T(1,128)}, /*index=5*/f32[1,12]{1,0:T(1,128)}, f32[12,4]{1,0:T(8,128)}) custom-call(f32[16,768]{1,0:T(8,128)} %copy-done.4), custom_call_target="tpu_custom_call" | custom-call | tf_op jit(solution)/shard_map/finish/pallas_call | solution.py:1455
  203.5 1.3 copy.74
  204.8 1.4 copy.75
  206.2 1.5 copy.73
  208.0 0.8 copy.76
  210.1 1.2 copy.72
  211.3 0.7 pad_maximum_fusion.1
  (171 shorter events, 5.1 us)
Async XLA Ops:
  3.5 6.1 %copy-start.66 = (f32[7,12,64]{2,0,1:T(8,128)S(1)}, f32[7,12,64]{2,0,1:T(8,128)}, u32[]{:S(2)}) copy-start(f32[7,12,64]{2,0,1:T(8,128)} %param.18) | copy-start | bytes 64516
  4.2 26.1 %copy-start = (bf16[768,768]{1,0:T(8,128)(2,1)}, bf16[768,768]{1,0:T(8,128)(2,1)S(1)}, u32[]{:S(2)}) copy-start(bf16[768,768]{1,0:T(8,128)(2,1)S(1)} %copy.56.refs_0_.wv_a) | copy-start | bytes 3538948
  5.0 12.2 %collective-permute-start.1 = (bf16[192,768]{1,0:T(8,128)(2,1)}, bf16[192,768]{1,0:T(8,128)(2,1)}, u32[]{:S(2)}, u32[]{:S(2)}) collective-permute-start(bf16[192,768]{1,0:T(8,128)(2,1)} %constant_dynamic-slice_fusion), channel_id=1, source_target_pairs={{0,1},{1,0},{2,3},{3,2},{4,5},{5,4},{6,7},{7,6},{8,9},{9,8},{10,11... | collective-permute-start | bytes 884744 | tf_op jit(solution)/shard_map/ppermute | solution.py:1130
  13.3 7.1 %collective-permute-start = (f32[48,768]{1,0:T(8,128)}, f32[48,768]{1,0:T(8,128)}, u32[]{:S(2)}, u32[]{:S(2)}) collective-permute-start(f32[48,768]{1,0:T(8,128)} %small.1.small_a), channel_id=1, source_target_pairs={{0,1},{1,0},{2,3},{3,2},{4,5},{5,4},{6,7},{7,6},{8,9},{9,8},{10,11... | collective-permute-start | bytes 442376 | tf_op jit(solution)/shard_map/ppermute | solution.py:1130
  15.0 5.4 %copy-start.7 = (bf16[1,640,768]{2,1,0:T(8,128)(2,1)S(1)}, bf16[1,640,768]{2,1,0:T(8,128)(2,1)}, u32[]{:S(2)}) copy-start(bf16[1,640,768]{2,1,0:T(8,128)(2,1)} %param.14) | copy-start | bytes 2949124
  15.0 5.4 %copy-start.11 = (bf16[768,256]{1,0:T(8,128)(2,1)S(1)}, bf16[768,256]{1,0:T(8,128)(2,1)}, u32[]{:S(2)}) copy-start(bf16[768,256]{1,0:T(8,128)(2,1)} %wbc_ref.1) | copy-start | bytes 1179652
  15.0 5.4 %copy-start.12 = (f32[48,768]{1,0:T(8,128)S(1)}, f32[48,768]{1,0:T(8,128)}, u32[]{:S(2)}) copy-start(f32[48,768]{1,0:T(8,128)} %small.1.small_a) | copy-start | bytes 442372
  15.0 5.4 %copy-start.13 = (f32[7,256]{1,0:T(8,128)S(1)}, f32[7,256]{1,0:T(8,128)}, u32[]{:S(2)}) copy-start(f32[7,256]{1,0:T(8,128)} %taps_ref.1) | copy-start | bytes 21508
  15.0 5.4 %copy-start.14 = (s32[1,1280]{1,0:T(1,128)S(1)}, s32[1,1280]{1,0:T(1,128)}, u32[]{:S(2)}) copy-start(s32[1,1280]{1,0:T(1,128)} %live_ref.1) | copy-start | bytes 15364
  15.1 23.6 %collective-permute-start.7 = (bf16[192,1536]{1,0:T(8,128)(2,1)S(1)}, bf16[192,1536]{1,0:T(8,128)(2,1)S(1)}, u32[]{:S(2)}, u32[]{:S(2)}) collective-permute-start(bf16[192,1536]{1,0:T(8,128)(2,1)S(1)} %fusion.4), channel_id=1, source_target_pairs={{0,1},{1,0},{2,3},{3,2},{4,5},{5,4},{6,7},{7,6},{8,9},{9,8},{10,11... | collective-permute-start | bytes 1769480 | tf_op jit(solution)/shard_map/ppermute | solution.py:1130
  17.2 8.6 %copy-start.5 = (f32[1,768]{1,0:T(1,128)}, f32[1,768]{1,0:T(1,128)S(1)}, u32[]{:S(2)}) copy-start(f32[1,768]{1,0:T(1,128)S(1)} %reshape.77.gain.pre) | copy-start | bytes 9220
  17.2 12.5 %collective-permute-start.2 = (bf16[192,768]{1,0:T(8,128)(2,1)}, bf16[192,768]{1,0:T(8,128)(2,1)S(1)}, u32[]{:S(2)}, u32[]{:S(2)}) collective-permute-start(bf16[192,768]{1,0:T(8,128)(2,1)} %collective-permute-done.1.refs_0_), channel_id=1, source_target_pairs={{0,4},{2,6},{4,0},{6,2},{8,12},{10,14},{12,8},{14,10},{16,20},{18,... | collective-permute-start | bytes 884744 | tf_op jit(solution)/shard_map/ppermute | solution.py:1134
  29.6 8.2 %copy-start.43 = (bf16[768,256]{1,0:T(8,128)(2,1)}, bf16[768,256]{1,0:T(8,128)(2,1)S(1)}, u32[]{:S(2)}) copy-start(bf16[768,256]{1,0:T(8,128)(2,1)S(1)} %get-tuple-element.177.wbc) | copy-start | bytes 1179652
  29.6 8.3 %copy-start.45 = (f32[640,1]{1,0:T(8,128)}, f32[640,1]{1,0:T(8,128)S(1)}, u32[]{:S(2)}) copy-start(f32[640,1]{1,0:T(8,128)S(1)} %get-tuple-element.178.rs) | copy-start | bytes 7684
  29.6 8.3 %copy-start.49 = (bf16[640,256]{1,0:T(8,128)(2,1)}, bf16[640,256]{1,0:T(8,128)(2,1)S(1)}, u32[]{:S(2)}) copy-start(bf16[640,256]{1,0:T(8,128)(2,1)S(1)} %get-tuple-element.168.maps) | copy-start | bytes 983044
  29.6 8.3 %copy-start.51 = (bf16[128,768]{1,0:T(8,128)(2,1)}, bf16[128,768]{1,0:T(8,128)(2,1)S(1)}, u32[]{:S(2)}) copy-start(bf16[128,768]{1,0:T(8,128)(2,1)S(1)} %get-tuple-element.176.wdt) | copy-start | bytes 589828
  29.6 10.4 %copy-start.47 = (f32[2,5,128,128]{3,2,1,0:T(8,128)}, f32[2,5,128,128]{3,2,1,0:T(8,128)S(1)}, u32[]{:S(2)}) copy-start(f32[2,5,128,128]{3,2,1,0:T(8,128)S(1)} %get-tuple-element.109.refs_2_.refs_5_.wt) | copy-start | bytes 1966084
  29.6 10.3 %copy-start.60 = (f32[8,1536]{1,0:T(8,128)}, f32[8,1536]{1,0:T(8,128)S(1)}, u32[]{:S(2)}) copy-start(f32[8,1536]{1,0:T(8,128)S(1)} %get-tuple-element.108.refs_1_.refs_4_.taps) | copy-start | bytes 147460
  29.6 28.0 %copy-start.19 = (f32[4,5,128,128]{3,2,1,0:T(8,128)}, f32[4,5,128,128]{3,2,1,0:T(8,128)S(1)}, u32[]{:S(2)}) copy-start(f32[4,5,128,128]{3,2,1,0:T(8,128)S(1)} %get-tuple-element.118.tb.coltt.rowst) | copy-start | bytes 3932164
  29.6 28.0 %copy-start.53 = (f32[128,128]{1,0:T(8,128)}, f32[128,128]{1,0:T(8,128)S(1)}, u32[]{:S(2)}) copy-start(f32[128,128]{1,0:T(8,128)S(1)} %get-tuple-element.110.refs_3_.refs_6_.dpt) | copy-start | bytes 196612
  29.6 28.0 %copy-start.62 = (f32[8,1536]{1,0:T(8,128)}, f32[8,1536]{1,0:T(8,128)S(1)}, u32[]{:S(2)}) copy-start(f32[8,1536]{1,0:T(8,128)S(1)} %get-tuple-element.119.skip) | copy-start | bytes 147460
  29.6 37.3 %copy-start.25 = (bf16[672,768]{1,0:T(8,128)(2,1)}, bf16[672,768]{1,0:T(8,128)(2,1)S(1)}, u32[]{:S(2)}) copy-start(bf16[672,768]{1,0:T(8,128)(2,1)S(1)} %get-tuple-element.106.normed) | copy-start | bytes 3096580
  29.7 10.3 %collective-permute-start.3 = (bf16[192,768]{1,0:T(8,128)(2,1)}, bf16[192,768]{1,0:T(8,128)(2,1)S(1)}, u32[]{:S(2)}, u32[]{:S(2)}) collective-permute-start(bf16[192,768]{1,0:T(8,128)(2,1)} %collective-permute-done.1.refs_0_), channel_id=1, source_target_pairs={{0,2},{2,0},{4,6},{6,4},{8,10},{10,8},{12,14},{14,12},{16,18},{18,... | collective-permute-start | bytes 884744 | tf_op jit(solution)/shard_map/ppermute | solution.py:1134
  29.7 10.2 %collective-permute-start.4 = (bf16[192,768]{1,0:T(8,128)(2,1)S(1)}, bf16[192,768]{1,0:T(8,128)(2,1)S(1)}, u32[]{:S(2)}, u32[]{:S(2)}) collective-permute-start(bf16[192,768]{1,0:T(8,128)(2,1)S(1)} %collective-permute-done.2.refs_1_), channel_id=1, source_target_pairs={{0,2},{2,0},{4,6},{6,4},{8,10},{10,8},{12,14},{14,12},{16,18},{18,... | collective-permute-start | bytes 884744 | tf_op jit(solution)/shard_map/ppermute | solution.py:1134
  37.9 11.8 %collective-permute-start.6 = (bf16[6,64,128]{2,1,0:T(8,128)(2,1)S(1)}, bf16[6,64,128]{2,1,0:T(8,128)(2,1)S(1)}, u32[]{:S(2)}, u32[]{:S(2)}) collective-permute-start(bf16[6,64,128]{2,1,0:T(8,128)(2,1)S(1)} %get-tuple-element.120), channel_id=1, source_target_pairs={{0,1},{1,0},{2,3},{3,2},{4,5},{5,4},{6,7},{7,6},{8,9},{9,8},{10,11... | collective-permute-start | bytes 294920 | tf_op jit(solution)/shard_map/ppermute | solution.py:1130
  38.7 28.3 %collective-permute-start.9 = (bf16[192,1536]{1,0:T(8,128)(2,1)S(1)}, bf16[192,1536]{1,0:T(8,128)(2,1)S(1)}, u32[]{:S(2)}, u32[]{:S(2)}) collective-permute-start(bf16[192,1536]{1,0:T(8,128)(2,1)S(1)} %collective-permute-done.7.p0), channel_id=1, source_target_pairs={{0,2},{2,0},{4,6},{6,4},{8,10},{10,8},{12,14},{14,12},{16,18},{18,... | collective-permute-start | bytes 1769480 | tf_op jit(solution)/shard_map/ppermute | solution.py:1134
  38.7 18.9 %collective-permute-start.8 = (bf16[192,1536]{1,0:T(8,128)(2,1)S(1)}, bf16[192,1536]{1,0:T(8,128)(2,1)S(1)}, u32[]{:S(2)}, u32[]{:S(2)}) collective-permute-start(bf16[192,1536]{1,0:T(8,128)(2,1)S(1)} %collective-permute-done.7.p0), channel_id=1, source_target_pairs={{0,4},{2,6},{4,0},{6,2},{8,12},{10,14},{12,8},{14,10},{16,20},{18,... | collective-permute-start | bytes 1769480 | tf_op jit(solution)/shard_map/ppermute | solution.py:1134
  48.2 9.3 %copy-start.27 = (bf16[672,1536]{1,0:T(8,128)(2,1)}, bf16[672,1536]{1,0:T(8,128)(2,1)S(1)}, u32[]{:S(2)}) copy-start(bf16[672,1536]{1,0:T(8,128)(2,1)S(1)} %get-tuple-element.155.vm) | copy-start | bytes 6193156
  48.2 9.3 %copy-start.31 = (bf16[640,1536]{1,0:T(8,128)(2,1)}, bf16[640,1536]{1,0:T(8,128)(2,1)S(1)}, u32[]{:S(2)}) copy-start(bf16[640,1536]{1,0:T(8,128)(2,1)S(1)} %get-tuple-element.126.ds_ref) | copy-start | bytes 5898244
  48.3 9.3 %copy-start.39 = (bf16[768,768]{1,0:T(8,128)(2,1)}, bf16[768,768]{1,0:T(8,128)(2,1)S(1)}, u32[]{:S(2)}) copy-start(bf16[768,768]{1,0:T(8,128)(2,1)S(1)} %get-tuple-element.156.wv_b) | copy-start | bytes 3538948
  48.3 9.4 %copy-start.29 = (bf16[640,1536]{1,0:T(8,128)(2,1)}, bf16[640,1536]{1,0:T(8,128)(2,1)S(1)}, u32[]{:S(2)}) copy-start(bf16[640,1536]{1,0:T(8,128)(2,1)S(1)} %get-tuple-element.115.xc_ref) | copy-start | bytes 5898244
  48.3 9.4 %collective-permute-start.5 = (bf16[6,64,128]{2,1,0:T(8,128)(2,1)S(1)}, bf16[6,64,128]{2,1,0:T(8,128)(2,1)S(1)}, u32[]{:S(2)}, u32[]{:S(2)}) collective-permute-start(bf16[6,64,128]{2,1,0:T(8,128)(2,1)S(1)} %get-tuple-element.117), channel_id=1, source_target_pairs={{0,1},{1,0},{2,3},{3,2},{4,5},{5,4},{6,7},{7,6},{8,9},{9,8},{10,11... | collective-permute-start | bytes 294920 | tf_op jit(solution)/shard_map/ppermute | solution.py:1130
  57.5 9.4 %collective-permute-start.10 = (bf16[192,1536]{1,0:T(8,128)(2,1)S(1)}, bf16[192,1536]{1,0:T(8,128)(2,1)S(1)}, u32[]{:S(2)}, u32[]{:S(2)}) collective-permute-start(bf16[192,1536]{1,0:T(8,128)(2,1)S(1)} %collective-permute-done.8.p1), channel_id=1, source_target_pairs={{0,2},{2,0},{4,6},{6,4},{8,10},{10,8},{12,14},{14,12},{16,18},{18,... | collective-permute-start | bytes 1769480 | tf_op jit(solution)/shard_map/ppermute | solution.py:1134
  57.7 9.3 %copy-start.3 = (bf16[12,64,768]{2,1,0:T(8,128)(2,1)S(1)}, bf16[12,64,768]{2,1,0:T(8,128)(2,1)}, u32[]{:S(2)}) copy-start(bf16[12,64,768]{2,1,0:T(8,128)(2,1)} %param.24) | copy-start | bytes 3538948
  57.7 9.3 %copy-start.9 = (bf16[1,640,768]{2,1,0:T(8,128)(2,1)S(1)}, bf16[1,640,768]{2,1,0:T(8,128)(2,1)}, u32[]{:S(2)}) copy-start(bf16[1,640,768]{2,1,0:T(8,128)(2,1)} %param.25) | copy-start | bytes 2949124
  86.6 11.0 %collective-permute-start.11 = (bf16[2,384,1536]{2,1,0:T(8,128)(2,1)}, bf16[2,384,1536]{2,1,0:T(8,128)(2,1)}, u32[]{:S(2)}, u32[]{:S(2)}) collective-permute-start(bf16[2,384,1536]{2,1,0:T(8,128)(2,1)} %get-tuple-element.134), channel_id=1, source_target_pairs={{0,2},{2,0},{4,6},{6,4},{8,10},{10,8},{12,14},{14,12},{16,18},{18,... | collective-permute-start | bytes 7077896 | tf_op jit(solution)/shard_map/ppermute | solution.py:1134
  94.4 10.9 %collective-permute-start.13 = (bf16[6,64,128]{2,1,0:T(8,128)(2,1)S(1)}, bf16[6,64,128]{2,1,0:T(8,128)(2,1)S(1)}, u32[]{:S(2)}, u32[]{:S(2)}) collective-permute-start(bf16[6,64,128]{2,1,0:T(8,128)(2,1)S(1)} %get-tuple-element.137), channel_id=1, source_target_pairs={{0,1},{1,0},{2,3},{3,2},{4,5},{5,4},{6,7},{7,6},{8,9},{9,8},{10,11... | collective-permute-start | bytes 294920 | tf_op jit(solution)/shard_map/ppermute | solution.py:1130
  97.7 7.6 %copy-start.32 = (bf16[640,1536]{1,0:T(8,128)(2,1)S(1)}, bf16[640,1536]{1,0:T(8,128)(2,1)}, u32[]{:S(2)}) copy-start(bf16[640,1536]{1,0:T(8,128)(2,1)} %copy-done.31) | copy-start | bytes 5898244
  97.7 7.6 %copy-start.34 = (bf16[12,6,128,128]{3,2,1,0:T(8,128)(2,1)S(1)}, bf16[12,6,128,128]{3,2,1,0:T(8,128)(2,1)}, u32[]{:S(2)}) copy-start(bf16[12,6,128,128]{3,2,1,0:T(8,128)(2,1)} %copy-done.33) | copy-start | bytes 7077892
  99.6 5.7 %copy-start.18 = (bf16[640,1536]{1,0:T(8,128)(2,1)S(1)}, bf16[640,1536]{1,0:T(8,128)(2,1)}, u32[]{:S(2)}) copy-start(bf16[640,1536]{1,0:T(8,128)(2,1)} %copy-done.16) | copy-start | bytes 5898244
  99.6 5.7 %copy-start.21 = (f32[4,5,128,128]{3,2,1,0:T(8,128)S(1)}, f32[4,5,128,128]{3,2,1,0:T(8,128)}, u32[]{:S(2)}) copy-start(f32[4,5,128,128]{3,2,1,0:T(8,128)} %copy-done.19) | copy-start | bytes 3932164
  99.6 5.7 %copy-start.24 = (f32[3,5,128,128]{3,2,1,0:T(8,128)S(1)}, f32[3,5,128,128]{3,2,1,0:T(8,128)}, u32[]{:S(2)}) copy-start(f32[3,5,128,128]{3,2,1,0:T(8,128)} %copy-done.22) | copy-start | bytes 2949124
  99.7 5.7 %copy-start.30 = (bf16[640,1536]{1,0:T(8,128)(2,1)S(1)}, bf16[640,1536]{1,0:T(8,128)(2,1)}, u32[]{:S(2)}) copy-start(bf16[640,1536]{1,0:T(8,128)(2,1)} %copy-done.29) | copy-start | bytes 5898244
  99.7 5.7 %copy-start.48 = (f32[2,5,128,128]{3,2,1,0:T(8,128)S(1)}, f32[2,5,128,128]{3,2,1,0:T(8,128)}, u32[]{:S(2)}) copy-start(f32[2,5,128,128]{3,2,1,0:T(8,128)} %copy-done.47) | copy-start | bytes 1966084
  99.7 5.7 %copy-start.55 = (f32[128,128]{1,0:T(8,128)S(1)}, f32[128,128]{1,0:T(8,128)}, u32[]{:S(2)}) copy-start(f32[128,128]{1,0:T(8,128)} %copy-done.53) | copy-start | bytes 196612
  99.7 5.7 %copy-start.63 = (f32[8,1536]{1,0:T(8,128)S(1)}, f32[8,1536]{1,0:T(8,128)}, u32[]{:S(2)}) copy-start(f32[8,1536]{1,0:T(8,128)} %copy-done.62) | copy-start | bytes 147460
  100.4 17.0 %collective-permute-start.12 = (bf16[6,64,128]{2,1,0:T(8,128)(2,1)S(1)}, bf16[6,64,128]{2,1,0:T(8,128)(2,1)S(1)}, u32[]{:S(2)}, u32[]{:S(2)}) collective-permute-start(bf16[6,64,128]{2,1,0:T(8,128)(2,1)S(1)} %get-tuple-element.136), channel_id=1, source_target_pairs={{0,1},{1,0},{2,3},{3,2},{4,5},{5,4},{6,7},{7,6},{8,9},{9,8},{10,11... | collective-permute-start | bytes 294920 | tf_op jit(solution)/shard_map/ppermute | solution.py:1130
  101.8 28.1 %collective-permute-start.14 = (bf16[4,48,1536]{2,1,0:T(8,128)(2,1)S(1)}, bf16[4,48,1536]{2,1,0:T(8,128)(2,1)S(1)}, u32[]{:S(2)}, u32[]{:S(2)}) collective-permute-start(bf16[4,48,1536]{2,1,0:T(8,128)(2,1)S(1)} %get-tuple-element.149), channel_id=1, source_target_pairs={{0,4},{2,6},{4,0},{6,2},{8,12},{10,14},{12,8},{14,10},{16,20},{18,... | collective-permute-start | bytes 1769480 | tf_op jit(solution)/shard_map/ppermute | solution.py:1134
  102.5 28.4 %collective-permute-start.15 = (bf16[4,48,1536]{2,1,0:T(8,128)(2,1)S(1)}, bf16[4,48,1536]{2,1,0:T(8,128)(2,1)S(1)}, u32[]{:S(2)}, u32[]{:S(2)}) collective-permute-start(bf16[4,48,1536]{2,1,0:T(8,128)(2,1)S(1)} %get-tuple-element.150), channel_id=1, source_target_pairs={{0,1},{1,0},{2,3},{3,2},{4,5},{5,4},{6,7},{7,6},{8,9},{9,8},{10,11... | collective-permute-start | bytes 1769480 | tf_op jit(solution)/shard_map/ppermute | solution.py:1130
  103.3 27.6 %collective-permute-start.16 = (bf16[4,48,1536]{2,1,0:T(8,128)(2,1)S(1)}, bf16[4,48,1536]{2,1,0:T(8,128)(2,1)S(1)}, u32[]{:S(2)}, u32[]{:S(2)}) collective-permute-start(bf16[4,48,1536]{2,1,0:T(8,128)(2,1)S(1)} %get-tuple-element.151), channel_id=1, source_target_pairs={{0,5},{1,4},{2,7},{3,6},{4,1},{5,0},{6,3},{7,2},{8,13},{9,12},{10,... | collective-permute-start | bytes 1769480 | tf_op jit(solution)/shard_map/ppermute | solution.py:1139
  116.6 19.8 %collective-permute-start.17 = (bf16[16,768]{1,0:T(8,128)(2,1)S(1)}, bf16[16,768]{1,0:T(8,128)(2,1)S(1)}, u32[]{:S(2)}, u32[]{:S(2)}) collective-permute-start(bf16[16,768]{1,0:T(8,128)(2,1)S(1)} %get-tuple-element.153), channel_id=1, source_target_pairs={{0,1},{1,0},{2,3},{3,2},{4,5},{5,4},{6,7},{7,6},{8,9},{9,8},{10,11... | collective-permute-start | bytes 73736 | tf_op jit(solution)/shard_map/ppermute | solution.py:1130
  128.5 7.9 %collective-permute-start.18 = (bf16[16,768]{1,0:T(8,128)(2,1)S(1)}, bf16[16,768]{1,0:T(8,128)(2,1)S(1)}, u32[]{:S(2)}, u32[]{:S(2)}) collective-permute-start(bf16[16,768]{1,0:T(8,128)(2,1)S(1)} %get-tuple-element.154), channel_id=1, source_target_pairs={{0,1},{1,0},{2,3},{3,2},{4,5},{5,4},{6,7},{7,6},{8,9},{9,8},{10,11... | collective-permute-start | bytes 73736 | tf_op jit(solution)/shard_map/ppermute | solution.py:1130
  135.3 24.0 %collective-permute-start.19 = (f32[16,256]{1,0:T(8,128)S(1)}, f32[16,256]{1,0:T(8,128)S(1)}, u32[]{:S(2)}, u32[]{:S(2)}) collective-permute-start(f32[16,256]{1,0:T(8,128)S(1)} %get-tuple-element.172), channel_id=1, source_target_pairs={{0,1},{1,0},{2,3},{3,2},{4,5},{5,4},{6,7},{7,6},{8,9},{9,8},{10,11... | collective-permute-start | bytes 49160 | tf_op jit(solution)/shard_map/ppermute | solution.py:1130
  136.5 22.8 %copy-start.6 = (f32[1,768]{1,0:T(1,128)S(1)}, f32[1,768]{1,0:T(1,128)}, u32[]{:S(2)}) copy-start(f32[1,768]{1,0:T(1,128)} %copy-done.5) | copy-start | bytes 9220
  136.5 22.8 %copy-start.8 = (bf16[1,640,768]{2,1,0:T(8,128)(2,1)S(1)}, bf16[1,640,768]{2,1,0:T(8,128)(2,1)}, u32[]{:S(2)}) copy-start(bf16[1,640,768]{2,1,0:T(8,128)(2,1)} %param.14) | copy-start | bytes 2949124
  136.5 22.8 %copy-start.10 = (bf16[1,640,768]{2,1,0:T(8,128)(2,1)S(1)}, bf16[1,640,768]{2,1,0:T(8,128)(2,1)}, u32[]{:S(2)}) copy-start(bf16[1,640,768]{2,1,0:T(8,128)(2,1)} %param.25) | copy-start | bytes 2949124
  136.6 22.8 %copy-start.36 = (f32[672,256]{1,0:T(8,128)S(1)}, f32[672,256]{1,0:T(8,128)}, u32[]{:S(2)}) copy-start(f32[672,256]{1,0:T(8,128)} %copy-done.35) | copy-start | bytes 2064388
  136.6 22.8 %copy-start.44 = (bf16[768,256]{1,0:T(8,128)(2,1)S(1)}, bf16[768,256]{1,0:T(8,128)(2,1)}, u32[]{:S(2)}) copy-start(bf16[768,256]{1,0:T(8,128)(2,1)} %copy-done.43) | copy-start | bytes 1179652
  136.6 22.8 %copy-start.46 = (f32[640,1]{1,0:T(8,128)S(1)}, f32[640,1]{1,0:T(8,128)}, u32[]{:S(2)}) copy-start(f32[640,1]{1,0:T(8,128)} %copy-done.45) | copy-start | bytes 7684
  136.6 22.8 %copy-start.52 = (bf16[128,768]{1,0:T(8,128)(2,1)S(1)}, bf16[128,768]{1,0:T(8,128)(2,1)}, u32[]{:S(2)}) copy-start(bf16[128,768]{1,0:T(8,128)(2,1)} %copy-done.51) | copy-start | bytes 589828
  154.9 18.1 %collective-permute-start.20 = (bf16[2,384,768]{2,1,0:T(8,128)(2,1)S(1)}, bf16[2,384,768]{2,1,0:T(8,128)(2,1)S(1)}, u32[]{:S(2)}, u32[]{:S(2)}) collective-permute-start(bf16[2,384,768]{2,1,0:T(8,128)(2,1)S(1)} %get-tuple-element.184), channel_id=1, source_target_pairs={{0,2},{2,0},{4,6},{6,4},{8,10},{10,8},{12,14},{14,12},{16,18},{18,... | collective-permute-start | bytes 3538952 | tf_op jit(solution)/shard_map/ppermute | solution.py:1134
  155.1 9.8 %collective-permute-start.21 = (bf16[48,1536]{1,0:T(8,128)(2,1)S(1)}, bf16[48,1536]{1,0:T(8,128)(2,1)S(1)}, u32[]{:S(2)}, u32[]{:S(2)}) collective-permute-start(bf16[48,1536]{1,0:T(8,128)(2,1)S(1)} %get-tuple-element.234), channel_id=1, source_target_pairs={{0,8},{2,10},{4,12},{6,14},{8,0},{10,2},{12,4},{14,6},{16,24},{18,... | collective-permute-start | bytes 442376 | tf_op jit(solution)/shard_map/ppermute | solution.py:1134
  156.7 10.4 %collective-permute-start.23 = (bf16[48,1536]{1,0:T(8,128)(2,1)S(1)}, bf16[48,1536]{1,0:T(8,128)(2,1)S(1)}, u32[]{:S(2)}, u32[]{:S(2)}) collective-permute-start(bf16[48,1536]{1,0:T(8,128)(2,1)S(1)} %get-tuple-element.235), channel_id=1, source_target_pairs={{0,24},{2,26},{4,28},{6,30},{8,16},{10,18},{12,20},{14,22},{16,8},... | collective-permute-start | bytes 442376 | tf_op jit(solution)/shard_map/ppermute | solution.py:1134
  159.2 13.8 %collective-permute-start.22 = (bf16[48,1536]{1,0:T(8,128)(2,1)S(1)}, bf16[48,1536]{1,0:T(8,128)(2,1)S(1)}, u32[]{:S(2)}, u32[]{:S(2)}) collective-permute-start(bf16[48,1536]{1,0:T(8,128)(2,1)S(1)} %get-tuple-element.236), channel_id=1, source_target_pairs={{0,16},{2,18},{4,20},{6,22},{8,24},{10,26},{12,28},{14,30},{16,0},... | collective-permute-start | bytes 442376 | tf_op jit(solution)/shard_map/ppermute | solution.py:1134
  (29 other events, 79.3 us)
